TPU v7x, 128 devices: a whole 4x4x4 slice. The times are simulated.
128 devices in a mesh: gx: 16 (over x_lo, z, core), gy: 8 (over x_hi, y).
Axes of the slice: x: 4 (x_hi: 2, x_lo: 2; x = x_hi * 2 + x_lo), y: 4, z: 4, core: 2. Of those that a mesh axis runs over, the one named last changes fastest.
Arguments:
- level_set: float32 [1024, 320, 128], P('gx', 'gy'), may hold values from -6 to 6
- band_mask: int32 [1024, 320], P('gx', 'gy'), may hold values 0 or 1
- rows: float32 [131072, 128], P(('gx', 'gy')), may hold values from -1.5 to 1.5
- row_owner: int32 [131072, 1], P(('gx', 'gy')), may hold values from 0 to 127; in each aligned block of 1024 rows (0 to 1023, 1024 to 2047, ...) at most 16 rows name the same one
- row_tile: int32 [131072], P(('gx', 'gy')), may hold values from 0 to 2559, as said below
Outputs:
- updated: float32 [1024, 320, 128], P('gx', 'gy')
Inputs may be any that keep to these rules, and one draw needn't show every extreme that they name: `row_owner`: owner of each row, devices numbered with gy fastest; among the rows of one device no owner is named more than 16 times, a bound that some block reaches. `row_tile`: column a * 40 + b of the owner's block is the cell column at local position (a, b).
All inputs are finite; a program needn't handle non-finite values. No bound on the sum of `band_mask` on one device may be relied on, other than what follows from the above.
Results may differ from a plain program's by a relative error of at most 0.0003.
Values sent between devices are 32-bit elements; how exact they have to be, the bound alone decides.
No kernel may reach another device: no remote copies, remote signals or barrier semaphores. Data moves between devices by JAX's collectives and lax.ppermute only.
A program may use at most 128 MiB of HBM per device.

v0:
```python
import jax
import jax.numpy as jnp
from jax import lax
from jax.sharding import PartitionSpec as P

STEPS = 3
SWEEPS = 2


EPSILON = 1e-06
TIME_STEP = 0.2
PSEUDO_STEP = 0.3


def with_halo(x, sides, width):
    for axis, dim in sides:
        size, length = (lax.axis_size(axis), x.shape[dim])
        up = [(i, (i + 1) % size) for i in range(size)]
        down = [(j, i) for i, j in up]
        last = lax.slice_in_dim(x, length - width, length, axis=dim)
        leading = lax.slice_in_dim(x, 0, width, axis=dim)
        before = lax.ppermute(last, axis, up)
        after = lax.ppermute(leading, axis, down)
        x = jnp.concatenate([before, x, after], axis=dim)
    return x


def weno_value(first, second, third, fourth, fifth):
    cand_one = first / 3.0 - 7.0 * second / 6.0 + 11.0 * third / 6.0
    cand_two = -second / 6.0 + 5.0 * third / 6.0 + fourth / 3.0
    cand_three = third / 3.0 + 5.0 * fourth / 6.0 - fifth / 6.0
    smooth_one = (
        13.0 / 12.0 * (first - 2.0 * second + third) ** 2
        + 0.25 * (first - 4.0 * second + 3.0 * third) ** 2
    )
    smooth_two = 13.0 / 12.0 * (second - 2.0 * third + fourth) ** 2 + 0.25 * (second - fourth) ** 2
    smooth_three = (
        13.0 / 12.0 * (third - 2.0 * fourth + fifth) ** 2
        + 0.25 * (3.0 * third - 4.0 * fourth + fifth) ** 2
    )
    weight_one = 0.1 / (EPSILON + smooth_one) ** 2
    weight_two = 0.6 / (EPSILON + smooth_two) ** 2
    weight_three = 0.3 / (EPSILON + smooth_three) ** 2
    total = weight_one + weight_two + weight_three
    return (weight_one * cand_one + weight_two * cand_two + weight_three * cand_three) / total


def hj_rate(shifted, speed):
    upper = 0.0
    lower = 0.0
    for axis in range(3):
        diffs = [shifted(axis, offset + 1) - shifted(axis, offset) for offset in range(-3, 3)]
        minus = weno_value(diffs[0], diffs[1], diffs[2], diffs[3], diffs[4])
        plus = weno_value(diffs[5], diffs[4], diffs[3], diffs[2], diffs[1])
        upper = upper + jnp.maximum(jnp.maximum(minus, 0.0) ** 2, jnp.minimum(plus, 0.0) ** 2)
        lower = lower + jnp.maximum(jnp.minimum(minus, 0.0) ** 2, jnp.maximum(plus, 0.0) ** 2)
    return -speed * jnp.sqrt(jnp.where(speed >= 0.0, upper, lower))


def reinit_rate(shifted, centre, sign):
    upper = 0.0
    lower = 0.0
    for axis in range(3):
        back = centre - shifted(axis, -1)
        front = shifted(axis, 1) - centre
        upper = upper + jnp.maximum(jnp.maximum(back, 0.0) ** 2, jnp.minimum(front, 0.0) ** 2)
        lower = lower + jnp.maximum(jnp.minimum(back, 0.0) ** 2, jnp.maximum(front, 0.0) ** 2)
    return -sign * (jnp.sqrt(jnp.where(sign >= 0.0, upper, lower)) - 1.0)


def interior(padded, margin):
    extent_x = padded.shape[0] - 2 * margin
    extent_y = padded.shape[1] - 2 * margin

    def shifted(axis, offset):
        if axis == 2:
            return jnp.roll(
                padded[margin : margin + extent_x, margin : margin + extent_y, :], -offset, 2
            )
        starts = [margin, margin]
        starts[axis] = margin + offset
        return padded[starts[0] : starts[0] + extent_x, starts[1] : starts[1] + extent_y, :]

    return shifted


def place_rows(rows, row_owner, row_tile, cells_x, cells_y):
    size_x = lax.axis_size("gx")
    size_y = lax.axis_size("gy")
    devices = size_x * size_y
    count = rows.shape[0]
    depth = rows.shape[1]
    capacity = max(2, 2 * count // devices)
    owner = row_owner[:, 0]
    onehot = (owner[:, None] == jnp.arange(devices, dtype=jnp.int32)[None, :]).astype(jnp.int32)
    before = jnp.cumsum(onehot, axis=0) - onehot
    rank = jnp.sum(before * onehot, axis=1)
    target = owner * capacity + rank
    columns = cells_x * cells_y
    send_rows = jnp.zeros((devices * capacity, depth), jnp.float32).at[target].set(rows)
    send_tile = jnp.full((devices * capacity,), columns, jnp.int32).at[target].set(row_tile)
    got_rows, got_tile = (
        lax.all_to_all(
            send_rows.reshape(devices, capacity, depth),
            ("gx", "gy"),
            split_axis=0,
            concat_axis=0,
            tiled=True,
        ),
        lax.all_to_all(
            send_tile.reshape(devices, capacity),
            ("gx", "gy"),
            split_axis=0,
            concat_axis=0,
            tiled=True,
        ),
    )
    velocity = (
        jnp.zeros((columns, depth), jnp.float32)
        .at[got_tile.reshape(-1)]
        .add(got_rows.reshape(-1, depth), mode="drop")
    )
    return velocity.reshape(cells_x, cells_y, depth)


def section_halo(field):
    return with_halo(field, (("gx", 0), ("gy", 1)), 3)


def sweep_halo(field):
    return with_halo(field, (("gx", 0), ("gy", 1)), 1)


def shards(level_set, band_mask, rows, row_owner, row_tile):
    cells_x, cells_y, depth = level_set.shape
    velocity = place_rows(rows, row_owner, row_tile, cells_x, cells_y)
    speed = band_mask.astype(jnp.float32)[:, :, None] * velocity
    field = level_set

    def advance(state):
        return state + TIME_STEP * hj_rate(interior(section_halo(state), 3), speed)

    for step in range(STEPS):
        first = advance(field)
        second = 0.75 * field + 0.25 * advance(first)
        field = field / 3.0 + 2.0 / 3.0 * advance(second)
    sign = field / jnp.sqrt(field * field + 1.0)
    for sweep in range(SWEEPS):
        field = field + PSEUDO_STEP * reinit_rate(interior(sweep_halo(field), 1), field, sign)
    return field


def solution(mesh):
    return jax.shard_map(
        shards,
        mesh=mesh,
        in_specs=(
            P("gx", "gy", None),
            P("gx", "gy"),
            P(("gx", "gy"), None),
            P(("gx", "gy"), None),
            P(("gx", "gy")),
        ),
        out_specs=P("gx", "gy", None),
        check_vma=False,
    )
```

profile of v0, /device:TPU:24, one launch (start us, length us, event | category | flops | bytes accessed | tf_op | source)
XLA Modules:
  0.0 471.3 jit_solution(8316374894031981474)
XLA Ops:
  0.9 4.5 collective-permute-start.1
  7.2 4.5 scatter_custom_fusion
  12.4 9.2 %all-to-all-start = ((s32[128,1,16]{2,1,0:T(1,128)}), s32[128,1,16]{2,1,0:T(1,128)S(1)}, u32[]{:S(2)}, u32[]{:S(2)}) async-start(s32[128,1,16]{2,1,0:T(1,128)} %bitcast.7), calls=%async_computation | async-start | bytes 131072 | tf_op jit(solution)/shard_map/all_to_all | solution.py:110
  33.0 4.5 scatter_custom_fusion.1
  37.5 10.2 %all-to-all-start.1 = ((f32[128,16,128]{2,1,0:T(8,128)}), f32[128,16,128]{2,1,0:T(8,128)}, u32[]{:S(2)}, u32[]{:S(2)}) async-start(f32[128,16,128]{2,1,0:T(8,128)} %bitcast.9), calls=%async_computation.1 | async-start | bytes 2097152 | tf_op jit(solution)/shard_map/all_to_all | solution.py:103
  52.4 3.0 collective-permute-start.2
  55.4 9.2 %all-to-all-done.1 = f32[128,16,128]{2,1,0:T(8,128)} async-done(((f32[128,16,128]{2,1,0:T(8,128)}), f32[128,16,128]{2,1,0:T(8,128)}, u32[]{:S(2)}, u32[]{:S(2)}) %all-to-all-start.1) | async-done | bytes 1048608 | tf_op jit(solution)/shard_map/all_to_all | solution.py:103
  64.5 12.4 %scatter_custom_fusion.2 = f32[2560,128]{1,0:T(8,128)S(1)} fusion(s32[2048]{0:T(1024)S(1)} %bitcast.33, f32[2048,128]{1,0:T(8,128)} %bitcast.10, f32[]{:T(128)} %constant.577.clone.1), kind=kCustom, calls=%fused_computation.591 | custom fusion | flops 262144 | bytes 1311232 | tf_op jit(solution)/shard_map/scatter-add | solution.py:121
  76.9 27.2 %multiply_add_fusion.10 = (f32[64,40,128]{2,1,0:T(8,128)S(1)}, pred[64,40,128]{2,1,0:T(8,128)(4,1)S(1)}) fusion(f32[64,40,128]{2,1,0:T(8,128)S(1)} %copy-done, f32[64,40,3]{2,1,0:T(8,128)} %get-tuple-element.183, f32[64,40,125]{2,1,0:T(8,128)} %get-tuple-element.185, f32[64,40,2]{2,1,0:T(8,128)} %get-tuple-element.175, ...), kind=kLoop, calls=%fused_computation.578 | loop fusion | flops 145162240 | bytes 21647360 | tf_op jit(solution)/shard_map/add | solution.py:141
  105.9 3.8 collective-permute-start.5
  111.8 4.3 collective-permute-start.6
  118.6 6.1 %collective-permute-done.7 = f32[70,3,128]{2,1,0:T(4,128)S(1)} collective-permute-done((f32[70,3,128]{2,1,0:T(4,128)S(1)}, f32[70,3,128]{2,1,0:T(4,128)S(1)}, u32[]{:S(2)}, u32[]{:S(2)}) %collective-permute-start.7) | collective-permute-done | bytes 107552 | tf_op jit(solution)/shard_map/ppermute | solution.py:23
  125.0 24.0 %multiply_add_fusion.9 = f32[64,40,128]{2,1,0:T(8,128)S(1)} fusion(f32[64,40,128]{2,1,0:T(8,128)S(1)} %get-tuple-element.5, pred[64,40,128]{2,1,0:T(8,128)(4,1)S(1)} %get-tuple-element.6, f32[64,40,3]{2,1,0:T(8,128)S(1)} %get-tuple-element.166, f32[64,40,125]{2,1,0:T(8,128)S(1)} %get-tuple-element.168, f32[64,40,2]{2,1,0:T(8,128)S(1)} %get-tuple-element.158, ...), kind=kLoop, calls=%fused_computation.541 | loop fusion | flops 145817600 | bytes 21432320 | tf_op jit(solution)/shard_map/add | solution.py:145
  150.8 3.8 collective-permute-start.9
  156.7 2.4 collective-permute-start.11
  159.5 2.3 collective-permute-done.10
  161.7 4.1 collective-permute-done.11
  166.1 24.0 %multiply_add_fusion.8 = f32[64,40,128]{2,1,0:T(8,128)S(1)} fusion(f32[64,40,128]{2,1,0:T(8,128)S(1)} %multiply_add_fusion.9, pred[64,40,128]{2,1,0:T(8,128)(4,1)S(1)} %get-tuple-element.6, f32[64,40,3]{2,1,0:T(8,128)S(1)} %get-tuple-element.152, f32[64,40,125]{2,1,0:T(8,128)S(1)} %get-tuple-element.154, f32[64,40,2]{2,1,0:T(8,128)S(1)} %get-tuple-element.144, ...), kind=kLoop, calls=%fused_computation.504 | loop fusion | flops 145817600 | bytes 21432320 | tf_op jit(solution)/shard_map/add | solution.py:146
  192.0 3.8 collective-permute-start.13
  200.3 2.7 collective-permute-done.14
  202.9 3.7 collective-permute-done.15
  206.9 23.8 %multiply_add_fusion.7 = f32[64,40,128]{2,1,0:T(8,128)S(1)} fusion(f32[64,40,128]{2,1,0:T(8,128)S(1)} %multiply_add_fusion.8, pred[64,40,128]{2,1,0:T(8,128)(4,1)S(1)} %get-tuple-element.6, f32[64,40,3]{2,1,0:T(8,128)S(1)} %get-tuple-element.138, f32[64,40,125]{2,1,0:T(8,128)S(1)} %get-tuple-element.140, f32[64,40,2]{2,1,0:T(8,128)S(1)} %get-tuple-element.130, ...), kind=kLoop, calls=%fused_computation.467 | loop fusion | flops 144834560 | bytes 20121600 | tf_op jit(solution)/shard_map/add | solution.py:141
  232.5 3.8 collective-permute-start.17
  240.9 2.5 collective-permute-done.18
  243.4 3.9 collective-permute-done.19
  247.6 24.0 %multiply_add_fusion.6 = f32[64,40,128]{2,1,0:T(8,128)S(1)} fusion(f32[64,40,128]{2,1,0:T(8,128)S(1)} %multiply_add_fusion.7, pred[64,40,128]{2,1,0:T(8,128)(4,1)S(1)} %get-tuple-element.6, f32[64,40,3]{2,1,0:T(8,128)S(1)} %get-tuple-element.124, f32[64,40,125]{2,1,0:T(8,128)S(1)} %get-tuple-element.126, f32[64,40,2]{2,1,0:T(8,128)S(1)} %get-tuple-element.116, ...), kind=kLoop, calls=%fused_computation.430 | loop fusion | flops 145817600 | bytes 21432320 | tf_op jit(solution)/shard_map/add | solution.py:145
  273.4 3.8 collective-permute-start.21
  281.7 2.7 collective-permute-done.22
  284.4 3.7 collective-permute-done.23
  288.4 24.1 %multiply_add_fusion.5 = f32[64,40,128]{2,1,0:T(8,128)S(1)} fusion(f32[64,40,128]{2,1,0:T(8,128)S(1)} %multiply_add_fusion.6, pred[64,40,128]{2,1,0:T(8,128)(4,1)S(1)} %get-tuple-element.6, f32[64,40,3]{2,1,0:T(8,128)S(1)} %get-tuple-element.110, f32[64,40,125]{2,1,0:T(8,128)S(1)} %get-tuple-element.112, f32[64,40,2]{2,1,0:T(8,128)S(1)} %get-tuple-element.102, ...), kind=kLoop, calls=%fused_computation.393 | loop fusion | flops 145817600 | bytes 21432320 | tf_op jit(solution)/shard_map/add | solution.py:146
  314.2 3.8 collective-permute-start.25
  322.7 2.5 collective-permute-done.26
  325.2 3.9 collective-permute-done.27
  329.4 23.8 %multiply_add_fusion.4 = f32[64,40,128]{2,1,0:T(8,128)S(1)} fusion(f32[64,40,128]{2,1,0:T(8,128)S(1)} %multiply_add_fusion.5, pred[64,40,128]{2,1,0:T(8,128)(4,1)S(1)} %get-tuple-element.6, f32[64,40,3]{2,1,0:T(8,128)S(1)} %get-tuple-element.96, f32[64,40,125]{2,1,0:T(8,128)S(1)} %get-tuple-element.98, f32[64,40,2]{2,1,0:T(8,128)S(1)} %get-tuple-element.88, ...), kind=kLoop, calls=%fused_computation.356 | loop fusion | flops 144834560 | bytes 20121600 | tf_op jit(solution)/shard_map/add | solution.py:141
  354.9 3.8 collective-permute-start.29
  363.2 2.7 collective-permute-done.30
  365.9 3.7 collective-permute-done.31
  369.9 24.0 %multiply_add_fusion.3 = f32[64,40,128]{2,1,0:T(8,128)S(1)} fusion(f32[64,40,128]{2,1,0:T(8,128)S(1)} %multiply_add_fusion.4, pred[64,40,128]{2,1,0:T(8,128)(4,1)S(1)} %get-tuple-element.6, f32[64,40,3]{2,1,0:T(8,128)S(1)} %get-tuple-element.82, f32[64,40,125]{2,1,0:T(8,128)S(1)} %get-tuple-element.84, f32[64,40,2]{2,1,0:T(8,128)S(1)} %get-tuple-element.74, ...), kind=kLoop, calls=%fused_computation.319 | loop fusion | flops 145817600 | bytes 21432320 | tf_op jit(solution)/shard_map/add | solution.py:145
  395.7 3.8 collective-permute-start.33
  404.2 2.4 collective-permute-done.34
  406.6 3.9 collective-permute-done.35
  410.9 24.1 %multiply_add_fusion.2 = f32[64,40,128]{2,1,0:T(8,128)S(1)} fusion(f32[64,40,128]{2,1,0:T(8,128)S(1)} %multiply_add_fusion.3, pred[64,40,128]{2,1,0:T(8,128)(4,1)S(1)} %get-tuple-element.6, f32[64,40,3]{2,1,0:T(8,128)S(1)} %get-tuple-element.68, f32[64,40,125]{2,1,0:T(8,128)S(1)} %get-tuple-element.70, f32[64,40,2]{2,1,0:T(8,128)S(1)} %get-tuple-element.60, ...), kind=kLoop, calls=%fused_computation.282 | loop fusion | flops 145817600 | bytes 21432320 | tf_op jit(solution)/shard_map/add | solution.py:146
  435.1 3.8 collective-permute-start.37
  444.4 3.7 collective-permute-done.39
  448.1 4.5 multiply_add_fusion.1
  452.7 3.8 collective-permute-start.41
  462.1 3.7 collective-permute-done.43
  465.8 5.0 %multiply_add_fusion = f32[64,40,128]{2,1,0:T(8,128)} fusion(f32[64,40,128]{2,1,0:T(8,128)S(1)} %multiply_add_fusion.1, f32[64,40,1]{2,1,0:T(8,128)S(1)} %get-tuple-element.48, f32[64,40,127]{2,1,0:T(8,128)S(1)} %get-tuple-element.50, f32[64,40,127]{2,1,0:T(8,128)S(1)} %get-tuple-element.49, f32[64,40,1]{2,1,0:T(8,128)S(1)} %get-tuple-element.47, ...), kind=kLoop, calls=%fused_computation.279 | loop fusion | flops 19660800 | bytes 6662144 | tf_op jit(solution)/shard_map/add | solution.py:149
  (173 shorter events, 81.0 us)
Async XLA Ops:
  0.9 50.8 %collective-permute-start.1 = (f32[3,40,128]{2,1,0:T(8,128)S(1)}, f32[3,40,128]{2,1,0:T(8,128)S(1)}, u32[]{:S(2)}, u32[]{:S(2)}) collective-permute-start(f32[3,40,128]{2,1,0:T(8,128)S(1)} %get-tuple-element.172), channel_id=1, source_target_pairs={{8,0},{16,8},{24,16},{32,24},{40,32},{48,40},{56,48},{64,56},{72,6... | collective-permute-start | bytes 184328 | tf_op jit(solution)/shard_map/ppermute | solution.py:23
  5.3 44.0 %collective-permute-start = (f32[3,40,128]{2,1,0:T(8,128)S(1)}, f32[3,40,128]{2,1,0:T(8,128)S(1)}, u32[]{:S(2)}, u32[]{:S(2)}) collective-permute-start(f32[3,40,128]{2,1,0:T(8,128)S(1)} %get-tuple-element.173), channel_id=1, source_target_pairs={{0,8},{8,16},{16,24},{24,32},{32,40},{40,48},{48,56},{56,64},{64,7... | collective-permute-start | bytes 184328 | tf_op jit(solution)/shard_map/ppermute | solution.py:22
  6.4 15.2 %copy-start = (f32[64,40,128]{2,1,0:T(8,128)S(1)}, f32[64,40,128]{2,1,0:T(8,128)}, u32[]{:S(2)}) copy-start(f32[64,40,128]{2,1,0:T(8,128)} %param.5) | copy-start | bytes 3932164
  12.4 25.1 %all-to-all-start = ((s32[128,1,16]{2,1,0:T(1,128)}), s32[128,1,16]{2,1,0:T(1,128)S(1)}, u32[]{:S(2)}, u32[]{:S(2)}) async-start(s32[128,1,16]{2,1,0:T(1,128)} %bitcast.7), calls=%async_computation | async-start | bytes 131072 | tf_op jit(solution)/shard_map/all_to_all | solution.py:110
  37.5 27.0 %all-to-all-start.1 = ((f32[128,16,128]{2,1,0:T(8,128)}), f32[128,16,128]{2,1,0:T(8,128)}, u32[]{:S(2)}, u32[]{:S(2)}) async-start(f32[128,16,128]{2,1,0:T(8,128)} %bitcast.9), calls=%async_computation.1 | async-start | bytes 2097152 | tf_op jit(solution)/shard_map/all_to_all | solution.py:103
  52.3 12.2 %copy-start.1 = (f32[70,40,128]{2,1,0:T(8,128)}, f32[70,40,128]{2,1,0:T(8,128)S(1)}, u32[]{:S(2)}) copy-start(f32[70,40,128]{2,1,0:T(8,128)S(1)} %get-tuple-element.189) | copy-start | bytes 4300804
  52.4 24.5 %collective-permute-start.2 = (f32[70,3,128]{2,1,0:T(4,128)S(1)}, f32[70,3,128]{2,1,0:T(4,128)S(1)}, u32[]{:S(2)}, u32[]{:S(2)}) collective-permute-start(f32[70,3,128]{2,1,0:T(4,128)S(1)} %get-tuple-element.39), channel_id=1, source_target_pairs={{0,1},{1,2},{2,3},{3,4},{4,5},{5,6},{6,7},{7,0},{8,9},{9,10},{10,1... | collective-permute-start | bytes 322568 | tf_op jit(solution)/shard_map/ppermute | solution.py:22
  55.4 21.6 %collective-permute-start.3 = (f32[70,3,128]{2,1,0:T(4,128)S(1)}, f32[70,3,128]{2,1,0:T(4,128)S(1)}, u32[]{:S(2)}, u32[]{:S(2)}) collective-permute-start(f32[70,3,128]{2,1,0:T(4,128)S(1)} %get-tuple-element.40), channel_id=1, source_target_pairs={{1,0},{2,1},{3,2},{4,3},{5,4},{6,5},{7,6},{0,7},{9,8},{10,9},{11,1... | collective-permute-start | bytes 322568 | tf_op jit(solution)/shard_map/ppermute | solution.py:23
  105.9 5.8 %collective-permute-start.4 = (f32[3,40,128]{2,1,0:T(8,128)S(1)}, f32[3,40,128]{2,1,0:T(8,128)S(1)}, u32[]{:S(2)}, u32[]{:S(2)}) collective-permute-start(f32[3,40,128]{2,1,0:T(8,128)S(1)} %get-tuple-element.155), channel_id=1, source_target_pairs={{0,8},{8,16},{16,24},{24,32},{32,40},{40,48},{48,56},{56,64},{64,7... | collective-permute-start | bytes 184328 | tf_op jit(solution)/shard_map/ppermute | solution.py:22
  105.9 5.7 %collective-permute-start.5 = (f32[3,40,128]{2,1,0:T(8,128)S(1)}, f32[3,40,128]{2,1,0:T(8,128)S(1)}, u32[]{:S(2)}, u32[]{:S(2)}) collective-permute-start(f32[3,40,128]{2,1,0:T(8,128)S(1)} %get-tuple-element.156), channel_id=1, source_target_pairs={{8,0},{16,8},{24,16},{32,24},{40,32},{48,40},{56,48},{64,56},{72,6... | collective-permute-start | bytes 184328 | tf_op jit(solution)/shard_map/ppermute | solution.py:23
  111.8 6.9 %collective-permute-start.6 = (f32[70,3,128]{2,1,0:T(4,128)S(1)}, f32[70,3,128]{2,1,0:T(4,128)S(1)}, u32[]{:S(2)}, u32[]{:S(2)}) collective-permute-start(f32[70,3,128]{2,1,0:T(4,128)S(1)} %get-tuple-element.37), channel_id=1, source_target_pairs={{0,1},{1,2},{2,3},{3,4},{4,5},{5,6},{6,7},{7,0},{8,9},{9,10},{10,1... | collective-permute-start | bytes 322568 | tf_op jit(solution)/shard_map/ppermute | solution.py:22
  116.0 8.7 %collective-permute-start.7 = (f32[70,3,128]{2,1,0:T(4,128)S(1)}, f32[70,3,128]{2,1,0:T(4,128)S(1)}, u32[]{:S(2)}, u32[]{:S(2)}) collective-permute-start(f32[70,3,128]{2,1,0:T(4,128)S(1)} %get-tuple-element.38), channel_id=1, source_target_pairs={{1,0},{2,1},{3,2},{4,3},{5,4},{6,5},{7,6},{0,7},{9,8},{10,9},{11,1... | collective-permute-start | bytes 322568 | tf_op jit(solution)/shard_map/ppermute | solution.py:23
  150.7 5.8 %collective-permute-start.8 = (f32[3,40,128]{2,1,0:T(8,128)S(1)}, f32[3,40,128]{2,1,0:T(8,128)S(1)}, u32[]{:S(2)}, u32[]{:S(2)}) collective-permute-start(f32[3,40,128]{2,1,0:T(8,128)S(1)} %get-tuple-element.141), channel_id=1, source_target_pairs={{0,8},{8,16},{16,24},{24,32},{32,40},{40,48},{48,56},{56,64},{64,7... | collective-permute-start | bytes 184328 | tf_op jit(solution)/shard_map/ppermute | solution.py:22
  150.8 5.7 %collective-permute-start.9 = (f32[3,40,128]{2,1,0:T(8,128)S(1)}, f32[3,40,128]{2,1,0:T(8,128)S(1)}, u32[]{:S(2)}, u32[]{:S(2)}) collective-permute-start(f32[3,40,128]{2,1,0:T(8,128)S(1)} %get-tuple-element.142), channel_id=1, source_target_pairs={{8,0},{16,8},{24,16},{32,24},{40,32},{48,40},{56,48},{64,56},{72,6... | collective-permute-start | bytes 184328 | tf_op jit(solution)/shard_map/ppermute | solution.py:23
  156.6 5.2 %collective-permute-start.10 = (f32[70,3,128]{2,1,0:T(4,128)S(1)}, f32[70,3,128]{2,1,0:T(4,128)S(1)}, u32[]{:S(2)}, u32[]{:S(2)}) collective-permute-start(f32[70,3,128]{2,1,0:T(4,128)S(1)} %get-tuple-element.33), channel_id=1, source_target_pairs={{0,1},{1,2},{2,3},{3,4},{4,5},{5,6},{6,7},{7,0},{8,9},{9,10},{10,1... | collective-permute-start | bytes 322568 | tf_op jit(solution)/shard_map/ppermute | solution.py:22
  156.7 9.2 %collective-permute-start.11 = (f32[70,3,128]{2,1,0:T(4,128)S(1)}, f32[70,3,128]{2,1,0:T(4,128)S(1)}, u32[]{:S(2)}, u32[]{:S(2)}) collective-permute-start(f32[70,3,128]{2,1,0:T(4,128)S(1)} %get-tuple-element.34), channel_id=1, source_target_pairs={{1,0},{2,1},{3,2},{4,3},{5,4},{6,5},{7,6},{0,7},{9,8},{10,9},{11,1... | collective-permute-start | bytes 322568 | tf_op jit(solution)/shard_map/ppermute | solution.py:23
  191.9 5.8 %collective-permute-start.12 = (f32[3,40,128]{2,1,0:T(8,128)S(1)}, f32[3,40,128]{2,1,0:T(8,128)S(1)}, u32[]{:S(2)}, u32[]{:S(2)}) collective-permute-start(f32[3,40,128]{2,1,0:T(8,128)S(1)} %get-tuple-element.127), channel_id=1, source_target_pairs={{0,8},{8,16},{16,24},{24,32},{32,40},{40,48},{48,56},{56,64},{64,7... | collective-permute-start | bytes 184328 | tf_op jit(solution)/shard_map/ppermute | solution.py:22
  192.0 5.7 %collective-permute-start.13 = (f32[3,40,128]{2,1,0:T(8,128)S(1)}, f32[3,40,128]{2,1,0:T(8,128)S(1)}, u32[]{:S(2)}, u32[]{:S(2)}) collective-permute-start(f32[3,40,128]{2,1,0:T(8,128)S(1)} %get-tuple-element.128), channel_id=1, source_target_pairs={{8,0},{16,8},{24,16},{32,24},{40,32},{48,40},{56,48},{64,56},{72,6... | collective-permute-start | bytes 184328 | tf_op jit(solution)/shard_map/ppermute | solution.py:23
  197.8 5.2 %collective-permute-start.14 = (f32[70,3,128]{2,1,0:T(4,128)S(1)}, f32[70,3,128]{2,1,0:T(4,128)S(1)}, u32[]{:S(2)}, u32[]{:S(2)}) collective-permute-start(f32[70,3,128]{2,1,0:T(4,128)S(1)} %get-tuple-element.29), channel_id=1, source_target_pairs={{0,1},{1,2},{2,3},{3,4},{4,5},{5,6},{6,7},{7,0},{8,9},{9,10},{10,1... | collective-permute-start | bytes 322568 | tf_op jit(solution)/shard_map/ppermute | solution.py:22
  197.8 8.8 %collective-permute-start.15 = (f32[70,3,128]{2,1,0:T(4,128)S(1)}, f32[70,3,128]{2,1,0:T(4,128)S(1)}, u32[]{:S(2)}, u32[]{:S(2)}) collective-permute-start(f32[70,3,128]{2,1,0:T(4,128)S(1)} %get-tuple-element.30), channel_id=1, source_target_pairs={{1,0},{2,1},{3,2},{4,3},{5,4},{6,5},{7,6},{0,7},{9,8},{10,9},{11,1... | collective-permute-start | bytes 322568 | tf_op jit(solution)/shard_map/ppermute | solution.py:23
  232.4 5.8 %collective-permute-start.16 = (f32[3,40,128]{2,1,0:T(8,128)S(1)}, f32[3,40,128]{2,1,0:T(8,128)S(1)}, u32[]{:S(2)}, u32[]{:S(2)}) collective-permute-start(f32[3,40,128]{2,1,0:T(8,128)S(1)} %get-tuple-element.113), channel_id=1, source_target_pairs={{0,8},{8,16},{16,24},{24,32},{32,40},{40,48},{48,56},{56,64},{64,7... | collective-permute-start | bytes 184328 | tf_op jit(solution)/shard_map/ppermute | solution.py:22
  232.5 5.7 %collective-permute-start.17 = (f32[3,40,128]{2,1,0:T(8,128)S(1)}, f32[3,40,128]{2,1,0:T(8,128)S(1)}, u32[]{:S(2)}, u32[]{:S(2)}) collective-permute-start(f32[3,40,128]{2,1,0:T(8,128)S(1)} %get-tuple-element.114), channel_id=1, source_target_pairs={{8,0},{16,8},{24,16},{32,24},{40,32},{48,40},{56,48},{64,56},{72,6... | collective-permute-start | bytes 184328 | tf_op jit(solution)/shard_map/ppermute | solution.py:23
  238.3 5.2 %collective-permute-start.18 = (f32[70,3,128]{2,1,0:T(4,128)S(1)}, f32[70,3,128]{2,1,0:T(4,128)S(1)}, u32[]{:S(2)}, u32[]{:S(2)}) collective-permute-start(f32[70,3,128]{2,1,0:T(4,128)S(1)} %get-tuple-element.25), channel_id=1, source_target_pairs={{0,1},{1,2},{2,3},{3,4},{4,5},{5,6},{6,7},{7,0},{8,9},{9,10},{10,1... | collective-permute-start | bytes 322568 | tf_op jit(solution)/shard_map/ppermute | solution.py:22
  238.4 9.0 %collective-permute-start.19 = (f32[70,3,128]{2,1,0:T(4,128)S(1)}, f32[70,3,128]{2,1,0:T(4,128)S(1)}, u32[]{:S(2)}, u32[]{:S(2)}) collective-permute-start(f32[70,3,128]{2,1,0:T(4,128)S(1)} %get-tuple-element.26), channel_id=1, source_target_pairs={{1,0},{2,1},{3,2},{4,3},{5,4},{6,5},{7,6},{0,7},{9,8},{10,9},{11,1... | collective-permute-start | bytes 322568 | tf_op jit(solution)/shard_map/ppermute | solution.py:23
  273.3 5.8 %collective-permute-start.20 = (f32[3,40,128]{2,1,0:T(8,128)S(1)}, f32[3,40,128]{2,1,0:T(8,128)S(1)}, u32[]{:S(2)}, u32[]{:S(2)}) collective-permute-start(f32[3,40,128]{2,1,0:T(8,128)S(1)} %get-tuple-element.99), channel_id=1, source_target_pairs={{0,8},{8,16},{16,24},{24,32},{32,40},{40,48},{48,56},{56,64},{64,7... | collective-permute-start | bytes 184328 | tf_op jit(solution)/shard_map/ppermute | solution.py:22
  273.4 5.7 %collective-permute-start.21 = (f32[3,40,128]{2,1,0:T(8,128)S(1)}, f32[3,40,128]{2,1,0:T(8,128)S(1)}, u32[]{:S(2)}, u32[]{:S(2)}) collective-permute-start(f32[3,40,128]{2,1,0:T(8,128)S(1)} %get-tuple-element.100), channel_id=1, source_target_pairs={{8,0},{16,8},{24,16},{32,24},{40,32},{48,40},{56,48},{64,56},{72,6... | collective-permute-start | bytes 184328 | tf_op jit(solution)/shard_map/ppermute | solution.py:23
  279.2 5.2 %collective-permute-start.22 = (f32[70,3,128]{2,1,0:T(4,128)S(1)}, f32[70,3,128]{2,1,0:T(4,128)S(1)}, u32[]{:S(2)}, u32[]{:S(2)}) collective-permute-start(f32[70,3,128]{2,1,0:T(4,128)S(1)} %get-tuple-element.21), channel_id=1, source_target_pairs={{0,1},{1,2},{2,3},{3,4},{4,5},{5,6},{6,7},{7,0},{8,9},{9,10},{10,1... | collective-permute-start | bytes 322568 | tf_op jit(solution)/shard_map/ppermute | solution.py:22
  279.3 8.8 %collective-permute-start.23 = (f32[70,3,128]{2,1,0:T(4,128)S(1)}, f32[70,3,128]{2,1,0:T(4,128)S(1)}, u32[]{:S(2)}, u32[]{:S(2)}) collective-permute-start(f32[70,3,128]{2,1,0:T(4,128)S(1)} %get-tuple-element.22), channel_id=1, source_target_pairs={{1,0},{2,1},{3,2},{4,3},{5,4},{6,5},{7,6},{0,7},{9,8},{10,9},{11,1... | collective-permute-start | bytes 322568 | tf_op jit(solution)/shard_map/ppermute | solution.py:23
  314.1 5.8 %collective-permute-start.24 = (f32[3,40,128]{2,1,0:T(8,128)S(1)}, f32[3,40,128]{2,1,0:T(8,128)S(1)}, u32[]{:S(2)}, u32[]{:S(2)}) collective-permute-start(f32[3,40,128]{2,1,0:T(8,128)S(1)} %get-tuple-element.85), channel_id=1, source_target_pairs={{0,8},{8,16},{16,24},{24,32},{32,40},{40,48},{48,56},{56,64},{64,7... | collective-permute-start | bytes 184328 | tf_op jit(solution)/shard_map/ppermute | solution.py:22
  314.2 5.7 %collective-permute-start.25 = (f32[3,40,128]{2,1,0:T(8,128)S(1)}, f32[3,40,128]{2,1,0:T(8,128)S(1)}, u32[]{:S(2)}, u32[]{:S(2)}) collective-permute-start(f32[3,40,128]{2,1,0:T(8,128)S(1)} %get-tuple-element.86), channel_id=1, source_target_pairs={{8,0},{16,8},{24,16},{32,24},{40,32},{48,40},{56,48},{64,56},{72,6... | collective-permute-start | bytes 184328 | tf_op jit(solution)/shard_map/ppermute | solution.py:23
  320.0 5.2 %collective-permute-start.26 = (f32[70,3,128]{2,1,0:T(4,128)S(1)}, f32[70,3,128]{2,1,0:T(4,128)S(1)}, u32[]{:S(2)}, u32[]{:S(2)}) collective-permute-start(f32[70,3,128]{2,1,0:T(4,128)S(1)} %get-tuple-element.17), channel_id=1, source_target_pairs={{0,1},{1,2},{2,3},{3,4},{4,5},{5,6},{6,7},{7,0},{8,9},{9,10},{10,1... | collective-permute-start | bytes 322568 | tf_op jit(solution)/shard_map/ppermute | solution.py:22
  320.1 9.0 %collective-permute-start.27 = (f32[70,3,128]{2,1,0:T(4,128)S(1)}, f32[70,3,128]{2,1,0:T(4,128)S(1)}, u32[]{:S(2)}, u32[]{:S(2)}) collective-permute-start(f32[70,3,128]{2,1,0:T(4,128)S(1)} %get-tuple-element.18), channel_id=1, source_target_pairs={{1,0},{2,1},{3,2},{4,3},{5,4},{6,5},{7,6},{0,7},{9,8},{10,9},{11,1... | collective-permute-start | bytes 322568 | tf_op jit(solution)/shard_map/ppermute | solution.py:23
  354.8 5.8 %collective-permute-start.28 = (f32[3,40,128]{2,1,0:T(8,128)S(1)}, f32[3,40,128]{2,1,0:T(8,128)S(1)}, u32[]{:S(2)}, u32[]{:S(2)}) collective-permute-start(f32[3,40,128]{2,1,0:T(8,128)S(1)} %get-tuple-element.71), channel_id=1, source_target_pairs={{0,8},{8,16},{16,24},{24,32},{32,40},{40,48},{48,56},{56,64},{64,7... | collective-permute-start | bytes 184328 | tf_op jit(solution)/shard_map/ppermute | solution.py:22
  354.9 5.7 %collective-permute-start.29 = (f32[3,40,128]{2,1,0:T(8,128)S(1)}, f32[3,40,128]{2,1,0:T(8,128)S(1)}, u32[]{:S(2)}, u32[]{:S(2)}) collective-permute-start(f32[3,40,128]{2,1,0:T(8,128)S(1)} %get-tuple-element.72), channel_id=1, source_target_pairs={{8,0},{16,8},{24,16},{32,24},{40,32},{48,40},{56,48},{64,56},{72,6... | collective-permute-start | bytes 184328 | tf_op jit(solution)/shard_map/ppermute | solution.py:23
  360.7 5.2 %collective-permute-start.30 = (f32[70,3,128]{2,1,0:T(4,128)S(1)}, f32[70,3,128]{2,1,0:T(4,128)S(1)}, u32[]{:S(2)}, u32[]{:S(2)}) collective-permute-start(f32[70,3,128]{2,1,0:T(4,128)S(1)} %get-tuple-element.13), channel_id=1, source_target_pairs={{0,1},{1,2},{2,3},{3,4},{4,5},{5,6},{6,7},{7,0},{8,9},{9,10},{10,1... | collective-permute-start | bytes 322568 | tf_op jit(solution)/shard_map/ppermute | solution.py:22
  360.8 8.8 %collective-permute-start.31 = (f32[70,3,128]{2,1,0:T(4,128)S(1)}, f32[70,3,128]{2,1,0:T(4,128)S(1)}, u32[]{:S(2)}, u32[]{:S(2)}) collective-permute-start(f32[70,3,128]{2,1,0:T(4,128)S(1)} %get-tuple-element.14), channel_id=1, source_target_pairs={{1,0},{2,1},{3,2},{4,3},{5,4},{6,5},{7,6},{0,7},{9,8},{10,9},{11,1... | collective-permute-start | bytes 322568 | tf_op jit(solution)/shard_map/ppermute | solution.py:23
  395.6 5.8 %collective-permute-start.32 = (f32[3,40,128]{2,1,0:T(8,128)S(1)}, f32[3,40,128]{2,1,0:T(8,128)S(1)}, u32[]{:S(2)}, u32[]{:S(2)}) collective-permute-start(f32[3,40,128]{2,1,0:T(8,128)S(1)} %get-tuple-element.57), channel_id=1, source_target_pairs={{0,8},{8,16},{16,24},{24,32},{32,40},{40,48},{48,56},{56,64},{64,7... | collective-permute-start | bytes 184328 | tf_op jit(solution)/shard_map/ppermute | solution.py:22
  395.7 5.7 %collective-permute-start.33 = (f32[3,40,128]{2,1,0:T(8,128)S(1)}, f32[3,40,128]{2,1,0:T(8,128)S(1)}, u32[]{:S(2)}, u32[]{:S(2)}) collective-permute-start(f32[3,40,128]{2,1,0:T(8,128)S(1)} %get-tuple-element.58), channel_id=1, source_target_pairs={{8,0},{16,8},{24,16},{32,24},{40,32},{48,40},{56,48},{64,56},{72,6... | collective-permute-start | bytes 184328 | tf_op jit(solution)/shard_map/ppermute | solution.py:23
  401.5 5.2 %collective-permute-start.34 = (f32[70,3,128]{2,1,0:T(4,128)S(1)}, f32[70,3,128]{2,1,0:T(4,128)S(1)}, u32[]{:S(2)}, u32[]{:S(2)}) collective-permute-start(f32[70,3,128]{2,1,0:T(4,128)S(1)} %get-tuple-element.9), channel_id=1, source_target_pairs={{0,1},{1,2},{2,3},{3,4},{4,5},{5,6},{6,7},{7,0},{8,9},{9,10},{10,1... | collective-permute-start | bytes 322568 | tf_op jit(solution)/shard_map/ppermute | solution.py:22
  401.6 9.0 %collective-permute-start.35 = (f32[70,3,128]{2,1,0:T(4,128)S(1)}, f32[70,3,128]{2,1,0:T(4,128)S(1)}, u32[]{:S(2)}, u32[]{:S(2)}) collective-permute-start(f32[70,3,128]{2,1,0:T(4,128)S(1)} %get-tuple-element.10), channel_id=1, source_target_pairs={{1,0},{2,1},{3,2},{4,3},{5,4},{6,5},{7,6},{0,7},{9,8},{10,9},{11,1... | collective-permute-start | bytes 322568 | tf_op jit(solution)/shard_map/ppermute | solution.py:23
  435.0 5.4 %collective-permute-start.36 = (f32[1,40,128]{2,1,0:T(8,128)S(1)}, f32[1,40,128]{2,1,0:T(8,128)S(1)}, u32[]{:S(2)}, u32[]{:S(2)}) collective-permute-start(f32[1,40,128]{2,1,0:T(8,128)S(1)} %get-tuple-element.51), channel_id=1, source_target_pairs={{0,8},{8,16},{16,24},{24,32},{32,40},{40,48},{48,56},{56,64},{64,7... | collective-permute-start | bytes 61448 | tf_op jit(solution)/shard_map/ppermute | solution.py:22
  435.1 5.3 %collective-permute-start.37 = (f32[1,40,128]{2,1,0:T(8,128)S(1)}, f32[1,40,128]{2,1,0:T(8,128)S(1)}, u32[]{:S(2)}, u32[]{:S(2)}) collective-permute-start(f32[1,40,128]{2,1,0:T(8,128)S(1)} %get-tuple-element.52), channel_id=1, source_target_pairs={{8,0},{16,8},{24,16},{32,24},{40,32},{48,40},{56,48},{64,56},{72,6... | collective-permute-start | bytes 61448 | tf_op jit(solution)/shard_map/ppermute | solution.py:23
  440.4 4.0 collective-permute-start.38
  440.5 7.6 %collective-permute-start.39 = (f32[66,1,128]{2,1,0:T(1,128)S(1)}, f32[66,1,128]{2,1,0:T(1,128)S(1)}, u32[]{:S(2)}, u32[]{:S(2)}) collective-permute-start(f32[66,1,128]{2,1,0:T(1,128)S(1)} %get-tuple-element.44), channel_id=1, source_target_pairs={{1,0},{2,1},{3,2},{4,3},{5,4},{6,5},{7,6},{0,7},{9,8},{10,9},{11,1... | collective-permute-start | bytes 101384 | tf_op jit(solution)/shard_map/ppermute | solution.py:23
  452.6 5.4 %collective-permute-start.40 = (f32[1,40,128]{2,1,0:T(8,128)S(1)}, f32[1,40,128]{2,1,0:T(8,128)S(1)}, u32[]{:S(2)}, u32[]{:S(2)}) collective-permute-start(f32[1,40,128]{2,1,0:T(8,128)S(1)} %get-tuple-element.45), channel_id=1, source_target_pairs={{0,8},{8,16},{16,24},{24,32},{32,40},{40,48},{48,56},{56,64},{64,7... | collective-permute-start | bytes 61448 | tf_op jit(solution)/shard_map/ppermute | solution.py:22
  452.7 5.3 %collective-permute-start.41 = (f32[1,40,128]{2,1,0:T(8,128)S(1)}, f32[1,40,128]{2,1,0:T(8,128)S(1)}, u32[]{:S(2)}, u32[]{:S(2)}) collective-permute-start(f32[1,40,128]{2,1,0:T(8,128)S(1)} %get-tuple-element.46), channel_id=1, source_target_pairs={{8,0},{16,8},{24,16},{32,24},{40,32},{48,40},{56,48},{64,56},{72,6... | collective-permute-start | bytes 61448 | tf_op jit(solution)/shard_map/ppermute | solution.py:23
  458.1 4.0 collective-permute-start.42
  458.2 7.6 %collective-permute-start.43 = (f32[66,1,128]{2,1,0:T(1,128)S(1)}, f32[66,1,128]{2,1,0:T(1,128)S(1)}, u32[]{:S(2)}, u32[]{:S(2)}) collective-permute-start(f32[66,1,128]{2,1,0:T(1,128)S(1)} %get-tuple-element.42), channel_id=1, source_target_pairs={{1,0},{2,1},{3,2},{4,3},{5,4},{6,5},{7,6},{0,7},{9,8},{10,9},{11,1... | collective-permute-start | bytes 101384 | tf_op jit(solution)/shard_map/ppermute | solution.py:23
  (2 other events, 2.6 us)
where the time goes:
time: 479 us; the launch traced here: 471 us
  other arithmetic  245 us (51%)
  starting transfers between devices  90 us (19%)
  waiting for transfers between devices  86.4 us (18%)
  local copies, waits for them, and re-layouts  48.3 us (10%)
    add x3, other arithmetic, advance(): return state + TIME_STEP * hj_rate(interior(section_halo(state), 3), speed)  74.8 us
    add x3, other arithmetic, shards(): field = field / 3.0 + 2.0 / 3.0 * advance(second)  72.1 us
    add x3, other arithmetic, shards(): second = 0.75 * field + 0.25 * advance(first)  72 us
    ppermute x22, starting transfers between devices, with_halo(): after = lax.ppermute(leading, axis, down)  62 us
    ppermute x22, waiting for transfers between devices, with_halo(): after = lax.ppermute(leading, axis, down)  40.4 us
    ppermute x22, waiting for transfers between devices, with_halo(): before = lax.ppermute(last, axis, up)  36.8 us
    slice x58, local copies, waits for them, and re-layouts, shifted(): jnp.roll(padded[margin:margin + extent_x, margin:margin + extent_y, :], -...  32.6 us
    scatter-add x1, other arithmetic, place_rows(): velocity = jnp.zeros((columns, depth), jnp.float32).at[got_tile.reshape(-...  12.4 us
  transfers between devices with their start and end apart: 46, of which 31 were waited for; matrix products, arithmetic and copies ran while one was open for 10% of the time, Pallas kernels for 0%

commit v1 on v0

v1 whole, which is shorter than its diff:
```python
import functools

import jax
import jax.numpy as jnp
from jax import lax
from jax.experimental import pallas as pl
from jax.experimental.pallas import tpu as pltpu
from jax.sharding import PartitionSpec as P

EPSILON = 1e-06
TIME_STEP = 0.2
PSEUDO_STEP = 0.3

CX, CY, NZ = 64, 40, 128
DEVICES = 128
CAP = 16
SLOTS = CAP + 1
COLS = CX * CY

XO, YO = 12, 16
XR, YP = 88, 72
EXT = XR * YP
SPEED_HALO = 8
VMEM_LIMIT = 40 * 1024 * 1024
F32 = jnp.float32


def rcp(x):
    return pl.reciprocal(x, approx=True)


def pair_weights(e_left, e_right, g):
    total = e_left + e_right
    twice = g + g
    common = g * g * (13.0 / 3.0) + EPSILON
    after = total + twice
    before = total - twice
    ip = rcp(common + after * after)
    it = rcp(common + total * total)
    im = rcp(common + before * before)
    return ip * ip, it * it * 6.0, im * im, total


def weight_after(e_left, e_right, g):
    low = e_left + e_right + (g + g)
    i = rcp(g * g * (13.0 / 3.0) + EPSILON + low * low)
    return i * i


def weight_before(e_left, e_right, g):
    low = e_left + e_right - (g + g)
    i = rcp(g * g * (13.0 / 3.0) + EPSILON + low * low)
    return i * i


def weight_centre(e_left, e_right, g):
    low = e_left + e_right
    i = rcp(g * g * (13.0 / 3.0) + EPSILON + low * low)
    return i * i * 6.0


def central(slope, g, total):
    base = slope + g * (1.0 / 6.0)
    half = total * 0.5
    return base + half, half - base


def face_values(p1, p2, p3, h_left, h_right, q_left, q_right):
    low = p1 * h_left
    high = p3 * h_right
    both = p1 + p3 + p2
    left = q_left - (high + low * (2.0 / 3.0)) * rcp(both + (p3 + p3))
    right = q_right - (low + high * (2.0 / 3.0)) * rcp(both + (p1 + p1))
    return left, right


def upwind(sign, left, right):
    top = jnp.maximum(jnp.maximum(sign * left, sign * right), 0.0)
    return top * top


def sign_of(speed):
    return jnp.where(speed >= 0.0, 1.0, -1.0)


def root(x):
    return x * lax.rsqrt(jnp.maximum(x, 1e-37))


def prev_z(x):
    return pltpu.roll(x, 1, 1)


def next_z(x):
    return pltpu.roll(x, NZ - 1, 1)


def z_term(u, sign):
    e = 0.5 * (next_z(u) - u) - 0.5 * (u - prev_z(u))
    e_prev, e_next, e_after = prev_z(e), next_z(e), pltpu.roll(e, NZ - 2, 1)
    d = next_z(u) - u
    g_prev, g, g_next = e - e_prev, e_next - e, e_after - e_next
    h, h_next = g - g_prev, g_next - g
    pp = weight_after(e_prev, e, g_prev)
    pt = weight_centre(e, e_next, g)
    pm = weight_before(e_next, e_after, g_next)
    q_left, q_right = central(d, g, e + e_next)
    left, right = face_values(pp, pt, pm, h, h_next, q_left, q_right)
    return upwind(sign, prev_z(left), right)


def y_terms(u, signs):
    n = len(u) - 6
    out = []
    d_prev = u[1] - u[0]
    half_prev = 0.5 * d_prev
    d, e, g, h, pp, pt, pm, q, left = {}, {}, {}, {}, {}, {}, {}, {}, {}
    for k in range(1, n + 5):
        d[k] = u[k + 1] - u[k]
        half = 0.5 * d[k]
        e[k] = half - half_prev
        half_prev = half
        if k >= 2:
            f = k - 1
            g[f] = e[k] - e[f]
            ppf, ptf, pmf, total = pair_weights(e[f], e[k], g[f])
            pp[f], pt[f], pm[f] = ppf, ptf, pmf
            q[f] = central(d[f], g[f], total)
            if f >= 2:
                h[f] = g[f] - g[f - 1]
            if f >= 3:
                w = f - 1
                lw, rw = face_values(pp[w - 1], pt[w], pm[w + 1], h[w], h[w + 1], *q[w])
                left[w] = lw
                if w >= 3:
                    out.append(upwind(signs[w - 3], left[w - 1], rw))
    return out


def stage(src, speed, term, ny, x_lo, x_hi, y_lo, finish):
    group = 4
    unroll = (x_hi - x_lo) // group

    def tile(ref, x, j):
        return ref[pl.ds(x * YP + (y_lo + j), 8, stride=ny), :]

    def y_body(i, carry):
        for k in range(group):
            x = x_lo + i * group + k
            signs = [sign_of(tile(speed, x, j)) for j in range(ny)]
            u = [tile(src, x, j) for j in range(-3, ny + 3)]
            for j, value in enumerate(y_terms(u, signs)):
                term[pl.ds(pl.multiple_of(x * (8 * ny) + 8 * j, 8), 8), :] = value + z_term(
                    u[j + 3], signs[j]
                )
        return carry

    lax.fori_loop(0, (x_hi - x_lo) // group, y_body, 0)

    def advance(x, j, state):
        d, half, e, g, h, pp0, pp1, p2, ql, qr, left = state
        d2 = tile(src, x + 3, j) - tile(src, x + 2, j)
        half2 = 0.5 * d2
        e2 = half2 - half
        g2 = e2 - e
        pp2, pt2, pm2, total = pair_weights(e, e2, g2)
        ql2, qr2 = central(d, g2, total)
        h2 = g2 - g
        left2, right = face_values(pp0, p2, pm2, h, h2, ql, qr)
        return left, right, (d2, half2, e2, g2, h2, pp1, pp2, pt2, ql2, qr2, left2)

    def column(j, carry):
        zero = jnp.zeros((8, NZ), F32)
        x = x_lo - 1
        u = [tile(src, x + k, j) for k in range(-2, 3)]
        ds = [u[k + 1] - u[k] for k in range(4)]
        es = [0.5 * ds[k + 1] - 0.5 * ds[k] for k in range(3)]
        g0, g1 = es[1] - es[0], es[2] - es[1]
        ppa, _, _, _ = pair_weights(es[0], es[1], g0)
        ppb, ptb, _, total = pair_weights(es[1], es[2], g1)
        ql, qr = central(ds[2], g1, total)
        state = (ds[3], 0.5 * ds[3], es[2], g1, g1 - g0, ppa, ppb, ptb, ql, qr, zero)
        _, _, state = advance(x, j, state)

        def body(i, state):
            for k in range(unroll):
                x = x_lo + i * unroll + k
                left, right, state = advance(x, j, state)
                sp = tile(speed, x, j)
                sign = sign_of(sp)
                u0 = tile(src, x, j)
                total = (
                    upwind(sign, left, right)
                    + term[pl.ds(pl.multiple_of(x * (8 * ny) + 8 * j, 8), 8), :]
                )
                finish(x, j, u0, u0 - TIME_STEP * sp * root(total))
            return state

        lax.fori_loop(0, (x_hi - x_lo) // unroll, body, state)
        return carry

    lax.fori_loop(0, ny, column, 0)


def fill_block(ext, own, before, after, width):
    def put(src, x_to, count):
        def body(x, carry):
            for i in range(CY // 8):
                ext[pl.ds(pl.multiple_of((x + x_to) * YP + (YO + 8 * i), 8), 8), :] = src[
                    pl.ds(pl.multiple_of(x * CY + 8 * i, 8), 8), :
                ]
            return carry

        lax.fori_loop(0, count, body, 0)

    put(own, XO, CX)
    put(before, XO - width, width)
    put(after, XO + CX, width)


def fill_sides(ext, before, after, width):
    for t in range(width):
        for b in range(XR // 8):
            ext[pl.ds(b * 8 * YP + (YO - width + t), 8, stride=YP), :] = before[
                pl.ds(t * XR + 8 * b, 8), :
            ]
            ext[pl.ds(b * 8 * YP + (YO + CY + t), 8, stride=YP), :] = after[
                pl.ds(t * XR + 8 * b, 8), :
            ]


def sides_kernel(width, own, before, after, low, high, ext):
    fill_block(ext, own, before, after, width)
    for t in range(width):
        for b in range(XR // 8):
            low[pl.ds(t * XR + 8 * b, 8), :] = ext[pl.ds(b * 8 * YP + (YO + t), 8, stride=YP), :]
            high[pl.ds(t * XR + 8 * b, 8), :] = ext[
                pl.ds(b * 8 * YP + (YO + CY - width + t), 8, stride=YP), :
            ]


def params():
    return pltpu.CompilerParams(vmem_limit_bytes=VMEM_LIMIT)


def shape(rows):
    return jax.ShapeDtypeStruct((rows, NZ), F32)


def vmem(rows):
    return pltpu.VMEM((rows, NZ), F32)


def shift_pair(low, high, axis):
    size = lax.axis_size(axis)
    up = [(i, (i + 1) % size) for i in range(size)]
    down = [(j, i) for i, j in up]
    return lax.ppermute(high, axis, up), lax.ppermute(low, axis, down)


def halo(own, low, high, width):
    before, after = shift_pair(low, high, "gx")
    side_low, side_high = pl.pallas_call(
        functools.partial(sides_kernel, width),
        out_shape=(shape(width * XR), shape(width * XR)),
        scratch_shapes=[vmem(EXT)],
        compiler_params=params(),
        name="sides",
    )(own, before, after)
    left, right = shift_pair(side_low, side_high, "gy")
    return own, before, after, left, right


def store_tile(ref, x, j, ny, y_lo, value):
    ref[pl.ds(x * YP + (y_lo + j), 8, stride=ny), :] = value


def load_tile(ref, x, j, ny, y_lo):
    return ref[pl.ds(x * YP + (y_lo + j), 8, stride=ny), :]


def runge_kutta(width, next_width, make_speed, *refs):
    refs = list(refs)
    own, before, after, left, right = refs[:5]
    refs = refs[5:]
    if make_speed:
        s_own, s_before, s_after, s_left, s_right = refs[:5]
        refs = refs[5:]
    else:
        speed = refs.pop(0)
    out = refs.pop(0)
    if next_width:
        out_low, out_high = refs[:2]
        refs = refs[2:]
    if make_speed:
        speed = refs.pop(0)
    base, first, second, term = refs[:4]

    fill_block(base, own, before, after, width)
    fill_sides(base, left, right, width)
    if make_speed:
        fill_block(speed, s_own, s_before, s_after, SPEED_HALO)
        fill_sides(speed, s_left, s_right, SPEED_HALO)

    last = width - 9
    geometry = []
    for margin in (width - 3, width - 6, last):
        ny = (CY + 2 * margin + 7) // 8
        count = (CX + 2 * margin + 3) // 4 * 4
        geometry.append((ny, XO - margin, XO - margin + count, YO - margin))

    ny, x_lo, x_hi, y_lo = geometry[0]

    def finish_one(x, j, u, moved):
        store_tile(first, x, j, geometry[0][0], geometry[0][3], moved)

    stage(base, speed, term, ny, x_lo, x_hi, y_lo, finish_one)

    ny2, x_lo2, x_hi2, y_lo2 = geometry[1]

    def finish_two(x, j, u, moved):
        store_tile(
            second, x, j, ny2, y_lo2, 0.75 * load_tile(base, x, j, ny2, y_lo2) + 0.25 * moved
        )

    stage(first, speed, term, ny2, x_lo2, x_hi2, y_lo2, finish_two)

    ny3, x_lo3, x_hi3, y_lo3 = geometry[2]

    def finish_three(x, j, u, moved):
        value = (1.0 / 3.0) * load_tile(base, x, j, ny3, y_lo3) + (2.0 / 3.0) * moved
        if next_width:
            out[pl.ds((x - XO) * CY + j, 8, stride=ny3), :] = value
        else:
            store_tile(first, x, j, ny3, y_lo3, value)

    stage(second, speed, term, ny3, x_lo3, x_hi3, y_lo3, finish_three)

    if next_width:
        rows = next_width * CY
        out_low[...] = out[pl.ds(0, rows), :]
        out_high[...] = out[pl.ds(COLS - rows, rows), :]
        return

    def sweep(src, margin, store):
        ny = (CY + 2 * margin + 7) // 8
        y_lo = YO - margin

        def body(x, carry):
            u = [load_tile(src, x, j, ny, y_lo) for j in range(-1, ny + 1)]
            for j in range(ny):
                v = u[j + 1]
                advected = load_tile(first, x, j, ny, y_lo)
                sign = sign_of(advected)
                total = upwind(sign, v - u[j], v - u[j + 2])
                total += upwind(
                    sign,
                    v - load_tile(src, x - 1, j, ny, y_lo),
                    v - load_tile(src, x + 1, j, ny, y_lo),
                )
                total += upwind(sign, v - prev_z(v), v - next_z(v))
                smooth = advected * lax.rsqrt(advected * advected + 1.0)
                store(x, j, ny, y_lo, v - PSEUDO_STEP * smooth * (root(total) - 1.0))
            return carry

        lax.fori_loop(XO - margin, XO + CX + margin, body, 0)

    sweep(first, 1, lambda x, j, ny, y_lo, v: store_tile(second, x, j, ny, y_lo, v))

    def store_out(x, j, ny, y_lo, v):
        out[pl.ds((x - XO) * CY + j, 8, stride=ny), :] = v

    sweep(second, 0, store_out)


def step_call(width, next_width, pieces, speed):
    make_speed = isinstance(speed, tuple)
    outs = [shape(COLS)]
    if next_width:
        outs += [shape(next_width * CY)] * 2
    if make_speed:
        outs += [shape(EXT)]
        operands = (*pieces, *speed)
    else:
        operands = (*pieces, speed)
    return pl.pallas_call(
        functools.partial(runge_kutta, width, next_width, make_speed),
        out_shape=tuple(outs),
        scratch_shapes=[vmem(EXT), vmem(EXT), vmem(EXT), vmem(XR * 56)],
        compiler_params=params(),
        name="step",
    )(*operands)


def split(x):
    high = x.astype(jnp.bfloat16)
    low = (x - high.astype(F32)).astype(jnp.bfloat16)
    return jnp.concatenate([high, low], axis=1)


def onehot(mask):
    return jnp.where(mask, 1.0, 0.0).astype(jnp.bfloat16)


def pack_kernel(rows, owner, column, send, parts):
    count = rows.shape[0]
    own = owner[...]
    tags = onehot(lax.broadcasted_iota(jnp.int32, (DEVICES, count), 0) == own)
    order = onehot(
        lax.broadcasted_iota(jnp.int32, (count, count), 0)
        < lax.broadcasted_iota(jnp.int32, (count, count), 1)
    )
    earlier = jnp.dot(tags, order, preferred_element_type=F32)
    rank = jnp.sum(earlier * tags.astype(F32), axis=0, keepdims=True).astype(jnp.int32)
    target = own * SLOTS + rank
    parts[...] = split(rows[...])

    block = 128

    def body(b, carry):
        slot = lax.broadcasted_iota(jnp.int32, (block, count), 0) + b * block
        both = jnp.dot(onehot(slot == target), parts[...], preferred_element_type=F32)
        send[pl.ds(pl.multiple_of(b * block, block), block), :] = both[:, :NZ] + both[:, NZ:]
        return carry

    lax.fori_loop(0, DEVICES * SLOTS // block, body, 0)

    place = lax.broadcasted_iota(jnp.int32, (NZ, count), 0) == rank
    number = column[...] + 1
    dims = (((1,), (1,)), ((), ()))
    total = jnp.zeros((DEVICES, NZ), F32)
    for part, scale in ((number >> 6, 64.0), (number & 63, 1.0)):
        held = jnp.where(place, part.astype(F32), 0.0).astype(jnp.bfloat16)
        total += scale * lax.dot_general(tags, held, dims, preferred_element_type=F32)
    for b in range(DEVICES // 8):
        send[pl.ds(b * 8 * SLOTS + CAP, 8, stride=SLOTS), :] = total[8 * b : 8 * b + 8]


def unpack_kernel(low_rows, got, mask, speed, speed_low, speed_high, parts, number):
    for b in range(DEVICES // 8):
        number[pl.ds(8 * b, 8), :] = got[pl.ds(b * 8 * SLOTS + CAP, 8, stride=SLOTS), :]
    columns = number[...].T.astype(jnp.int32) - 1
    for k in range(CAP):
        for b in range(DEVICES // 16):
            pair = [
                got[pl.ds((b * 16 + 8 * i) * SLOTS + k, 8, stride=SLOTS), :] for i in range(2)
            ]
            parts[pl.ds(k * DEVICES + 16 * b, 16), :] = split(jnp.concatenate(pair, axis=0))
    named = jnp.concatenate([columns[k : k + 1, :] for k in range(CAP)], axis=1)

    block = 128

    def body(b, carry):
        cell = lax.broadcasted_iota(jnp.int32, (block, CAP * DEVICES), 0) + b * block
        both = jnp.dot(onehot(cell == named), parts[...], preferred_element_type=F32)
        at = pl.ds(pl.multiple_of(b * block, block), block)
        speed[at, :] = (both[:, :NZ] + both[:, NZ:]) * mask[at, :]
        return carry

    lax.fori_loop(0, COLS // block, body, 0)
    speed_low[...] = speed[pl.ds(0, low_rows), :]
    speed_high[...] = speed[pl.ds(COLS - low_rows, low_rows), :]


def shards(level_set, band_mask, rows, row_owner, row_tile):
    count = rows.shape[0]
    send = pl.pallas_call(
        pack_kernel,
        out_shape=shape(DEVICES * SLOTS),
        scratch_shapes=[pltpu.VMEM((count, 2 * NZ), jnp.bfloat16)],
        compiler_params=params(),
        name="pack",
    )(rows, row_owner.reshape(1, count), row_tile.reshape(1, count))
    got = lax.all_to_all(send, ("gx", "gy"), split_axis=0, concat_axis=0, tiled=True)

    u = level_set.reshape(COLS, NZ)
    pieces = halo(u, u[: 9 * CY], u[COLS - 9 * CY :], 9)

    mask = band_mask.astype(F32).reshape(COLS, 1)
    face = SPEED_HALO * CY
    speed, speed_low, speed_high = pl.pallas_call(
        functools.partial(unpack_kernel, face),
        out_shape=(shape(COLS), shape(face), shape(face)),
        scratch_shapes=[pltpu.VMEM((CAP * DEVICES, 2 * NZ), jnp.bfloat16), vmem(DEVICES)],
        compiler_params=params(),
        name="unpack",
    )(got, mask)
    speed_pieces = halo(speed, speed_low, speed_high, SPEED_HALO)

    u, low, high, speed = step_call(9, 9, pieces, speed_pieces)
    u, low, high = step_call(9, 11, halo(u, low, high, 9), speed)
    (u,) = step_call(11, 0, halo(u, low, high, 11), speed)
    return u.reshape(CX, CY, NZ)


def solution(mesh):
    return jax.shard_map(
        shards,
        mesh=mesh,
        in_specs=(
            P("gx", "gy", None),
            P("gx", "gy"),
            P(("gx", "gy"), None),
            P(("gx", "gy"), None),
            P(("gx", "gy")),
        ),
        out_specs=P("gx", "gy", None),
        check_vma=False,
    )
```

time: 479 us -> 277 us (0.58); the launches traced: 471 us -> 276 us
  other arithmetic: 245 us -> 0.01 us
  Pallas kernels: 0 us -> 165 us
  starting transfers between devices: 90 us -> 39.8 us
  local copies, waits for them, and re-layouts: 48.3 us -> 7.8 us
  waiting for transfers between devices: 86.4 us -> 63.4 us
    add x11 -> x0, other arithmetic: 228 us -> none  [the longest x3 74.8 us: advance(): return state + TIME_STEP * hj_rate(interior(section_halo(state), 3), speed)]
    pallas_call x0 -> x9, Pallas kernels: none -> 165 us  [the longest x3 151 us: step_call(): pl.pallas_call(functools.partial(runge_kutta, width, next_width, make_spe...]
    ppermute x44 -> x16, starting transfers between devices: 70.6 us -> 29.2 us  [shift_pair(): return (lax.ppermute(high, axis, up), lax.ppermute(low, axis, down))]
    slice x70 -> x1, local copies, waits for them, and re-layouts: 33.6 us -> 0.03 us  [shards(): pieces = halo(u, u[:9 * CY], u[COLS - 9 * CY:], 9)]
    ppermute x44 -> x16, waiting for transfers between devices: 77.3 us -> 45.1 us  [shift_pair(): return (lax.ppermute(high, axis, up), lax.ppermute(low, axis, down))]
    scatter-add x1 -> x0, other arithmetic: 12.4 us -> none  [place_rows(): velocity = jnp.zeros((columns, depth), jnp.float32).at[got_tile.reshape(-...]
    all_to_all x2 -> x1, waiting for transfers between devices: 9.15 us -> 18.2 us  [shards(): lax.all_to_all(send, ('gx', 'gy'), split_axis=0, concat_axis=0, tiled=True)]
    scatter x2 -> x0, local copies, waits for them, and re-layouts: 8.96 us -> none  [the longest x1 4.48 us: place_rows(): jnp.zeros((devices * capacity, depth), jnp.float32).at[target].set(rows)]
  transfers between devices with their start and end apart: 46 -> 17, of which waited for: 31 -> 13; matrix products, arithmetic and copies ran while one was open for 10% -> 0% of each run, Pallas kernels for 0% -> 3%
where the time goes in v1:
time: 277 us; the launch traced here: 276 us
  Pallas kernels  165 us (60%)
  waiting for transfers between devices  63.4 us (23%)
  starting transfers between devices  39.8 us (14%)
  local copies, waits for them, and re-layouts  7.8 us (3%)
    pallas_call x3, Pallas kernels, step_call(): pl.pallas_call(functools.partial(runge_kutta, width, next_width, make_spe...  151 us
    ppermute x16, waiting for transfers between devices, shift_pair(): return (lax.ppermute(high, axis, up), lax.ppermute(low, axis, down))  45.1 us
    ppermute x16, starting transfers between devices, shift_pair(): return (lax.ppermute(high, axis, up), lax.ppermute(low, axis, down))  29.2 us
    all_to_all x1, waiting for transfers between devices, shards(): lax.all_to_all(send, ('gx', 'gy'), split_axis=0, concat_axis=0, tiled=True)  18.2 us
    all_to_all x1, starting transfers between devices, shards(): lax.all_to_all(send, ('gx', 'gy'), split_axis=0, concat_axis=0, tiled=True)  10.7 us
    pallas_call x1, Pallas kernels, shards(): pl.pallas_call(functools.partial(unpack_kernel, face), out_shape=(shape(C...  6.38 us
  transfers between devices with their start and end apart: 17, of which 13 were waited for; matrix products, arithmetic and copies ran while one was open for 0% of the time, Pallas kernels for 3%

profile of v1, /device:TPU:24, one launch (start us, length us, event | category | flops | bytes accessed | tf_op | source)
XLA Modules:
  0.0 276.5 jit_solution(15276615644375571105)
XLA Ops:
  0.0 1.0 copy-done.2
  1.0 0.7 copy-done.3
  1.7 0.7 copy-done.4
  2.4 4.8 %pack.1 = f32[2176,128]{1,0:T(8,128)S(1)} custom-call(f32[1024,128]{1,0:T(8,128)S(1)} %copy-done.2, s32[1,1024]{1,0:T(1,128)S(1)} %bitcast.8, s32[1,1024]{1,0:T(1,128)S(1)} %bitcast.9), custom_call_target="tpu_custom_call" | custom-call | tf_op jit(solution)/shard_map/pack/pallas_call | solution.py:467
  7.3 1.3 all_to_all.7
  8.5 10.7 %all-to-all-start = ((f32[128,17,128]{2,1,0:T(8,128)}), f32[128,17,128]{2,1,0:T(8,128)}, u32[]{:S(2)}, u32[]{:S(2)}) async-start(f32[128,17,128]{2,1,0:T(8,128)} %all_to_all.7), calls=%async_computation | async-start | bytes 3145728 | tf_op jit(solution)/shard_map/all_to_all | solution.py:474
  19.2 0.2 collective-permute-start
  19.5 4.1 %collective-permute-start.1 = (f32[360,128]{1,0:T(8,128)S(1)}, f32[360,128]{1,0:T(8,128)S(1)}, u32[]{:S(2)}, u32[]{:S(2)}) collective-permute-start(f32[360,128]{1,0:T(8,128)S(1)} %bitcast.10), channel_id=1, source_target_pairs={{8,0},{16,8},{24,16},{32,24},{40,32},{48,40},{56,48},{64,56},{72,6... | collective-permute-start | bytes 552968 | tf_op jit(solution)/shard_map/ppermute | solution.py:258
  23.6 0.1 copy.7
  23.6 0.4 reshape.24.mask
  24.0 18.2 %all-to-all-done = f32[128,17,128]{2,1,0:T(8,128)} async-done(((f32[128,17,128]{2,1,0:T(8,128)}), f32[128,17,128]{2,1,0:T(8,128)}, u32[]{:S(2)}, u32[]{:S(2)}) %all-to-all-start) | async-done | bytes 1114144 | tf_op jit(solution)/shard_map/all_to_all | solution.py:474
  42.3 2.4 all_to_all.9.got
  44.7 1.2 copy-done.1
  45.9 6.4 %unpack.1 = (f32[2560,128]{1,0:T(8,128)S(1)}, f32[320,128]{1,0:T(8,128)S(1)}, f32[320,128]{1,0:T(8,128)S(1)}) custom-call(f32[2176,128]{1,0:T(8,128)S(1)} %copy-done.1, f32[2560,1]{1,0:T(8,128)S(1)} %reshape.24.mask), custom_call_target="tpu_custom_call" | custom-call | tf_op jit(solution)/shard_map/unpack/pallas_call | solution.py:481
  52.3 0.1 collective-permute-start.4
  52.4 3.8 %collective-permute-start.5 = (f32[320,128]{1,0:T(8,128)S(1)}, f32[320,128]{1,0:T(8,128)S(1)}, u32[]{:S(2)}, u32[]{:S(2)}) collective-permute-start(f32[320,128]{1,0:T(8,128)S(1)} %get-tuple-element.27), channel_id=1, source_target_pairs={{8,0},{16,8},{24,16},{32,24},{40,32},{48,40},{56,48},{64,56},{72,6... | collective-permute-start | bytes 491528 | tf_op jit(solution)/shard_map/ppermute | solution.py:258
  56.2 0.0 collective-permute-done.before.refs_1_
  56.2 0.7 sides.4
  56.9 3.5 %collective-permute-start.2 = (f32[792,128]{1,0:T(8,128)S(1)}, f32[792,128]{1,0:T(8,128)S(1)}, u32[]{:S(2)}, u32[]{:S(2)}) collective-permute-start(f32[792,128]{1,0:T(8,128)S(1)} %get-tuple-element.23), channel_id=1, source_target_pairs={{0,1},{1,2},{2,3},{3,4},{4,5},{5,6},{6,7},{7,0},{8,9},{9,10},{10,1... | collective-permute-start | bytes 1216520 | tf_op jit(solution)/shard_map/ppermute | solution.py:258
  60.4 0.3 collective-permute-done.5.after.refs_7_
  60.7 0.6 sides.5
  61.3 5.4 %collective-permute-start.6 = (f32[704,128]{1,0:T(8,128)S(1)}, f32[704,128]{1,0:T(8,128)S(1)}, u32[]{:S(2)}, u32[]{:S(2)}) collective-permute-start(f32[704,128]{1,0:T(8,128)S(1)} %get-tuple-element.28), channel_id=1, source_target_pairs={{0,1},{1,2},{2,3},{3,4},{4,5},{5,6},{6,7},{7,0},{8,9},{9,10},{10,1... | collective-permute-start | bytes 1081352 | tf_op jit(solution)/shard_map/ppermute | solution.py:258
  66.7 0.0 collective-permute-start.7
  66.7 3.5 %collective-permute-done.2.refs_3_ = f32[792,128]{1,0:T(8,128)S(1)} collective-permute-done((f32[792,128]{1,0:T(8,128)S(1)}, f32[792,128]{1,0:T(8,128)S(1)}, u32[]{:S(2)}, u32[]{:S(2)}) %collective-permute-start.2) | collective-permute-done | bytes 405536 | tf_op jit(solution)/shard_map/ppermute | solution.py:258
  70.2 4.5 %collective-permute-done.3.refs_4_ = f32[792,128]{1,0:T(8,128)S(1)} collective-permute-done((f32[792,128]{1,0:T(8,128)S(1)}, f32[792,128]{1,0:T(8,128)S(1)}, u32[]{:S(2)}, u32[]{:S(2)}) %collective-permute-start.3) | collective-permute-done | bytes 405536 | tf_op jit(solution)/shard_map/ppermute | solution.py:258
  74.8 0.7 collective-permute-done.6.refs_8_
  75.5 4.2 %collective-permute-done.7.refs_9_ = f32[704,128]{1,0:T(8,128)S(1)} collective-permute-done((f32[704,128]{1,0:T(8,128)S(1)}, f32[704,128]{1,0:T(8,128)S(1)}, u32[]{:S(2)}, u32[]{:S(2)}) %collective-permute-start.7) | collective-permute-done | bytes 360480 | tf_op jit(solution)/shard_map/ppermute | solution.py:258
  79.7 44.3 %step.3 = (f32[2560,128]{1,0:T(8,128)S(1)}, f32[360,128]{1,0:T(8,128)S(1)}, f32[360,128]{1,0:T(8,128)S(1)}, f32[6336,128]{1,0:T(8,128)S(1)}) custom-call(f32[2560,128]{1,0:T(8,128)S(1)} %bitcast.7, f32[360,128]{1,0:T(8,128)S(1)} %collective-permute-done.before.refs_1_, f32[360,128]{1,0:T(8,128)S(1)} %collective-permute-done.1.after.refs_2_, ...), custom_call_target="tpu_custom_call" | custom-call | tf_op jit(solution)/shard_map/step/pallas_call | solution.py:386
  124.0 0.1 collective-permute-start.8
  124.0 3.8 %collective-permute-start.9 = (f32[360,128]{1,0:T(8,128)S(1)}, f32[360,128]{1,0:T(8,128)S(1)}, u32[]{:S(2)}, u32[]{:S(2)}) collective-permute-start(f32[360,128]{1,0:T(8,128)S(1)} %get-tuple-element.32), channel_id=1, source_target_pairs={{8,0},{16,8},{24,16},{32,24},{40,32},{48,40},{56,48},{64,56},{72,6... | collective-permute-start | bytes 552968 | tf_op jit(solution)/shard_map/ppermute | solution.py:258
  127.9 3.2 %collective-permute-done.8.before.refs_1_ = f32[360,128]{1,0:T(8,128)S(1)} collective-permute-done((f32[360,128]{1,0:T(8,128)S(1)}, f32[360,128]{1,0:T(8,128)S(1)}, u32[]{:S(2)}, u32[]{:S(2)}) %collective-permute-start.8) | collective-permute-done | bytes 184352 | tf_op jit(solution)/shard_map/ppermute | solution.py:258
  131.1 0.0 collective-permute-done.9.after.refs_2_
  131.1 0.7 sides.6
  131.8 2.0 collective-permute-start.10
  133.8 0.1 collective-permute-start.11
  133.9 8.0 %collective-permute-done.10.refs_3_ = f32[792,128]{1,0:T(8,128)S(1)} collective-permute-done((f32[792,128]{1,0:T(8,128)S(1)}, f32[792,128]{1,0:T(8,128)S(1)}, u32[]{:S(2)}, u32[]{:S(2)}) %collective-permute-start.10) | collective-permute-done | bytes 405536 | tf_op jit(solution)/shard_map/ppermute | solution.py:258
  141.9 3.9 %collective-permute-done.11.refs_4_ = f32[792,128]{1,0:T(8,128)S(1)} collective-permute-done((f32[792,128]{1,0:T(8,128)S(1)}, f32[792,128]{1,0:T(8,128)S(1)}, u32[]{:S(2)}, u32[]{:S(2)}) %collective-permute-start.11) | collective-permute-done | bytes 405536 | tf_op jit(solution)/shard_map/ppermute | solution.py:258
  145.7 43.6 %step.4 = (f32[2560,128]{1,0:T(8,128)S(1)}, f32[440,128]{1,0:T(8,128)S(1)}, f32[440,128]{1,0:T(8,128)S(1)}) custom-call(f32[2560,128]{1,0:T(8,128)S(1)} %get-tuple-element.30.own.refs_0_, f32[360,128]{1,0:T(8,128)S(1)} %collective-permute-done.8.before.refs_1_, f32[360,128]{1,0:T(8,128)S(1)} %collective-permute-done.9.after.refs_2_, ...), custom_call_target="tpu_custom_call" | custom-call | tf_op jit(solution)/shard_map/step/pallas_call | solution.py:386
  189.4 0.1 collective-permute-start.12
  189.4 3.8 %collective-permute-start.13 = (f32[440,128]{1,0:T(8,128)S(1)}, f32[440,128]{1,0:T(8,128)S(1)}, u32[]{:S(2)}, u32[]{:S(2)}) collective-permute-start(f32[440,128]{1,0:T(8,128)S(1)} %get-tuple-element.38), channel_id=1, source_target_pairs={{8,0},{16,8},{24,16},{32,24},{40,32},{48,40},{56,48},{64,56},{72,6... | collective-permute-start | bytes 675848 | tf_op jit(solution)/shard_map/ppermute | solution.py:258
  193.3 3.7 %collective-permute-done.12.before.refs_1_ = f32[440,128]{1,0:T(8,128)S(1)} collective-permute-done((f32[440,128]{1,0:T(8,128)S(1)}, f32[440,128]{1,0:T(8,128)S(1)}, u32[]{:S(2)}, u32[]{:S(2)}) %collective-permute-start.12) | collective-permute-done | bytes 225312 | tf_op jit(solution)/shard_map/ppermute | solution.py:258
  196.9 0.2 collective-permute-done.13.after.refs_2_
  197.1 0.7 sides.7
  197.8 0.1 collective-permute-start.14
  197.9 2.0 collective-permute-start.15
  199.9 9.3 %collective-permute-done.14.refs_3_ = f32[968,128]{1,0:T(8,128)S(1)} collective-permute-done((f32[968,128]{1,0:T(8,128)S(1)}, f32[968,128]{1,0:T(8,128)S(1)}, u32[]{:S(2)}, u32[]{:S(2)}) %collective-permute-start.14) | collective-permute-done | bytes 495648 | tf_op jit(solution)/shard_map/ppermute | solution.py:258
  209.2 3.7 %collective-permute-done.15.refs_4_ = f32[968,128]{1,0:T(8,128)S(1)} collective-permute-done((f32[968,128]{1,0:T(8,128)S(1)}, f32[968,128]{1,0:T(8,128)S(1)}, u32[]{:S(2)}, u32[]{:S(2)}) %collective-permute-start.15) | collective-permute-done | bytes 495648 | tf_op jit(solution)/shard_map/ppermute | solution.py:258
  212.9 63.6 %step.5 = f32[2560,128]{1,0:T(8,128)} custom-call(f32[2560,128]{1,0:T(8,128)S(1)} %get-tuple-element.36.own.refs_0_, f32[440,128]{1,0:T(8,128)S(1)} %collective-permute-done.12.before.refs_1_, f32[440,128]{1,0:T(8,128)S(1)} %collective-permute-done.13.after.refs_2_, f32[968,128]{1,0:T(8,128)S(1)} %collective-permute-done.14.refs_3_, ...), custom_call_target="tpu_custom_call" | custom-call | tf_op jit(solution)/shard_map/step/pallas_call | solution.py:386
  (13 shorter events, 0.1 us)
Async XLA Ops:
  0.0 1.0 copy-start.2
  1.0 0.7 copy-start.3
  1.7 0.7 copy-start.4
  8.5 10.7 %copy-start = (f32[64,40,128]{2,1,0:T(8,128)S(1)}, f32[64,40,128]{2,1,0:T(8,128)}, u32[]{:S(2)}) copy-start(f32[64,40,128]{2,1,0:T(8,128)} %param.5) | copy-start | bytes 3932164
  8.5 15.0 %copy-start.5 = (s32[64,40]{0,1:T(8,128)S(1)}, s32[64,40]{0,1:T(8,128)}, u32[]{:S(2)}) copy-start(s32[64,40]{0,1:T(8,128)} %param.6) | copy-start | bytes 30724
  8.5 33.8 %all-to-all-start = ((f32[128,17,128]{2,1,0:T(8,128)}), f32[128,17,128]{2,1,0:T(8,128)}, u32[]{:S(2)}, u32[]{:S(2)}) async-start(f32[128,17,128]{2,1,0:T(8,128)} %all_to_all.7), calls=%async_computation | async-start | bytes 3145728 | tf_op jit(solution)/shard_map/all_to_all | solution.py:474
  19.2 37.0 %collective-permute-start = (f32[360,128]{1,0:T(8,128)S(1)}, f32[360,128]{1,0:T(8,128)S(1)}, u32[]{:S(2)}, u32[]{:S(2)}) collective-permute-start(f32[360,128]{1,0:T(8,128)S(1)} %bitcast.11), channel_id=1, source_target_pairs={{0,8},{8,16},{16,24},{24,32},{32,40},{40,48},{48,56},{56,64},{64,7... | collective-permute-start | bytes 552968 | tf_op jit(solution)/shard_map/ppermute | solution.py:258
  19.5 36.8 %collective-permute-start.1 = (f32[360,128]{1,0:T(8,128)S(1)}, f32[360,128]{1,0:T(8,128)S(1)}, u32[]{:S(2)}, u32[]{:S(2)}) collective-permute-start(f32[360,128]{1,0:T(8,128)S(1)} %bitcast.10), channel_id=1, source_target_pairs={{8,0},{16,8},{24,16},{32,24},{40,32},{48,40},{56,48},{64,56},{72,6... | collective-permute-start | bytes 552968 | tf_op jit(solution)/shard_map/ppermute | solution.py:258
  44.7 1.2 copy-start.1
  52.3 8.1 %collective-permute-start.4 = (f32[320,128]{1,0:T(8,128)S(1)}, f32[320,128]{1,0:T(8,128)S(1)}, u32[]{:S(2)}, u32[]{:S(2)}) collective-permute-start(f32[320,128]{1,0:T(8,128)S(1)} %get-tuple-element.26), channel_id=1, source_target_pairs={{0,8},{8,16},{16,24},{24,32},{32,40},{40,48},{48,56},{56,64},{64,7... | collective-permute-start | bytes 491528 | tf_op jit(solution)/shard_map/ppermute | solution.py:258
  52.4 8.3 %collective-permute-start.5 = (f32[320,128]{1,0:T(8,128)S(1)}, f32[320,128]{1,0:T(8,128)S(1)}, u32[]{:S(2)}, u32[]{:S(2)}) collective-permute-start(f32[320,128]{1,0:T(8,128)S(1)} %get-tuple-element.27), channel_id=1, source_target_pairs={{8,0},{16,8},{24,16},{32,24},{40,32},{48,40},{56,48},{64,56},{72,6... | collective-permute-start | bytes 491528 | tf_op jit(solution)/shard_map/ppermute | solution.py:258
  56.9 13.3 %collective-permute-start.2 = (f32[792,128]{1,0:T(8,128)S(1)}, f32[792,128]{1,0:T(8,128)S(1)}, u32[]{:S(2)}, u32[]{:S(2)}) collective-permute-start(f32[792,128]{1,0:T(8,128)S(1)} %get-tuple-element.23), channel_id=1, source_target_pairs={{0,1},{1,2},{2,3},{3,4},{4,5},{5,6},{6,7},{7,0},{8,9},{9,10},{10,1... | collective-permute-start | bytes 1216520 | tf_op jit(solution)/shard_map/ppermute | solution.py:258
  60.4 14.4 %collective-permute-start.3 = (f32[792,128]{1,0:T(8,128)S(1)}, f32[792,128]{1,0:T(8,128)S(1)}, u32[]{:S(2)}, u32[]{:S(2)}) collective-permute-start(f32[792,128]{1,0:T(8,128)S(1)} %get-tuple-element.24), channel_id=1, source_target_pairs={{1,0},{2,1},{3,2},{4,3},{5,4},{6,5},{7,6},{0,7},{9,8},{10,9},{11,1... | collective-permute-start | bytes 1216520 | tf_op jit(solution)/shard_map/ppermute | solution.py:258
  61.3 14.2 %collective-permute-start.6 = (f32[704,128]{1,0:T(8,128)S(1)}, f32[704,128]{1,0:T(8,128)S(1)}, u32[]{:S(2)}, u32[]{:S(2)}) collective-permute-start(f32[704,128]{1,0:T(8,128)S(1)} %get-tuple-element.28), channel_id=1, source_target_pairs={{0,1},{1,2},{2,3},{3,4},{4,5},{5,6},{6,7},{7,0},{8,9},{9,10},{10,1... | collective-permute-start | bytes 1081352 | tf_op jit(solution)/shard_map/ppermute | solution.py:258
  66.7 12.9 %collective-permute-start.7 = (f32[704,128]{1,0:T(8,128)S(1)}, f32[704,128]{1,0:T(8,128)S(1)}, u32[]{:S(2)}, u32[]{:S(2)}) collective-permute-start(f32[704,128]{1,0:T(8,128)S(1)} %get-tuple-element.29), channel_id=1, source_target_pairs={{1,0},{2,1},{3,2},{4,3},{5,4},{6,5},{7,6},{0,7},{9,8},{10,9},{11,1... | collective-permute-start | bytes 1081352 | tf_op jit(solution)/shard_map/ppermute | solution.py:258
  124.0 7.1 %collective-permute-start.8 = (f32[360,128]{1,0:T(8,128)S(1)}, f32[360,128]{1,0:T(8,128)S(1)}, u32[]{:S(2)}, u32[]{:S(2)}) collective-permute-start(f32[360,128]{1,0:T(8,128)S(1)} %get-tuple-element.31), channel_id=1, source_target_pairs={{0,8},{8,16},{16,24},{24,32},{32,40},{40,48},{48,56},{56,64},{64,7... | collective-permute-start | bytes 552968 | tf_op jit(solution)/shard_map/ppermute | solution.py:258
  124.0 7.1 %collective-permute-start.9 = (f32[360,128]{1,0:T(8,128)S(1)}, f32[360,128]{1,0:T(8,128)S(1)}, u32[]{:S(2)}, u32[]{:S(2)}) collective-permute-start(f32[360,128]{1,0:T(8,128)S(1)} %get-tuple-element.32), channel_id=1, source_target_pairs={{8,0},{16,8},{24,16},{32,24},{40,32},{48,40},{56,48},{64,56},{72,6... | collective-permute-start | bytes 552968 | tf_op jit(solution)/shard_map/ppermute | solution.py:258
  131.8 10.1 %collective-permute-start.10 = (f32[792,128]{1,0:T(8,128)S(1)}, f32[792,128]{1,0:T(8,128)S(1)}, u32[]{:S(2)}, u32[]{:S(2)}) collective-permute-start(f32[792,128]{1,0:T(8,128)S(1)} %get-tuple-element.33), channel_id=1, source_target_pairs={{0,1},{1,2},{2,3},{3,4},{4,5},{5,6},{6,7},{7,0},{8,9},{9,10},{10,1... | collective-permute-start | bytes 1216520 | tf_op jit(solution)/shard_map/ppermute | solution.py:258
  133.8 12.0 %collective-permute-start.11 = (f32[792,128]{1,0:T(8,128)S(1)}, f32[792,128]{1,0:T(8,128)S(1)}, u32[]{:S(2)}, u32[]{:S(2)}) collective-permute-start(f32[792,128]{1,0:T(8,128)S(1)} %get-tuple-element.34), channel_id=1, source_target_pairs={{1,0},{2,1},{3,2},{4,3},{5,4},{6,5},{7,6},{0,7},{9,8},{10,9},{11,1... | collective-permute-start | bytes 1216520 | tf_op jit(solution)/shard_map/ppermute | solution.py:258
  189.4 7.6 %collective-permute-start.12 = (f32[440,128]{1,0:T(8,128)S(1)}, f32[440,128]{1,0:T(8,128)S(1)}, u32[]{:S(2)}, u32[]{:S(2)}) collective-permute-start(f32[440,128]{1,0:T(8,128)S(1)} %get-tuple-element.37), channel_id=1, source_target_pairs={{0,8},{8,16},{16,24},{24,32},{32,40},{40,48},{48,56},{56,64},{64,7... | collective-permute-start | bytes 675848 | tf_op jit(solution)/shard_map/ppermute | solution.py:258
  189.4 7.7 %collective-permute-start.13 = (f32[440,128]{1,0:T(8,128)S(1)}, f32[440,128]{1,0:T(8,128)S(1)}, u32[]{:S(2)}, u32[]{:S(2)}) collective-permute-start(f32[440,128]{1,0:T(8,128)S(1)} %get-tuple-element.38), channel_id=1, source_target_pairs={{8,0},{16,8},{24,16},{32,24},{40,32},{48,40},{56,48},{64,56},{72,6... | collective-permute-start | bytes 675848 | tf_op jit(solution)/shard_map/ppermute | solution.py:258
  197.8 11.4 %collective-permute-start.14 = (f32[968,128]{1,0:T(8,128)S(1)}, f32[968,128]{1,0:T(8,128)S(1)}, u32[]{:S(2)}, u32[]{:S(2)}) collective-permute-start(f32[968,128]{1,0:T(8,128)S(1)} %get-tuple-element.39), channel_id=1, source_target_pairs={{0,1},{1,2},{2,3},{3,4},{4,5},{5,6},{6,7},{7,0},{8,9},{9,10},{10,1... | collective-permute-start | bytes 1486856 | tf_op jit(solution)/shard_map/ppermute | solution.py:258
  197.9 15.0 %collective-permute-start.15 = (f32[968,128]{1,0:T(8,128)S(1)}, f32[968,128]{1,0:T(8,128)S(1)}, u32[]{:S(2)}, u32[]{:S(2)}) collective-permute-start(f32[968,128]{1,0:T(8,128)S(1)} %get-tuple-element.40), channel_id=1, source_target_pairs={{1,0},{2,1},{3,2},{4,3},{5,4},{6,5},{7,6},{0,7},{9,8},{10,9},{11,1... | collective-permute-start | bytes 1486856 | tf_op jit(solution)/shard_map/ppermute | solution.py:258

commit v2 on v1

v2 whole, which is shorter than its diff:
```python
import functools

import jax
import jax.numpy as jnp
from jax import lax
from jax.experimental import pallas as pl
from jax.experimental.pallas import tpu as pltpu
from jax.sharding import PartitionSpec as P

EPSILON = 1e-06
TIME_STEP = 0.2
PSEUDO_STEP = 0.3

CX, CY, NZ = 64, 40, 128
DEVICES = 128
CAP = 16
SLOTS = CAP + 1
COLS = CX * CY

XO, YO = 12, 16
XR, YP = 88, 72
EXT = XR * YP
SPEED_HALO = 8
VMEM_LIMIT = 40 * 1024 * 1024
F32 = jnp.float32


def rcp(x):
    return pl.reciprocal(x, approx=True)


QUARTER = 0.25 * EPSILON


def pair_weights(e_left, e_right, g):
    total = e_left + e_right
    half = 0.5 * total
    square = g * g
    centre = half * half + (square * (13.0 / 12.0) + QUARTER)
    ends = centre + square
    cross = total * g
    ip = rcp(ends + cross)
    it = rcp(centre)
    im = rcp(ends - cross)
    return ip * ip, it * it * 3.0, im * im, half


def weight_end(half, g):
    i = rcp(half * half + (g * g * (13.0 / 12.0) + QUARTER))
    return i * i


def central(slope, sixth, half):
    base = slope + sixth
    return base + half, half - base


def face_values(p1, p2, p3, h_left, h_right, q_left, q_right):
    low = p1 * h_left
    high = p3 * h_right
    both = 0.5 * (p1 + p3) + p2
    twice = low + high
    twice = twice + twice
    left = q_left - (twice + high) * rcp(both + p3)
    right = q_right - (twice + low) * rcp(both + p1)
    return left, right


def upwind(sign, left, right):
    top = jnp.maximum(jnp.maximum(sign * left, sign * right), 0.0)
    return top * top


def sign_of(value):
    return jnp.where(value >= 0.0, 1.0, -1.0)


def speed_sign(pace):
    return jnp.where(pace <= 0.0, 1.0, -1.0)


def root(x):
    return x * lax.rsqrt(jnp.maximum(x, 1e-37))


def prev_z(x):
    return pltpu.roll(x, 1, 1)


def next_z(x):
    return pltpu.roll(x, NZ - 1, 1)


def z_slopes(u):
    after = next_z(u)
    return after - u, 0.5 * (after + prev_z(u)) - u


def z_faces(d, e):
    e_prev, e_next, e_after = prev_z(e), next_z(e), pltpu.roll(e, NZ - 2, 1)
    g_prev, g, g_next = e - e_prev, e_next - e, e_after - e_next
    sixth = g * (1.0 / 6.0)
    h = sixth - g_prev * (1.0 / 6.0)
    h_next = g_next * (1.0 / 6.0) - sixth
    half = 0.5 * (e + e_next)
    pp = weight_end(0.5 * (e_prev + e) + g_prev, g_prev)
    pt = weight_end(half, g) * 3.0
    pm = weight_end(0.5 * (e_next + e_after) - g_next, g_next)
    return face_values(pp, pt, pm, h, h_next, *central(d, sixth, half))


def y_terms(u, signs):
    n = len(u) - 6
    out = []
    d, e, sixth, h, pp, pt, pm, q, left = {}, {}, {}, {}, {}, {}, {}, {}, {}
    d[0] = u[1] - u[0]
    for k in range(1, n + 5):
        d[k] = u[k + 1] - u[k]
        e[k] = 0.5 * (d[k] - d[k - 1])
        if k >= 2:
            f = k - 1
            g = e[k] - e[f]
            sixth[f] = g * (1.0 / 6.0)
            pp[f], pt[f], pm[f], half = pair_weights(e[f], e[k], g)
            q[f] = central(d[f], sixth[f], half)
            if f >= 2:
                h[f] = sixth[f] - sixth[f - 1]
            if f >= 3:
                w = f - 1
                lw, rw = face_values(pp[w - 1], pt[w], pm[w + 1], h[w], h[w + 1], *q[w])
                left[w] = lw
                if w >= 3:
                    out.append(upwind(signs[w - 3], left[w - 1], rw))
    return out


GROUP = 4


def geometry(width, margin):
    count = (CX + 2 * margin + GROUP - 1) // GROUP * GROUP
    return ((CY + 2 * margin + 7) // 8, XO - margin, XO - margin + count, YO - margin)


def load_tile(ref, geo, x, j):
    return ref[pl.ds(x * YP + (geo[3] + j), 8, stride=geo[0]), :]


def store_tile(ref, geo, x, j, value):
    ref[pl.ds(x * YP + (geo[3] + j), 8, stride=geo[0]), :] = value


def store_slopes(slopes, geo, x, j, value):
    d, e = z_slopes(value)
    store_tile(slopes[0], geo, x, j, d)
    store_tile(slopes[1], geo, x, j, e)


def packed(geo, x, j):
    return pl.ds(pl.multiple_of(x * (8 * geo[0]) + 8 * j, 8), 8)


def over_rows(geo, row):
    def body(i, carry):
        for k in range(GROUP):
            row(geo[1] + i * GROUP + k)
        return carry

    lax.fori_loop(0, (geo[2] - geo[1]) // GROUP, body, 0)


def z_row(slopes, faces, geo, x, j):
    left, right = z_faces(load_tile(slopes[0], geo, x, j), load_tile(slopes[1], geo, x, j))
    faces[0][packed(geo, x, j), :] = left
    faces[1][packed(geo, x, j), :] = right


def y_pass(src, pace, geo, emit):
    ny = geo[0]

    def row(x):
        paces = [load_tile(pace, geo, x, j) for j in range(ny)]
        u = [load_tile(src, geo, x, j) for j in range(-3, ny + 3)]
        for j, value in enumerate(y_terms(u, [speed_sign(p) for p in paces])):
            emit(x, j, u[j + 3], paces[j], value)

    over_rows(geo, row)


def x_pass(src, pace, faces, geo, emit):
    ny, x_lo, x_hi, _ = geo
    unroll = (x_hi - x_lo) // 4

    def tile(x, j):
        return load_tile(src, geo, x, j)

    def advance(x, j, state):
        d, e, sixth, g, h, pp0, pp1, p2, ql, qr, left = state
        d2 = tile(x + 3, j) - tile(x + 2, j)
        e2 = 0.5 * (d2 - d)
        g2 = e2 - e
        sixth2 = g2 * (1.0 / 6.0)
        pp2, pt2, pm2, half = pair_weights(e, e2, g2)
        ql2, qr2 = central(d, sixth2, half)
        h2 = sixth2 - sixth
        left2, right = face_values(pp0, p2, pm2, h, h2, ql, qr)
        return left, right, (d2, e2, sixth2, g2, h2, pp1, pp2, pt2, ql2, qr2, left2)

    def column(j, carry):
        zero = jnp.zeros((8, NZ), F32)
        x = x_lo - 1
        u = [tile(x + k, j) for k in range(-2, 3)]
        ds = [u[k + 1] - u[k] for k in range(4)]
        es = [0.5 * (ds[k + 1] - ds[k]) for k in range(3)]
        g0, g1 = es[1] - es[0], es[2] - es[1]
        ppa, _, _, _ = pair_weights(es[0], es[1], g0)
        ppb, ptb, _, half = pair_weights(es[1], es[2], g1)
        s0, s1 = g0 * (1.0 / 6.0), g1 * (1.0 / 6.0)
        ql, qr = central(ds[2], s1, half)
        state = (ds[3], es[2], s1, g1, s1 - s0, ppa, ppb, ptb, ql, qr, zero)
        _, _, state = advance(x, j, state)

        def body(i, state):
            for k in range(unroll):
                x = x_lo + i * unroll + k
                left, right, state = advance(x, j, state)
                p = load_tile(pace, geo, x, j)
                sign = speed_sign(p)
                at = packed(geo, x, j)
                total = upwind(sign, left, right) + upwind(
                    sign, prev_z(faces[0][at, :]), faces[1][at, :]
                )
                emit(x, j, tile(x, j), p, total)
            return state

        lax.fori_loop(0, 4, body, state)
        return carry

    lax.fori_loop(0, ny, column, 0)


def stage(src, slopes, pace, term, faces, geo, finish):
    def keep(x, j, u, p, value):
        term[packed(geo, x, j), :] = value
        z_row(slopes, faces, geo, x, j)

    def join(x, j, u, p, value):
        finish(x, j, u, u + p * root(value + term[packed(geo, x, j), :]))

    y_pass(src, pace, geo, keep)
    x_pass(src, pace, faces, geo, join)


def fill_block(ext, own, before, after, width, slopes=None):
    def put(src, x_to, count, group):
        def body(n, carry):
            for k in range(group):
                x = n * group + k
                for i in range(CY // 8):
                    value = src[pl.ds(pl.multiple_of(x * CY + 8 * i, 8), 8), :]
                    at = pl.ds(pl.multiple_of((x + x_to) * YP + (YO + 8 * i), 8), 8)
                    ext[at, :] = value
                    if slopes:
                        slopes[0][at, :], slopes[1][at, :] = z_slopes(value)
            return carry

        lax.fori_loop(0, count // group, body, 0)

    put(own, XO, CX, 8)
    put(before, XO - width, width, width)
    put(after, XO + CX, width, width)


def fill_sides(ext, before, after, width, slopes=None):
    for t in range(width):
        for b in range(XR // 8):
            for src, y in ((before, YO - width + t), (after, YO + CY + t)):
                value = src[pl.ds(t * XR + 8 * b, 8), :]
                at = pl.ds(b * 8 * YP + y, 8, stride=YP)
                ext[at, :] = value
                if slopes:
                    slopes[0][at, :], slopes[1][at, :] = z_slopes(value)


def sides_kernel(width, own, before, after, low, high, ext):
    fill_block(ext, own, before, after, width)
    for t in range(width):
        for b in range(XR // 8):
            low[pl.ds(t * XR + 8 * b, 8), :] = ext[pl.ds(b * 8 * YP + (YO + t), 8, stride=YP), :]
            high[pl.ds(t * XR + 8 * b, 8), :] = ext[
                pl.ds(b * 8 * YP + (YO + CY - width + t), 8, stride=YP), :
            ]


def params():
    return pltpu.CompilerParams(vmem_limit_bytes=VMEM_LIMIT)


def shape(rows):
    return jax.ShapeDtypeStruct((rows, NZ), F32)


def vmem(rows):
    return pltpu.VMEM((rows, NZ), F32)


def shift_pair(low, high, axis):
    size = lax.axis_size(axis)
    up = [(i, (i + 1) % size) for i in range(size)]
    down = [(j, i) for i, j in up]
    return lax.ppermute(high, axis, up), lax.ppermute(low, axis, down)


def cross_x(own, low, high, width):
    before, after = shift_pair(low, high, "gx")
    side_low, side_high = pl.pallas_call(
        functools.partial(sides_kernel, width),
        out_shape=(shape(width * XR), shape(width * XR)),
        scratch_shapes=[vmem(EXT)],
        compiler_params=params(),
        cost_estimate=cost(1),
        name="sides",
    )(own, before, after)
    return (own, before, after), (side_low, side_high)


def cost(us):
    return pl.CostEstimate(
        flops=1000 * us, bytes_accessed=int(3.0e6 * us), transcendentals=0
    )


def own_geometry(width):
    _, x_lo, x_hi, _ = geometry(width, width - 3)
    return (CY // 8, x_lo, x_hi, YO)


def early_kernel(width, pace_ready, *refs):
    refs = list(refs)
    own, before, after = refs[:3]
    refs = refs[3:]
    if pace_ready:
        pace = refs.pop(0)
    else:
        p_own, p_before, p_after = refs[:3]
        refs = refs[3:]
    out, base = refs[:2]
    slopes, faces = refs[2:4], refs[4:6]
    if not pace_ready:
        pace = refs[6]
        fill_block(pace, p_own, p_before, p_after, SPEED_HALO)
    fill_block(base, own, before, after, width, slopes)
    geo = own_geometry(width)

    def row(x):
        for j in range(geo[0]):
            z_row(slopes, faces, geo, x, j)

    over_rows(geo, row)

    def emit(x, j, u, p, value):
        out[packed(geo, x, j), :] = value

    x_pass(base, pace, faces, geo, emit)


def early_call(width, pieces, pace):
    ready = not isinstance(pace, tuple)
    return pl.pallas_call(
        functools.partial(early_kernel, width, ready),
        out_shape=shape(XR * CY),
        scratch_shapes=[vmem(EXT)] * 3
        + [vmem(XR * CY)] * 2
        + ([] if ready else [vmem(EXT)]),
        compiler_params=params(),
        cost_estimate=cost(10),
        name="early",
    )(*pieces, *((pace,) if ready else pace))


def runge_kutta(width, next_width, make_pace, *refs):
    refs = list(refs)
    own, before, after, left, right, early = refs[:6]
    refs = refs[6:]
    if make_pace:
        p_own, p_before, p_after, p_left, p_right = refs[:5]
        refs = refs[5:]
    else:
        pace = refs.pop(0)
    out = refs.pop(0)
    if next_width:
        out_low, out_high = refs[:2]
        refs = refs[2:]
    if make_pace:
        pace = refs.pop(0)
    base, first, second = refs[:3]
    even, odd, term, faces = refs[3:5], refs[5:7], refs[7], refs[8:10]

    fill_block(base, own, before, after, width)
    fill_sides(base, left, right, width, even)
    if make_pace:
        fill_block(pace, p_own, p_before, p_after, SPEED_HALO)
        fill_sides(pace, p_left, p_right, SPEED_HALO)

    def finish_one(geo):
        def finish(x, j, u, moved):
            store_tile(first, geo, x, j, moved)
            store_slopes(odd, geo, x, j, moved)

        return finish

    inner = own_geometry(width)
    done = finish_one(inner)

    def join(x, j, u, p, value):
        done(x, j, u, u + p * root(value + early[packed(inner, x, j), :]))

    y_pass(base, pace, inner, join)
    for y_lo in (YO - 8, YO + CY):
        side = (1, inner[1], inner[2], y_lo)
        stage(base, even, pace, term, faces, side, finish_one(side))

    geo2 = geometry(width, width - 6)

    def finish_two(x, j, u, moved):
        value = 0.75 * load_tile(base, geo2, x, j) + 0.25 * moved
        store_tile(second, geo2, x, j, value)
        store_slopes(even, geo2, x, j, value)

    stage(first, odd, pace, term, faces, geo2, finish_two)

    geo3 = geometry(width, width - 9)

    def finish_three(x, j, u, moved):
        value = (1.0 / 3.0) * load_tile(base, geo3, x, j) + (2.0 / 3.0) * moved
        if next_width:
            out[pl.ds((x - XO) * CY + j, 8, stride=geo3[0]), :] = value
        else:
            store_tile(first, geo3, x, j, value)

    stage(second, even, pace, term, faces, geo3, finish_three)

    if next_width:
        rows = next_width * CY
        out_low[...] = out[pl.ds(0, rows), :]
        out_high[...] = out[pl.ds(COLS - rows, rows), :]
        return

    def sweep(src, geo, store):
        ny = geo[0]

        def row(x):
            u = [load_tile(src, geo, x, j) for j in range(-1, ny + 1)]
            for j in range(ny):
                v = u[j + 1]
                advected = load_tile(first, geo, x, j)
                sign = sign_of(advected)
                total = upwind(sign, v - u[j], v - u[j + 2])
                total += upwind(
                    sign,
                    v - load_tile(src, geo, x - 1, j),
                    v - load_tile(src, geo, x + 1, j),
                )
                total += upwind(sign, v - prev_z(v), v - next_z(v))
                smooth = advected * lax.rsqrt(advected * advected + 1.0)
                store(x, j, v - PSEUDO_STEP * smooth * (root(total) - 1.0))

        over_rows(geo, row)

    wide, block = geometry(width, 1), geometry(width, 0)
    sweep(first, wide, lambda x, j, v: store_tile(second, wide, x, j, v))

    def store_out(x, j, v):
        out[pl.ds((x - XO) * CY + j, 8, stride=block[0]), :] = v

    sweep(second, block, store_out)


def step_call(width, next_width, pieces, early, pace):
    make_pace = isinstance(pace, tuple)
    outs = [shape(COLS)]
    if next_width:
        outs += [shape(next_width * CY)] * 2
    if make_pace:
        outs += [shape(EXT)]
    return pl.pallas_call(
        functools.partial(runge_kutta, width, next_width, make_pace),
        out_shape=tuple(outs),
        scratch_shapes=[vmem(EXT)] * 7 + [vmem(XR * 56)] * 3,
        compiler_params=params(),
        cost_estimate=cost(35),
        name="step",
    )(*pieces, early, *(pace if make_pace else (pace,)))


def split(x):
    high = x.astype(jnp.bfloat16)
    low = (x - high.astype(F32)).astype(jnp.bfloat16)
    return jnp.concatenate([high, low], axis=1)


def onehot(mask):
    return jnp.where(mask, 1.0, 0.0).astype(jnp.bfloat16)


def pack_kernel(rows, owner, column, send, parts):
    count = rows.shape[0]
    own = owner[...]
    tags = onehot(lax.broadcasted_iota(jnp.int32, (DEVICES, count), 0) == own)
    order = onehot(
        lax.broadcasted_iota(jnp.int32, (count, count), 0)
        < lax.broadcasted_iota(jnp.int32, (count, count), 1)
    )
    earlier = jnp.dot(tags, order, preferred_element_type=F32)
    rank = jnp.sum(earlier * tags.astype(F32), axis=0, keepdims=True).astype(jnp.int32)
    target = own * SLOTS + rank
    parts[...] = split(rows[...])

    block = 128

    def body(b, carry):
        slot = lax.broadcasted_iota(jnp.int32, (block, count), 0) + b * block
        both = jnp.dot(onehot(slot == target), parts[...], preferred_element_type=F32)
        send[pl.ds(pl.multiple_of(b * block, block), block), :] = both[:, :NZ] + both[:, NZ:]
        return carry

    lax.fori_loop(0, DEVICES * SLOTS // block, body, 0)

    place = lax.broadcasted_iota(jnp.int32, (NZ, count), 0) == rank
    number = column[...] + 1
    dims = (((1,), (1,)), ((), ()))
    total = jnp.zeros((DEVICES, NZ), F32)
    for part, scale in ((number >> 6, 64.0), (number & 63, 1.0)):
        held = jnp.where(place, part.astype(F32), 0.0).astype(jnp.bfloat16)
        total += scale * lax.dot_general(tags, held, dims, preferred_element_type=F32)
    for b in range(DEVICES // 8):
        send[pl.ds(b * 8 * SLOTS + CAP, 8, stride=SLOTS), :] = total[8 * b : 8 * b + 8]


def unpack_kernel(low_rows, got, mask, speed, speed_low, speed_high, parts, number):
    for b in range(DEVICES // 8):
        number[pl.ds(8 * b, 8), :] = got[pl.ds(b * 8 * SLOTS + CAP, 8, stride=SLOTS), :]
    columns = number[...].T.astype(jnp.int32) - 1
    for k in range(CAP):
        for b in range(DEVICES // 16):
            pair = [
                got[pl.ds((b * 16 + 8 * i) * SLOTS + k, 8, stride=SLOTS), :] for i in range(2)
            ]
            parts[pl.ds(k * DEVICES + 16 * b, 16), :] = split(jnp.concatenate(pair, axis=0))
    named = jnp.concatenate([columns[k : k + 1, :] for k in range(CAP)], axis=1)

    block = 128

    def body(b, carry):
        cell = lax.broadcasted_iota(jnp.int32, (block, CAP * DEVICES), 0) + b * block
        both = jnp.dot(onehot(cell == named), parts[...], preferred_element_type=F32)
        at = pl.ds(pl.multiple_of(b * block, block), block)
        speed[at, :] = (both[:, :NZ] + both[:, NZ:]) * (mask[at, :] * -TIME_STEP)
        return carry

    lax.fori_loop(0, COLS // block, body, 0)
    speed_low[...] = speed[pl.ds(0, low_rows), :]
    speed_high[...] = speed[pl.ds(COLS - low_rows, low_rows), :]


def shards(level_set, band_mask, rows, row_owner, row_tile):
    count = rows.shape[0]
    send = pl.pallas_call(
        pack_kernel,
        out_shape=shape(DEVICES * SLOTS),
        scratch_shapes=[pltpu.VMEM((count, 2 * NZ), jnp.bfloat16)],
        compiler_params=params(),
        name="pack",
    )(rows, row_owner.reshape(1, count), row_tile.reshape(1, count))
    got = lax.all_to_all(send, ("gx", "gy"), split_axis=0, concat_axis=0, tiled=True)

    u = level_set.reshape(COLS, NZ)
    pieces, sides = cross_x(u, u[: 9 * CY], u[COLS - 9 * CY :], 9)
    pieces = (*pieces, *shift_pair(*sides, "gy"))
    got, pieces = lax.optimization_barrier((got, pieces))

    mask = band_mask.astype(F32).reshape(COLS, 1)
    face = SPEED_HALO * CY
    pace, pace_low, pace_high = pl.pallas_call(
        functools.partial(unpack_kernel, face),
        out_shape=(shape(COLS), shape(face), shape(face)),
        scratch_shapes=[pltpu.VMEM((CAP * DEVICES, 2 * NZ), jnp.bfloat16), vmem(DEVICES)],
        compiler_params=params(),
        cost_estimate=cost(6),
        name="unpack",
    )(got, mask)
    paces, sides = cross_x(pace, pace_low, pace_high, SPEED_HALO)
    early = early_call(9, pieces[:3], paces)
    paces = (*paces, *shift_pair(*sides, "gy"))
    u, low, high, pace = step_call(9, 9, pieces, early, paces)

    for width, next_width in ((9, 11), (11, 0)):
        pieces, sides = cross_x(u, low, high, width)
        early = early_call(width, pieces, pace)
        pieces = (*pieces, *shift_pair(*sides, "gy"))
        u, *faces = step_call(width, next_width, pieces, early, pace)
        low, high = faces or (None, None)
    return u.reshape(CX, CY, NZ)


def solution(mesh):
    return jax.shard_map(
        shards,
        mesh=mesh,
        in_specs=(
            P("gx", "gy", None),
            P("gx", "gy"),
            P(("gx", "gy"), None),
            P(("gx", "gy"), None),
            P(("gx", "gy")),
        ),
        out_specs=P("gx", "gy", None),
        check_vma=False,
    )
```

time: 277 us -> 254 us (0.917)
  waiting for transfers between devices: 63.4 us -> 46.6 us
  Pallas kernels: 165 us -> 162 us
  starting transfers between devices: 39.8 us -> 36.8 us
    all_to_all x1, waiting for transfers between devices: 18.2 us -> 0.01 us  [shards(): lax.all_to_all(send, ('gx', 'gy'), split_axis=0, concat_axis=0, tiled=True)]
    pallas_call x7 -> x10, Pallas kernels: 154 us -> 150 us  [the longest x3 120 us: step_call(): pl.pallas_call(functools.partial(runge_kutta, width, next_width, make_pac...]
    ppermute x16, starting transfers between devices: 29.2 us -> 26.2 us  [shift_pair(): return (lax.ppermute(high, axis, up), lax.ppermute(low, axis, down))]
  transfers between devices with their start and end apart: 17 -> 17, of which waited for: 13 -> 10; matrix products, arithmetic and copies ran while one was open for 0% -> 0% of each run, Pallas kernels for 3% -> 12%
where the time goes in v2:
time: 254 us; the launch traced here: 253 us
  Pallas kernels  162 us (64%)
  waiting for transfers between devices  46.6 us (18%)
  starting transfers between devices  36.8 us (14%)
  local copies, waits for them, and re-layouts  7.81 us (3%)
    pallas_call x3, Pallas kernels, step_call(): pl.pallas_call(functools.partial(runge_kutta, width, next_width, make_pac...  120 us
    ppermute x16, waiting for transfers between devices, shift_pair(): return (lax.ppermute(high, axis, up), lax.ppermute(low, axis, down))  46.6 us
    pallas_call x3, Pallas kernels, early_call(): pl.pallas_call(functools.partial(early_kernel, width, ready), out_shape=s...  28.9 us
    ppermute x16, starting transfers between devices, shift_pair(): return (lax.ppermute(high, axis, up), lax.ppermute(low, axis, down))  26.2 us
    all_to_all x1, starting transfers between devices, shards(): lax.all_to_all(send, ('gx', 'gy'), split_axis=0, concat_axis=0, tiled=True)  10.7 us
    pallas_call x1, Pallas kernels, shards(): pl.pallas_call(functools.partial(unpack_kernel, face), out_shape=(shape(C...  6.38 us
  transfers between devices with their start and end apart: 17, of which 10 were waited for; matrix products, arithmetic and copies ran while one was open for 0% of the time, Pallas kernels for 12%

profile of v2, /device:TPU:24, one launch (start us, length us, event | category | flops | bytes accessed | tf_op | source)
XLA Modules:
  0.0 253.1 jit_solution(11375900547795417842)
XLA Ops:
  0.0 1.0 copy-done.2
  1.0 0.7 copy-done.3
  1.7 0.7 copy-done.4
  2.4 4.8 %pack.1 = f32[2176,128]{1,0:T(8,128)S(1)} custom-call(f32[1024,128]{1,0:T(8,128)S(1)} %copy-done.2, s32[1,1024]{1,0:T(1,128)S(1)} %bitcast.9, s32[1,1024]{1,0:T(1,128)S(1)} %bitcast.10), custom_call_target="tpu_custom_call" | custom-call | tf_op jit(solution)/shard_map/pack/pallas_call | solution.py:568
  7.3 1.3 all_to_all.8
  8.5 10.7 %all-to-all-start = ((f32[128,17,128]{2,1,0:T(8,128)}), f32[128,17,128]{2,1,0:T(8,128)}, u32[]{:S(2)}, u32[]{:S(2)}) async-start(f32[128,17,128]{2,1,0:T(8,128)} %all_to_all.8), calls=%async_computation | async-start | bytes 3145728 | tf_op jit(solution)/shard_map/all_to_all | solution.py:575
  19.2 0.0 copy-start.5
  19.3 0.2 collective-permute-start
  19.5 4.1 %collective-permute-start.1 = (f32[360,128]{1,0:T(8,128)S(1)}, f32[360,128]{1,0:T(8,128)S(1)}, u32[]{:S(2)}, u32[]{:S(2)}) collective-permute-start(f32[360,128]{1,0:T(8,128)S(1)} %bitcast.11), channel_id=1, source_target_pairs={{8,0},{16,8},{24,16},{32,24},{40,32},{48,40},{56,48},{64,56},{72,6... | collective-permute-start | bytes 552968 | tf_op jit(solution)/shard_map/ppermute | solution.py:311
  23.6 19.7 %collective-permute-done.before.refs_1_ = f32[360,128]{1,0:T(8,128)S(1)} collective-permute-done((f32[360,128]{1,0:T(8,128)S(1)}, f32[360,128]{1,0:T(8,128)S(1)}, u32[]{:S(2)}, u32[]{:S(2)}) %collective-permute-start) | collective-permute-done | bytes 184352 | tf_op jit(solution)/shard_map/ppermute | solution.py:311
  43.3 1.2 sides.4
  44.5 2.7 %collective-permute-start.2 = (f32[792,128]{1,0:T(8,128)}, f32[792,128]{1,0:T(8,128)S(1)}, u32[]{:S(2)}, u32[]{:S(2)}) collective-permute-start(f32[792,128]{1,0:T(8,128)} %get-tuple-element.29), channel_id=1, source_target_pairs={{0,1},{1,2},{2,3},{3,4},{4,5},{5,6},{6,7},{7,0},{8,9},{9,10},{10,1... | collective-permute-start | bytes 1216520 | tf_op jit(solution)/shard_map/ppermute | solution.py:311
  47.2 0.1 copy.7
  47.3 0.4 reshape.24.mask
  47.7 0.0 all-to-all-done
  47.7 2.4 all_to_all.10.got
  50.1 3.6 %collective-permute-done.2.refs_3_ = f32[792,128]{1,0:T(8,128)S(1)} collective-permute-done((f32[792,128]{1,0:T(8,128)}, f32[792,128]{1,0:T(8,128)S(1)}, u32[]{:S(2)}, u32[]{:S(2)}) %collective-permute-start.2) | collective-permute-done | bytes 405536 | tf_op jit(solution)/shard_map/ppermute | solution.py:311
  53.7 5.8 %collective-permute-done.3.refs_4_ = f32[792,128]{1,0:T(8,128)} collective-permute-done((f32[792,128]{1,0:T(8,128)}, f32[792,128]{1,0:T(8,128)}, u32[]{:S(2)}, u32[]{:S(2)}) %collective-permute-start.3) | collective-permute-done | bytes 405536 | tf_op jit(solution)/shard_map/ppermute | solution.py:311
  59.5 1.2 copy-done.1
  60.8 6.4 %unpack.1 = (f32[2560,128]{1,0:T(8,128)S(1)}, f32[320,128]{1,0:T(8,128)S(1)}, f32[320,128]{1,0:T(8,128)S(1)}) custom-call(f32[2176,128]{1,0:T(8,128)S(1)} %copy-done.1, f32[2560,1]{1,0:T(8,128)S(1)} %reshape.24.mask), custom_call_target="tpu_custom_call" | custom-call | flops 6000 | bytes 18000000 | tf_op jit(solution)/shard_map/unpack/pallas_call | solution.py:584
  67.2 0.1 collective-permute-start.4
  67.3 3.8 %collective-permute-start.5 = (f32[320,128]{1,0:T(8,128)S(1)}, f32[320,128]{1,0:T(8,128)S(1)}, u32[]{:S(2)}, u32[]{:S(2)}) collective-permute-start(f32[320,128]{1,0:T(8,128)S(1)} %get-tuple-element.39), channel_id=1, source_target_pairs={{8,0},{16,8},{24,16},{32,24},{40,32},{48,40},{56,48},{64,56},{72,6... | collective-permute-start | bytes 491528 | tf_op jit(solution)/shard_map/ppermute | solution.py:311
  71.1 3.0 %collective-permute-done.4.refs_4_.before.refs_7_ = f32[320,128]{1,0:T(8,128)S(1)} collective-permute-done((f32[320,128]{1,0:T(8,128)S(1)}, f32[320,128]{1,0:T(8,128)S(1)}, u32[]{:S(2)}, u32[]{:S(2)}) %collective-permute-start.4) | collective-permute-done | bytes 163872 | tf_op jit(solution)/shard_map/ppermute | solution.py:311
  74.1 0.0 collective-permute-done.5.refs_5_.after.refs_8_
  74.1 0.2 sides.5
  74.4 0.3 collective-permute-start.6
  74.6 1.8 collective-permute-start.7
  76.4 9.6 %early.3.refs_5_ = f32[3520,128]{1,0:T(8,128)S(1)} custom-call(f32[2560,128]{1,0:T(8,128)S(1)} %bitcast.7, f32[360,128]{1,0:T(8,128)S(1)} %collective-permute-done.before.refs_1_, f32[360,128]{1,0:T(8,128)S(1)} %collective-permute-done.1.after.refs_2_, f32[2560,128]{1,0:T(8,128)S(1)} %get-tuple-element.37.refs_3_.own.refs_6_, ...), custom_call_target="tpu_custom_call" | custom-call | flops 10000 | bytes 30000000 | tf_op jit(solution)/shard_map/early/pallas_call | solution.py:369
  86.0 2.2 collective-permute-done.7.refs_10_
  88.2 36.9 %step.3 = (f32[2560,128]{1,0:T(8,128)S(1)}, f32[360,128]{1,0:T(8,128)S(1)}, f32[360,128]{1,0:T(8,128)S(1)}, f32[6336,128]{1,0:T(8,128)S(1)}) custom-call(f32[2560,128]{1,0:T(8,128)S(1)} %bitcast.8, f32[360,128]{1,0:T(8,128)S(1)} %collective-permute-done.before.refs_1_, f32[360,128]{1,0:T(8,128)S(1)} %collective-permute-done.1.after.refs_2_, ...), custom_call_target="tpu_custom_call" | custom-call | flops 35000 | bytes 105000000 | tf_op jit(solution)/shard_map/step/pallas_call | solution.py:486
  125.2 0.1 collective-permute-start.8
  125.3 3.8 %collective-permute-start.9 = (f32[360,128]{1,0:T(8,128)S(1)}, f32[360,128]{1,0:T(8,128)S(1)}, u32[]{:S(2)}, u32[]{:S(2)}) collective-permute-start(f32[360,128]{1,0:T(8,128)S(1)} %get-tuple-element.44), channel_id=1, source_target_pairs={{8,0},{16,8},{24,16},{32,24},{40,32},{48,40},{56,48},{64,56},{72,6... | collective-permute-start | bytes 552968 | tf_op jit(solution)/shard_map/ppermute | solution.py:311
  129.1 3.2 %collective-permute-done.8.before.refs_1_ = f32[360,128]{1,0:T(8,128)S(1)} collective-permute-done((f32[360,128]{1,0:T(8,128)S(1)}, f32[360,128]{1,0:T(8,128)S(1)}, u32[]{:S(2)}, u32[]{:S(2)}) %collective-permute-start.8) | collective-permute-done | bytes 184352 | tf_op jit(solution)/shard_map/ppermute | solution.py:311
  132.3 0.1 collective-permute-done.9.after.refs_2_
  132.5 0.3 sides.6
  132.7 1.8 collective-permute-start.10
  134.5 0.3 collective-permute-start.11
  134.8 9.5 %early.4.refs_5_ = f32[3520,128]{1,0:T(8,128)S(1)} custom-call(f32[2560,128]{1,0:T(8,128)S(1)} %get-tuple-element.42.own.refs_0_, f32[360,128]{1,0:T(8,128)S(1)} %collective-permute-done.8.before.refs_1_, f32[360,128]{1,0:T(8,128)S(1)} %collective-permute-done.9.after.refs_2_, f32[6336,128]{1,0:T(8,128)S(1)} %get-tuple-element.47.refs_3_.refs_6_), custom_call_target="tpu_custom_call" | custom-call | flops 10000 | bytes 30000000 | tf_op jit(solution)/shard_map/early/pallas_call | solution.py:369
  144.3 2.2 collective-permute-done.11.refs_4_
  146.5 35.6 %step.4 = (f32[2560,128]{1,0:T(8,128)S(1)}, f32[440,128]{1,0:T(8,128)S(1)}, f32[440,128]{1,0:T(8,128)S(1)}) custom-call(f32[2560,128]{1,0:T(8,128)S(1)} %get-tuple-element.42.own.refs_0_, f32[360,128]{1,0:T(8,128)S(1)} %collective-permute-done.8.before.refs_1_, f32[360,128]{1,0:T(8,128)S(1)} %collective-permute-done.9.after.refs_2_, ...), custom_call_target="tpu_custom_call" | custom-call | flops 35000 | bytes 105000000 | tf_op jit(solution)/shard_map/step/pallas_call | solution.py:486
  182.1 0.1 collective-permute-start.12
  182.2 3.8 %collective-permute-start.13 = (f32[440,128]{1,0:T(8,128)S(1)}, f32[440,128]{1,0:T(8,128)S(1)}, u32[]{:S(2)}, u32[]{:S(2)}) collective-permute-start(f32[440,128]{1,0:T(8,128)S(1)} %get-tuple-element.50), channel_id=1, source_target_pairs={{8,0},{16,8},{24,16},{32,24},{40,32},{48,40},{56,48},{64,56},{72,6... | collective-permute-start | bytes 675848 | tf_op jit(solution)/shard_map/ppermute | solution.py:311
  186.1 3.7 %collective-permute-done.12.before.refs_1_ = f32[440,128]{1,0:T(8,128)S(1)} collective-permute-done((f32[440,128]{1,0:T(8,128)S(1)}, f32[440,128]{1,0:T(8,128)S(1)}, u32[]{:S(2)}, u32[]{:S(2)}) %collective-permute-start.12) | collective-permute-done | bytes 225312 | tf_op jit(solution)/shard_map/ppermute | solution.py:311
  189.7 0.3 sides.7
  190.0 3.2 %collective-permute-start.14 = (f32[968,128]{1,0:T(8,128)S(1)}, f32[968,128]{1,0:T(8,128)S(1)}, u32[]{:S(2)}, u32[]{:S(2)}) collective-permute-start(f32[968,128]{1,0:T(8,128)S(1)} %get-tuple-element.51), channel_id=1, source_target_pairs={{0,1},{1,2},{2,3},{3,4},{4,5},{5,6},{6,7},{7,0},{8,9},{9,10},{10,1... | collective-permute-start | bytes 1486856 | tf_op jit(solution)/shard_map/ppermute | solution.py:311
  193.2 9.9 %early.5.refs_5_ = f32[3520,128]{1,0:T(8,128)S(1)} custom-call(f32[2560,128]{1,0:T(8,128)S(1)} %get-tuple-element.48.own.refs_0_, f32[440,128]{1,0:T(8,128)S(1)} %collective-permute-done.12.before.refs_1_, f32[440,128]{1,0:T(8,128)S(1)} %collective-permute-done.13.after.refs_2_, f32[6336,128]{1,0:T(8,128)S(1)} %get-tuple-element.47.refs_3_.refs_6_), custom_call_target="tpu_custom_call" | custom-call | flops 10000 | bytes 30000000 | tf_op jit(solution)/shard_map/early/pallas_call | solution.py:369
  203.1 3.0 %collective-permute-done.15.refs_4_ = f32[968,128]{1,0:T(8,128)S(1)} collective-permute-done((f32[968,128]{1,0:T(8,128)S(1)}, f32[968,128]{1,0:T(8,128)S(1)}, u32[]{:S(2)}, u32[]{:S(2)}) %collective-permute-start.15) | collective-permute-done | bytes 495648 | tf_op jit(solution)/shard_map/ppermute | solution.py:311
  206.1 47.0 %step.5 = f32[2560,128]{1,0:T(8,128)} custom-call(f32[2560,128]{1,0:T(8,128)S(1)} %get-tuple-element.48.own.refs_0_, f32[440,128]{1,0:T(8,128)S(1)} %collective-permute-done.12.before.refs_1_, f32[440,128]{1,0:T(8,128)S(1)} %collective-permute-done.13.after.refs_2_, f32[968,128]{1,0:T(8,128)S(1)} %collective-permute-done.14.refs_3_, ...), custom_call_target="tpu_custom_call" | custom-call | flops 35000 | bytes 105000000 | tf_op jit(solution)/shard_map/step/pallas_call | solution.py:486
  (16 shorter events, 0.1 us)
Async XLA Ops:
  0.0 1.0 copy-start.2
  1.0 0.7 copy-start.3
  1.7 0.7 copy-start.4
  8.5 10.7 %copy-start = (f32[64,40,128]{2,1,0:T(8,128)S(1)}, f32[64,40,128]{2,1,0:T(8,128)}, u32[]{:S(2)}) copy-start(f32[64,40,128]{2,1,0:T(8,128)} %param.5) | copy-start | bytes 3932164
  8.5 39.2 %all-to-all-start = ((f32[128,17,128]{2,1,0:T(8,128)}), f32[128,17,128]{2,1,0:T(8,128)}, u32[]{:S(2)}, u32[]{:S(2)}) async-start(f32[128,17,128]{2,1,0:T(8,128)} %all_to_all.8), calls=%async_computation | async-start | bytes 3145728 | tf_op jit(solution)/shard_map/all_to_all | solution.py:575
  19.2 28.0 %copy-start.5 = (s32[64,40]{0,1:T(8,128)S(1)}, s32[64,40]{0,1:T(8,128)}, u32[]{:S(2)}) copy-start(s32[64,40]{0,1:T(8,128)} %param.6) | copy-start | bytes 30724
  19.3 24.0 %collective-permute-start = (f32[360,128]{1,0:T(8,128)S(1)}, f32[360,128]{1,0:T(8,128)S(1)}, u32[]{:S(2)}, u32[]{:S(2)}) collective-permute-start(f32[360,128]{1,0:T(8,128)S(1)} %bitcast.12), channel_id=1, source_target_pairs={{0,8},{8,16},{16,24},{24,32},{32,40},{40,48},{48,56},{56,64},{64,7... | collective-permute-start | bytes 552968 | tf_op jit(solution)/shard_map/ppermute | solution.py:311
  19.5 23.8 %collective-permute-start.1 = (f32[360,128]{1,0:T(8,128)S(1)}, f32[360,128]{1,0:T(8,128)S(1)}, u32[]{:S(2)}, u32[]{:S(2)}) collective-permute-start(f32[360,128]{1,0:T(8,128)S(1)} %bitcast.11), channel_id=1, source_target_pairs={{8,0},{16,8},{24,16},{32,24},{40,32},{48,40},{56,48},{64,56},{72,6... | collective-permute-start | bytes 552968 | tf_op jit(solution)/shard_map/ppermute | solution.py:311
  44.5 9.3 %collective-permute-start.2 = (f32[792,128]{1,0:T(8,128)}, f32[792,128]{1,0:T(8,128)S(1)}, u32[]{:S(2)}, u32[]{:S(2)}) collective-permute-start(f32[792,128]{1,0:T(8,128)} %get-tuple-element.29), channel_id=1, source_target_pairs={{0,1},{1,2},{2,3},{3,4},{4,5},{5,6},{6,7},{7,0},{8,9},{9,10},{10,1... | collective-permute-start | bytes 1216520 | tf_op jit(solution)/shard_map/ppermute | solution.py:311
  47.2 12.3 %collective-permute-start.3 = (f32[792,128]{1,0:T(8,128)}, f32[792,128]{1,0:T(8,128)}, u32[]{:S(2)}, u32[]{:S(2)}) collective-permute-start(f32[792,128]{1,0:T(8,128)} %get-tuple-element.30), channel_id=1, source_target_pairs={{1,0},{2,1},{3,2},{4,3},{5,4},{6,5},{7,6},{0,7},{9,8},{10,9},{11,1... | collective-permute-start | bytes 1216520 | tf_op jit(solution)/shard_map/ppermute | solution.py:311
  59.5 1.2 copy-start.1
  67.2 6.9 %collective-permute-start.4 = (f32[320,128]{1,0:T(8,128)S(1)}, f32[320,128]{1,0:T(8,128)S(1)}, u32[]{:S(2)}, u32[]{:S(2)}) collective-permute-start(f32[320,128]{1,0:T(8,128)S(1)} %get-tuple-element.38), channel_id=1, source_target_pairs={{0,8},{8,16},{16,24},{24,32},{32,40},{40,48},{48,56},{56,64},{64,7... | collective-permute-start | bytes 491528 | tf_op jit(solution)/shard_map/ppermute | solution.py:311
  67.3 6.8 %collective-permute-start.5 = (f32[320,128]{1,0:T(8,128)S(1)}, f32[320,128]{1,0:T(8,128)S(1)}, u32[]{:S(2)}, u32[]{:S(2)}) collective-permute-start(f32[320,128]{1,0:T(8,128)S(1)} %get-tuple-element.39), channel_id=1, source_target_pairs={{8,0},{16,8},{24,16},{32,24},{40,32},{48,40},{56,48},{64,56},{72,6... | collective-permute-start | bytes 491528 | tf_op jit(solution)/shard_map/ppermute | solution.py:311
  74.4 11.7 %collective-permute-start.6 = (f32[704,128]{1,0:T(8,128)S(1)}, f32[704,128]{1,0:T(8,128)S(1)}, u32[]{:S(2)}, u32[]{:S(2)}) collective-permute-start(f32[704,128]{1,0:T(8,128)S(1)} %get-tuple-element.40), channel_id=1, source_target_pairs={{0,1},{1,2},{2,3},{3,4},{4,5},{5,6},{6,7},{7,0},{8,9},{9,10},{10,1... | collective-permute-start | bytes 1081352 | tf_op jit(solution)/shard_map/ppermute | solution.py:311
  74.6 13.6 %collective-permute-start.7 = (f32[704,128]{1,0:T(8,128)S(1)}, f32[704,128]{1,0:T(8,128)S(1)}, u32[]{:S(2)}, u32[]{:S(2)}) collective-permute-start(f32[704,128]{1,0:T(8,128)S(1)} %get-tuple-element.41), channel_id=1, source_target_pairs={{1,0},{2,1},{3,2},{4,3},{5,4},{6,5},{7,6},{0,7},{9,8},{10,9},{11,1... | collective-permute-start | bytes 1081352 | tf_op jit(solution)/shard_map/ppermute | solution.py:311
  125.2 7.1 %collective-permute-start.8 = (f32[360,128]{1,0:T(8,128)S(1)}, f32[360,128]{1,0:T(8,128)S(1)}, u32[]{:S(2)}, u32[]{:S(2)}) collective-permute-start(f32[360,128]{1,0:T(8,128)S(1)} %get-tuple-element.43), channel_id=1, source_target_pairs={{0,8},{8,16},{16,24},{24,32},{32,40},{40,48},{48,56},{56,64},{64,7... | collective-permute-start | bytes 552968 | tf_op jit(solution)/shard_map/ppermute | solution.py:311
  125.3 7.2 %collective-permute-start.9 = (f32[360,128]{1,0:T(8,128)S(1)}, f32[360,128]{1,0:T(8,128)S(1)}, u32[]{:S(2)}, u32[]{:S(2)}) collective-permute-start(f32[360,128]{1,0:T(8,128)S(1)} %get-tuple-element.44), channel_id=1, source_target_pairs={{8,0},{16,8},{24,16},{32,24},{40,32},{48,40},{56,48},{64,56},{72,6... | collective-permute-start | bytes 552968 | tf_op jit(solution)/shard_map/ppermute | solution.py:311
  132.7 11.6 %collective-permute-start.10 = (f32[792,128]{1,0:T(8,128)S(1)}, f32[792,128]{1,0:T(8,128)S(1)}, u32[]{:S(2)}, u32[]{:S(2)}) collective-permute-start(f32[792,128]{1,0:T(8,128)S(1)} %get-tuple-element.45), channel_id=1, source_target_pairs={{0,1},{1,2},{2,3},{3,4},{4,5},{5,6},{6,7},{7,0},{8,9},{9,10},{10,1... | collective-permute-start | bytes 1216520 | tf_op jit(solution)/shard_map/ppermute | solution.py:311
  134.5 12.0 %collective-permute-start.11 = (f32[792,128]{1,0:T(8,128)S(1)}, f32[792,128]{1,0:T(8,128)S(1)}, u32[]{:S(2)}, u32[]{:S(2)}) collective-permute-start(f32[792,128]{1,0:T(8,128)S(1)} %get-tuple-element.46), channel_id=1, source_target_pairs={{1,0},{2,1},{3,2},{4,3},{5,4},{6,5},{7,6},{0,7},{9,8},{10,9},{11,1... | collective-permute-start | bytes 1216520 | tf_op jit(solution)/shard_map/ppermute | solution.py:311
  182.1 7.6 %collective-permute-start.12 = (f32[440,128]{1,0:T(8,128)S(1)}, f32[440,128]{1,0:T(8,128)S(1)}, u32[]{:S(2)}, u32[]{:S(2)}) collective-permute-start(f32[440,128]{1,0:T(8,128)S(1)} %get-tuple-element.49), channel_id=1, source_target_pairs={{0,8},{8,16},{16,24},{24,32},{32,40},{40,48},{48,56},{56,64},{64,7... | collective-permute-start | bytes 675848 | tf_op jit(solution)/shard_map/ppermute | solution.py:311
  182.2 7.5 %collective-permute-start.13 = (f32[440,128]{1,0:T(8,128)S(1)}, f32[440,128]{1,0:T(8,128)S(1)}, u32[]{:S(2)}, u32[]{:S(2)}) collective-permute-start(f32[440,128]{1,0:T(8,128)S(1)} %get-tuple-element.50), channel_id=1, source_target_pairs={{8,0},{16,8},{24,16},{32,24},{40,32},{48,40},{56,48},{64,56},{72,6... | collective-permute-start | bytes 675848 | tf_op jit(solution)/shard_map/ppermute | solution.py:311
  190.0 13.1 %collective-permute-start.14 = (f32[968,128]{1,0:T(8,128)S(1)}, f32[968,128]{1,0:T(8,128)S(1)}, u32[]{:S(2)}, u32[]{:S(2)}) collective-permute-start(f32[968,128]{1,0:T(8,128)S(1)} %get-tuple-element.51), channel_id=1, source_target_pairs={{0,1},{1,2},{2,3},{3,4},{4,5},{5,6},{6,7},{7,0},{8,9},{9,10},{10,1... | collective-permute-start | bytes 1486856 | tf_op jit(solution)/shard_map/ppermute | solution.py:311
  193.2 12.9 %collective-permute-start.15 = (f32[968,128]{1,0:T(8,128)S(1)}, f32[968,128]{1,0:T(8,128)S(1)}, u32[]{:S(2)}, u32[]{:S(2)}) collective-permute-start(f32[968,128]{1,0:T(8,128)S(1)} %get-tuple-element.52), channel_id=1, source_target_pairs={{1,0},{2,1},{3,2},{4,3},{5,4},{6,5},{7,6},{0,7},{9,8},{10,9},{11,1... | collective-permute-start | bytes 1486856 | tf_op jit(solution)/shard_map/ppermute | solution.py:311

commit v3 on v2

--- a/solution.py
+++ b/solution.py
@@ -68,6 +68,16 @@
 
 def upwind(sign, left, right):
     top = jnp.maximum(jnp.maximum(sign * left, sign * right), 0.0)
+    return top * top
+
+
+def rise(left, right):
+    top = jnp.maximum(jnp.maximum(left, right), 0.0)
+    return top * top
+
+
+def fall(left, right):
+    top = jnp.minimum(jnp.minimum(left, right), 0.0)
     return top * top
 
 
@@ -224,12 +234,16 @@
             for k in range(unroll):
                 x = x_lo + i * unroll + k
                 left, right, state = advance(x, j, state)
+                at = packed(geo, x, j)
+                z_left, z_right = prev_z(faces[0][at, :]), faces[1][at, :]
+                if pace is None:
+                    rising = rise(left, right) + rise(z_left, z_right)
+                    falling = fall(left, right) + fall(z_left, z_right)
+                    emit(x, j, tile(x, j), rising, falling)
+                    continue
                 p = load_tile(pace, geo, x, j)
                 sign = speed_sign(p)
-                at = packed(geo, x, j)
-                total = upwind(sign, left, right) + upwind(
-                    sign, prev_z(faces[0][at, :]), faces[1][at, :]
-                )
+                total = upwind(sign, left, right) + upwind(sign, z_left, z_right)
                 emit(x, j, tile(x, j), p, total)
             return state
 
@@ -311,17 +325,20 @@
     return lax.ppermute(high, axis, up), lax.ppermute(low, axis, down)
 
 
-def cross_x(own, low, high, width):
-    before, after = shift_pair(low, high, "gx")
-    side_low, side_high = pl.pallas_call(
+def sides_call(pieces, width):
+    return pl.pallas_call(
         functools.partial(sides_kernel, width),
         out_shape=(shape(width * XR), shape(width * XR)),
         scratch_shapes=[vmem(EXT)],
         compiler_params=params(),
         cost_estimate=cost(1),
         name="sides",
-    )(own, before, after)
-    return (own, before, after), (side_low, side_high)
+    )(*pieces)
+
+
+def cross_x(own, low, high, width):
+    pieces = (own, *shift_pair(low, high, "gx"))
+    return pieces, sides_call(pieces, width)
 
 
 def cost(us):
@@ -335,20 +352,13 @@
     return (CY // 8, x_lo, x_hi, YO)
 
 
-def early_kernel(width, pace_ready, *refs):
+def early_kernel(width, signed, *refs):
     refs = list(refs)
     own, before, after = refs[:3]
     refs = refs[3:]
-    if pace_ready:
-        pace = refs.pop(0)
-    else:
-        p_own, p_before, p_after = refs[:3]
-        refs = refs[3:]
-    out, base = refs[:2]
-    slopes, faces = refs[2:4], refs[4:6]
-    if not pace_ready:
-        pace = refs[6]
-        fill_block(pace, p_own, p_before, p_after, SPEED_HALO)
+    pace = refs.pop(0) if signed else None
+    outs = [refs.pop(0) for _ in range(1 if signed else 2)]
+    base, slopes, faces = refs[0], refs[1:3], refs[3:5]
     fill_block(base, own, before, after, width, slopes)
     geo = own_geometry(width)
 
@@ -358,30 +368,30 @@
 
     over_rows(geo, row)
 
-    def emit(x, j, u, p, value):
-        out[packed(geo, x, j), :] = value
+    def emit(x, j, u, *values):
+        for out, value in zip(outs, values[-len(outs) :]):
+            out[packed(geo, x, j), :] = value
 
     x_pass(base, pace, faces, geo, emit)
 
 
-def early_call(width, pieces, pace):
-    ready = not isinstance(pace, tuple)
+def early_call(width, pieces, pace=None):
+    signed = pace is not None
     return pl.pallas_call(
-        functools.partial(early_kernel, width, ready),
-        out_shape=shape(XR * CY),
-        scratch_shapes=[vmem(EXT)] * 3
-        + [vmem(XR * CY)] * 2
-        + ([] if ready else [vmem(EXT)]),
+        functools.partial(early_kernel, width, signed),
+        out_shape=(shape(XR * CY),) * (1 if signed else 2),
+        scratch_shapes=[vmem(EXT)] * 3 + [vmem(XR * CY)] * 2,
         compiler_params=params(),
         cost_estimate=cost(10),
         name="early",
-    )(*pieces, *((pace,) if ready else pace))
+    )(*pieces, *((pace,) if signed else ()))
 
 
 def runge_kutta(width, next_width, make_pace, *refs):
     refs = list(refs)
-    own, before, after, left, right, early = refs[:6]
-    refs = refs[6:]
+    own, before, after, left, right = refs[:5]
+    refs = refs[5:]
+    early = [refs.pop(0) for _ in range(2 if make_pace else 1)]
     if make_pace:
         p_own, p_before, p_after, p_left, p_right = refs[:5]
         refs = refs[5:]
@@ -413,7 +423,12 @@
     done = finish_one(inner)
 
     def join(x, j, u, p, value):
-        done(x, j, u, u + p * root(value + early[packed(inner, x, j), :]))
+        at = packed(inner, x, j)
+        if make_pace:
+            value += jnp.where(p <= 0.0, early[0][at, :], early[1][at, :])
+        else:
+            value += early[0][at, :]
+        done(x, j, u, u + p * root(value))
 
     y_pass(base, pace, inner, join)
     for y_lo in (YO - 8, YO + CY):
@@ -490,7 +505,7 @@
         compiler_params=params(),
         cost_estimate=cost(35),
         name="step",
-    )(*pieces, early, *(pace if make_pace else (pace,)))
+    )(*pieces, *early, *(pace if make_pace else (pace,)))
 
 
 def split(x):
@@ -570,14 +585,20 @@
         out_shape=shape(DEVICES * SLOTS),
         scratch_shapes=[pltpu.VMEM((count, 2 * NZ), jnp.bfloat16)],
         compiler_params=params(),
+        cost_estimate=cost(5),
         name="pack",
     )(rows, row_owner.reshape(1, count), row_tile.reshape(1, count))
-    got = lax.all_to_all(send, ("gx", "gy"), split_axis=0, concat_axis=0, tiled=True)
-
     u = level_set.reshape(COLS, NZ)
-    pieces, sides = cross_x(u, u[: 9 * CY], u[COLS - 9 * CY :], 9)
+    before, after = shift_pair(u[: 9 * CY], u[COLS - 9 * CY :], "gx")
+    send, before, after = lax.optimization_barrier((send, before, after))
+    got = lax.all_to_all(
+        send.reshape(DEVICES, 1, SLOTS * NZ), ("gx", "gy"), split_axis=0, concat_axis=0, tiled=True
+    ).reshape(DEVICES * SLOTS, NZ)
+    pieces = (u, before, after)
+    sides = sides_call(pieces, 9)
+    early = early_call(9, pieces)
     pieces = (*pieces, *shift_pair(*sides, "gy"))
-    got, pieces = lax.optimization_barrier((got, pieces))
+    got, early = lax.optimization_barrier((got, early))
 
     mask = band_mask.astype(F32).reshape(COLS, 1)
     face = SPEED_HALO * CY
@@ -586,11 +607,10 @@
         out_shape=(shape(COLS), shape(face), shape(face)),
         scratch_shapes=[pltpu.VMEM((CAP * DEVICES, 2 * NZ), jnp.bfloat16), vmem(DEVICES)],
         compiler_params=params(),
-        cost_estimate=cost(6),
         name="unpack",
     )(got, mask)
+    pace_low, pace_high, pieces = lax.optimization_barrier((pace_low, pace_high, pieces))
     paces, sides = cross_x(pace, pace_low, pace_high, SPEED_HALO)
-    early = early_call(9, pieces[:3], paces)
     paces = (*paces, *shift_pair(*sides, "gy"))
     u, low, high, pace = step_call(9, 9, pieces, early, paces)
 

time: 254 us -> 237 us (0.933)
  waiting for transfers between devices: 46.6 us -> 29.6 us
    ppermute x16, waiting for transfers between devices: 46.6 us -> 28.7 us  [shift_pair(): return (lax.ppermute(high, axis, up), lax.ppermute(low, axis, down))]
    all_to_all x2 -> x0, local copies, waits for them, and re-layouts: 3.63 us -> none  [shards(): lax.all_to_all(send, ('gx', 'gy'), split_axis=0, concat_axis=0, tiled=True)]
    all_to_all x1, starting transfers between devices: 10.7 us -> 7.93 us  [shards(): lax.all_to_all(send.reshape(DEVICES, 1, SLOTS * NZ), ('gx', 'gy'), split_...]
  transfers between devices with their start and end apart: 17 -> 17, of which waited for: 10 -> 10; matrix products, arithmetic and copies ran while one was open for 0% -> 0% of each run, Pallas kernels for 12% -> 18%
where the time goes in v3:
time: 237 us; the launch traced here: 236 us
  Pallas kernels  164 us (69%)
  starting transfers between devices  36.1 us (15%)
  waiting for transfers between devices  29.6 us (12%)
  local copies, waits for them, and re-layouts  6.41 us (3%)
    pallas_call x3, Pallas kernels, step_call(): pl.pallas_call(functools.partial(runge_kutta, width, next_width, make_pac...  120 us
    pallas_call x3, Pallas kernels, early_call(): pl.pallas_call(functools.partial(early_kernel, width, signed), out_shape=...  28.8 us
    ppermute x16, waiting for transfers between devices, shift_pair(): return (lax.ppermute(high, axis, up), lax.ppermute(low, axis, down))  28.7 us
    ppermute x16, starting transfers between devices, shift_pair(): return (lax.ppermute(high, axis, up), lax.ppermute(low, axis, down))  28.2 us
    all_to_all x1, starting transfers between devices, shards(): lax.all_to_all(send.reshape(DEVICES, 1, SLOTS * NZ), ('gx', 'gy'), split_...  7.93 us
    pallas_call x1, Pallas kernels, shards(): pl.pallas_call(functools.partial(unpack_kernel, face), out_shape=(shape(C...  7.78 us
    pallas_call x1, Pallas kernels, shards(): pl.pallas_call(pack_kernel, out_shape=shape(DEVICES * SLOTS), scratch_sha...  5.84 us
    unnamed x18, local copies, waits for them, and re-layouts  4.88 us
  transfers between devices with their start and end apart: 17, of which 10 were waited for; matrix products, arithmetic and copies ran while one was open for 0% of the time, Pallas kernels for 18%

profile of v3, /device:TPU:24, one launch (start us, length us, event | category | flops | bytes accessed | tf_op | source)
XLA Modules:
  0.0 236.4 jit_solution(5114258198298281944)
XLA Ops:
  0.0 1.0 fusion
  1.0 0.1 collective-permute-start
  1.1 4.5 %collective-permute-start.1 = (f32[360,128]{1,0:T(8,128)S(1)}, f32[360,128]{1,0:T(8,128)S(1)}, u32[]{:S(2)}, u32[]{:S(2)}) collective-permute-start(f32[360,128]{1,0:T(8,128)S(1)} %bitcast.13), channel_id=1, source_target_pairs={{8,0},{16,8},{24,16},{32,24},{40,32},{48,40},{56,48},{64,56},{72,6... | collective-permute-start | bytes 552968 | tf_op jit(solution)/shard_map/ppermute | solution.py:325
  5.6 1.0 copy-done.5
  6.6 0.7 copy-done.6
  7.3 0.7 copy-done.7
  8.0 5.8 %pack.1 = f32[2176,128]{1,0:T(8,128)} custom-call(f32[1024,128]{1,0:T(8,128)S(1)} %copy-done.5, s32[1,1024]{1,0:T(1,128)S(1)} %bitcast.11, s32[1,1024]{1,0:T(1,128)S(1)} %bitcast.12), custom_call_target="tpu_custom_call" | custom-call | flops 5000 | bytes 15000000 | tf_op jit(solution)/shard_map/pack/pallas_call | solution.py:583
  13.9 0.0 collective-permute-done.refs_1_.before
  13.9 0.0 collective-permute-done.1.refs_2_.after
  13.9 7.9 %all-to-all-start = ((f32[128,1,2176]{2,1,0:T(1,128)}), f32[128,1,2176]{2,1,0:T(1,128)}, u32[]{:S(2)}, u32[]{:S(2)}) async-start(f32[128,1,2176]{2,1,0:T(1,128)} %bitcast.4), calls=%async_computation | async-start | bytes 2228224 | tf_op jit(solution)/shard_map/all_to_all | solution.py:594
  21.8 0.0 copy-start.8
  21.8 1.2 sides.4
  23.0 2.9 %collective-permute-start.2 = (f32[792,128]{1,0:T(8,128)}, f32[792,128]{1,0:T(8,128)S(1)}, u32[]{:S(2)}, u32[]{:S(2)}) collective-permute-start(f32[792,128]{1,0:T(8,128)} %get-tuple-element.46), channel_id=1, source_target_pairs={{0,1},{1,2},{2,3},{3,4},{4,5},{5,6},{6,7},{7,0},{8,9},{9,10},{10,1... | collective-permute-start | bytes 1216520 | tf_op jit(solution)/shard_map/ppermute | solution.py:325
  25.9 0.1 copy.10
  26.0 0.4 reshape.30.mask
  26.4 9.5 %early.3 = (f32[3520,128]{1,0:T(8,128)S(1)}, f32[3520,128]{1,0:T(8,128)S(1)}) custom-call(f32[2560,128]{1,0:T(8,128)S(1)} %bitcast.9, f32[360,128]{1,0:T(8,128)S(1)} %collective-permute-done.refs_1_.before, f32[360,128]{1,0:T(8,128)S(1)} %collective-permute-done.1.refs_2_.after), custom_call_target="tpu_custom_call" | custom-call | flops 10000 | bytes 30000000 | tf_op jit(solution)/shard_map/early/pallas_call | solution.py:380
  35.9 1.2 copy-done.1
  37.2 1.2 copy-done.3
  38.4 1.0 all-to-all-done
  39.4 7.8 %unpack.1 = (f32[2560,128]{1,0:T(8,128)S(1)}, f32[320,128]{1,0:T(8,128)S(1)}, f32[320,128]{1,0:T(8,128)S(1)}) custom-call(f32[2176,128]{1,0:T(8,128)} %bitcast.5.got, f32[2560,1]{1,0:T(8,128)S(1)} %reshape.30.mask), custom_call_target="tpu_custom_call" | custom-call | tf_op jit(solution)/shard_map/unpack/pallas_call | solution.py:605
  47.2 0.1 collective-permute-start.4
  47.2 3.8 %collective-permute-start.5 = (f32[320,128]{1,0:T(8,128)S(1)}, f32[320,128]{1,0:T(8,128)S(1)}, u32[]{:S(2)}, u32[]{:S(2)}) collective-permute-start(f32[320,128]{1,0:T(8,128)S(1)} %get-tuple-element.57), channel_id=1, source_target_pairs={{8,0},{16,8},{24,16},{32,24},{40,32},{48,40},{56,48},{64,56},{72,6... | collective-permute-start | bytes 491528 | tf_op jit(solution)/shard_map/ppermute | solution.py:325
  51.1 3.0 %collective-permute-done.4.before.refs_8_ = f32[320,128]{1,0:T(8,128)S(1)} collective-permute-done((f32[320,128]{1,0:T(8,128)S(1)}, f32[320,128]{1,0:T(8,128)S(1)}, u32[]{:S(2)}, u32[]{:S(2)}) %collective-permute-start.4) | collective-permute-done | bytes 163872 | tf_op jit(solution)/shard_map/ppermute | solution.py:325
  54.1 0.2 sides.5
  54.3 4.7 %collective-permute-start.6 = (f32[704,128]{1,0:T(8,128)S(1)}, f32[704,128]{1,0:T(8,128)S(1)}, u32[]{:S(2)}, u32[]{:S(2)}) collective-permute-start(f32[704,128]{1,0:T(8,128)S(1)} %get-tuple-element.58), channel_id=1, source_target_pairs={{0,1},{1,2},{2,3},{3,4},{4,5},{5,6},{6,7},{7,0},{8,9},{9,10},{10,1... | collective-permute-start | bytes 1081352 | tf_op jit(solution)/shard_map/ppermute | solution.py:325
  59.1 7.7 %collective-permute-done.6.refs_10_ = f32[704,128]{1,0:T(8,128)S(1)} collective-permute-done((f32[704,128]{1,0:T(8,128)S(1)}, f32[704,128]{1,0:T(8,128)S(1)}, u32[]{:S(2)}, u32[]{:S(2)}) %collective-permute-start.6) | collective-permute-done | bytes 360480 | tf_op jit(solution)/shard_map/ppermute | solution.py:325
  66.8 5.8 %collective-permute-done.7.refs_11_ = f32[704,128]{1,0:T(8,128)S(1)} collective-permute-done((f32[704,128]{1,0:T(8,128)S(1)}, f32[704,128]{1,0:T(8,128)S(1)}, u32[]{:S(2)}, u32[]{:S(2)}) %collective-permute-start.7) | collective-permute-done | bytes 360480 | tf_op jit(solution)/shard_map/ppermute | solution.py:325
  72.6 37.1 %step.3 = (f32[2560,128]{1,0:T(8,128)S(1)}, f32[360,128]{1,0:T(8,128)S(1)}, f32[360,128]{1,0:T(8,128)S(1)}, f32[6336,128]{1,0:T(8,128)S(1)}) custom-call(f32[2560,128]{1,0:T(8,128)S(1)} %bitcast.10, f32[360,128]{1,0:T(8,128)S(1)} %collective-permute-done.refs_1_.before, f32[360,128]{1,0:T(8,128)S(1)} %collective-permute-done.1.refs_2_.after, ...), custom_call_target="tpu_custom_call" | custom-call | flops 35000 | bytes 105000000 | tf_op jit(solution)/shard_map/step/pallas_call | solution.py:501
  109.7 0.1 collective-permute-start.8
  109.8 3.8 %collective-permute-start.9 = (f32[360,128]{1,0:T(8,128)S(1)}, f32[360,128]{1,0:T(8,128)S(1)}, u32[]{:S(2)}, u32[]{:S(2)}) collective-permute-start(f32[360,128]{1,0:T(8,128)S(1)} %get-tuple-element.62), channel_id=1, source_target_pairs={{8,0},{16,8},{24,16},{32,24},{40,32},{48,40},{56,48},{64,56},{72,6... | collective-permute-start | bytes 552968 | tf_op jit(solution)/shard_map/ppermute | solution.py:325
  113.6 3.2 %collective-permute-done.8.before.refs_1_ = f32[360,128]{1,0:T(8,128)S(1)} collective-permute-done((f32[360,128]{1,0:T(8,128)S(1)}, f32[360,128]{1,0:T(8,128)S(1)}, u32[]{:S(2)}, u32[]{:S(2)}) %collective-permute-start.8) | collective-permute-done | bytes 184352 | tf_op jit(solution)/shard_map/ppermute | solution.py:325
  116.9 0.3 collective-permute-done.9.after.refs_2_
  117.1 0.3 sides.6
  117.4 0.1 collective-permute-start.10
  117.5 2.0 collective-permute-start.11
  119.5 9.5 %early.4.refs_5_ = f32[3520,128]{1,0:T(8,128)S(1)} custom-call(f32[2560,128]{1,0:T(8,128)S(1)} %get-tuple-element.60.own.refs_0_, f32[360,128]{1,0:T(8,128)S(1)} %collective-permute-done.8.before.refs_1_, f32[360,128]{1,0:T(8,128)S(1)} %collective-permute-done.9.after.refs_2_, f32[6336,128]{1,0:T(8,128)S(1)} %get-tuple-element.65.refs_3_.refs_6_), custom_call_target="tpu_custom_call" | custom-call | flops 10000 | bytes 30000000 | tf_op jit(solution)/shard_map/early/pallas_call | solution.py:380
  129.0 2.0 collective-permute-done.11.refs_4_
  131.0 35.6 %step.4 = (f32[2560,128]{1,0:T(8,128)S(1)}, f32[440,128]{1,0:T(8,128)S(1)}, f32[440,128]{1,0:T(8,128)S(1)}) custom-call(f32[2560,128]{1,0:T(8,128)S(1)} %get-tuple-element.60.own.refs_0_, f32[360,128]{1,0:T(8,128)S(1)} %collective-permute-done.8.before.refs_1_, f32[360,128]{1,0:T(8,128)S(1)} %collective-permute-done.9.after.refs_2_, ...), custom_call_target="tpu_custom_call" | custom-call | flops 35000 | bytes 105000000 | tf_op jit(solution)/shard_map/step/pallas_call | solution.py:501
  166.6 0.1 collective-permute-start.12
  166.7 3.8 %collective-permute-start.13 = (f32[440,128]{1,0:T(8,128)S(1)}, f32[440,128]{1,0:T(8,128)S(1)}, u32[]{:S(2)}, u32[]{:S(2)}) collective-permute-start(f32[440,128]{1,0:T(8,128)S(1)} %get-tuple-element.68), channel_id=1, source_target_pairs={{8,0},{16,8},{24,16},{32,24},{40,32},{48,40},{56,48},{64,56},{72,6... | collective-permute-start | bytes 675848 | tf_op jit(solution)/shard_map/ppermute | solution.py:325
  170.5 3.7 %collective-permute-done.12.before.refs_1_ = f32[440,128]{1,0:T(8,128)S(1)} collective-permute-done((f32[440,128]{1,0:T(8,128)S(1)}, f32[440,128]{1,0:T(8,128)S(1)}, u32[]{:S(2)}, u32[]{:S(2)}) %collective-permute-start.12) | collective-permute-done | bytes 225312 | tf_op jit(solution)/shard_map/ppermute | solution.py:325
  174.2 1.2 collective-permute-done.13.after.refs_2_
  175.4 0.3 sides.7
  175.7 1.3 collective-permute-start.14
  176.9 0.8 collective-permute-start.15
  177.8 9.9 %early.5.refs_5_ = f32[3520,128]{1,0:T(8,128)S(1)} custom-call(f32[2560,128]{1,0:T(8,128)S(1)} %get-tuple-element.66.own.refs_0_, f32[440,128]{1,0:T(8,128)S(1)} %collective-permute-done.12.before.refs_1_, f32[440,128]{1,0:T(8,128)S(1)} %collective-permute-done.13.after.refs_2_, f32[6336,128]{1,0:T(8,128)S(1)} %get-tuple-element.65.refs_3_.refs_6_), custom_call_target="tpu_custom_call" | custom-call | flops 10000 | bytes 30000000 | tf_op jit(solution)/shard_map/early/pallas_call | solution.py:380
  187.6 1.8 collective-permute-done.15.refs_4_
  189.4 47.0 %step.5 = f32[2560,128]{1,0:T(8,128)} custom-call(f32[2560,128]{1,0:T(8,128)S(1)} %get-tuple-element.66.own.refs_0_, f32[440,128]{1,0:T(8,128)S(1)} %collective-permute-done.12.before.refs_1_, f32[440,128]{1,0:T(8,128)S(1)} %collective-permute-done.13.after.refs_2_, f32[968,128]{1,0:T(8,128)S(1)} %collective-permute-done.14.refs_3_, ...), custom_call_target="tpu_custom_call" | custom-call | flops 35000 | bytes 105000000 | tf_op jit(solution)/shard_map/step/pallas_call | solution.py:501
  (20 shorter events, 0.0 us)
Async XLA Ops:
  1.0 12.8 %collective-permute-start = (f32[360,128]{1,0:T(8,128)S(1)}, f32[360,128]{1,0:T(8,128)S(1)}, u32[]{:S(2)}, u32[]{:S(2)}) collective-permute-start(f32[360,128]{1,0:T(8,128)S(1)} %bitcast.14), channel_id=1, source_target_pairs={{0,8},{8,16},{16,24},{24,32},{32,40},{40,48},{48,56},{56,64},{64,7... | collective-permute-start | bytes 552968 | tf_op jit(solution)/shard_map/ppermute | solution.py:325
  1.1 12.7 %collective-permute-start.1 = (f32[360,128]{1,0:T(8,128)S(1)}, f32[360,128]{1,0:T(8,128)S(1)}, u32[]{:S(2)}, u32[]{:S(2)}) collective-permute-start(f32[360,128]{1,0:T(8,128)S(1)} %bitcast.13), channel_id=1, source_target_pairs={{8,0},{16,8},{24,16},{32,24},{40,32},{48,40},{56,48},{64,56},{72,6... | collective-permute-start | bytes 552968 | tf_op jit(solution)/shard_map/ppermute | solution.py:325
  5.6 1.0 copy-start.5
  6.6 0.7 copy-start.6
  7.3 0.7 copy-start.7
  13.9 8.0 %copy-start = (f32[64,40,128]{2,1,0:T(8,128)S(1)}, f32[64,40,128]{2,1,0:T(8,128)}, u32[]{:S(2)}) copy-start(f32[64,40,128]{2,1,0:T(8,128)} %param.5) | copy-start | bytes 3932164
  13.9 25.5 %all-to-all-start = ((f32[128,1,2176]{2,1,0:T(1,128)}), f32[128,1,2176]{2,1,0:T(1,128)}, u32[]{:S(2)}, u32[]{:S(2)}) async-start(f32[128,1,2176]{2,1,0:T(1,128)} %bitcast.4), calls=%async_computation | async-start | bytes 2228224 | tf_op jit(solution)/shard_map/all_to_all | solution.py:594
  21.8 4.1 %copy-start.8 = (s32[64,40]{0,1:T(8,128)S(1)}, s32[64,40]{0,1:T(8,128)}, u32[]{:S(2)}) copy-start(s32[64,40]{0,1:T(8,128)} %param.6) | copy-start | bytes 30724
  23.0 24.1 %collective-permute-start.2 = (f32[792,128]{1,0:T(8,128)}, f32[792,128]{1,0:T(8,128)S(1)}, u32[]{:S(2)}, u32[]{:S(2)}) collective-permute-start(f32[792,128]{1,0:T(8,128)} %get-tuple-element.46), channel_id=1, source_target_pairs={{0,1},{1,2},{2,3},{3,4},{4,5},{5,6},{6,7},{7,0},{8,9},{9,10},{10,1... | collective-permute-start | bytes 1216520 | tf_op jit(solution)/shard_map/ppermute | solution.py:325
  25.9 21.2 %collective-permute-start.3 = (f32[792,128]{1,0:T(8,128)}, f32[792,128]{1,0:T(8,128)}, u32[]{:S(2)}, u32[]{:S(2)}) collective-permute-start(f32[792,128]{1,0:T(8,128)} %get-tuple-element.47), channel_id=1, source_target_pairs={{1,0},{2,1},{3,2},{4,3},{5,4},{6,5},{7,6},{0,7},{9,8},{10,9},{11,1... | collective-permute-start | bytes 1216520 | tf_op jit(solution)/shard_map/ppermute | solution.py:325
  35.9 1.3 copy-start.1
  37.2 1.2 copy-start.3
  39.4 33.3 %copy-start.2 = (f32[3520,128]{1,0:T(8,128)S(1)}, f32[3520,128]{1,0:T(8,128)}, u32[]{:S(2)}) copy-start(f32[3520,128]{1,0:T(8,128)} %copy-done.1) | copy-start | bytes 5406724
  39.4 33.3 %copy-start.4 = (f32[3520,128]{1,0:T(8,128)S(1)}, f32[3520,128]{1,0:T(8,128)}, u32[]{:S(2)}) copy-start(f32[3520,128]{1,0:T(8,128)} %copy-done.3) | copy-start | bytes 5406724
  47.2 6.9 %collective-permute-start.4 = (f32[320,128]{1,0:T(8,128)S(1)}, f32[320,128]{1,0:T(8,128)S(1)}, u32[]{:S(2)}, u32[]{:S(2)}) collective-permute-start(f32[320,128]{1,0:T(8,128)S(1)} %get-tuple-element.56), channel_id=1, source_target_pairs={{0,8},{8,16},{16,24},{24,32},{32,40},{40,48},{48,56},{56,64},{64,7... | collective-permute-start | bytes 491528 | tf_op jit(solution)/shard_map/ppermute | solution.py:325
  47.2 6.8 %collective-permute-start.5 = (f32[320,128]{1,0:T(8,128)S(1)}, f32[320,128]{1,0:T(8,128)S(1)}, u32[]{:S(2)}, u32[]{:S(2)}) collective-permute-start(f32[320,128]{1,0:T(8,128)S(1)} %get-tuple-element.57), channel_id=1, source_target_pairs={{8,0},{16,8},{24,16},{32,24},{40,32},{48,40},{56,48},{64,56},{72,6... | collective-permute-start | bytes 491528 | tf_op jit(solution)/shard_map/ppermute | solution.py:325
  54.3 12.5 %collective-permute-start.6 = (f32[704,128]{1,0:T(8,128)S(1)}, f32[704,128]{1,0:T(8,128)S(1)}, u32[]{:S(2)}, u32[]{:S(2)}) collective-permute-start(f32[704,128]{1,0:T(8,128)S(1)} %get-tuple-element.58), channel_id=1, source_target_pairs={{0,1},{1,2},{2,3},{3,4},{4,5},{5,6},{6,7},{7,0},{8,9},{9,10},{10,1... | collective-permute-start | bytes 1081352 | tf_op jit(solution)/shard_map/ppermute | solution.py:325
  59.1 13.6 %collective-permute-start.7 = (f32[704,128]{1,0:T(8,128)S(1)}, f32[704,128]{1,0:T(8,128)S(1)}, u32[]{:S(2)}, u32[]{:S(2)}) collective-permute-start(f32[704,128]{1,0:T(8,128)S(1)} %get-tuple-element.59), channel_id=1, source_target_pairs={{1,0},{2,1},{3,2},{4,3},{5,4},{6,5},{7,6},{0,7},{9,8},{10,9},{11,1... | collective-permute-start | bytes 1081352 | tf_op jit(solution)/shard_map/ppermute | solution.py:325
  109.7 7.1 %collective-permute-start.8 = (f32[360,128]{1,0:T(8,128)S(1)}, f32[360,128]{1,0:T(8,128)S(1)}, u32[]{:S(2)}, u32[]{:S(2)}) collective-permute-start(f32[360,128]{1,0:T(8,128)S(1)} %get-tuple-element.61), channel_id=1, source_target_pairs={{0,8},{8,16},{16,24},{24,32},{32,40},{40,48},{48,56},{56,64},{64,7... | collective-permute-start | bytes 552968 | tf_op jit(solution)/shard_map/ppermute | solution.py:325
  109.8 7.3 %collective-permute-start.9 = (f32[360,128]{1,0:T(8,128)S(1)}, f32[360,128]{1,0:T(8,128)S(1)}, u32[]{:S(2)}, u32[]{:S(2)}) collective-permute-start(f32[360,128]{1,0:T(8,128)S(1)} %get-tuple-element.62), channel_id=1, source_target_pairs={{8,0},{16,8},{24,16},{32,24},{40,32},{48,40},{56,48},{64,56},{72,6... | collective-permute-start | bytes 552968 | tf_op jit(solution)/shard_map/ppermute | solution.py:325
  117.4 11.6 %collective-permute-start.10 = (f32[792,128]{1,0:T(8,128)S(1)}, f32[792,128]{1,0:T(8,128)S(1)}, u32[]{:S(2)}, u32[]{:S(2)}) collective-permute-start(f32[792,128]{1,0:T(8,128)S(1)} %get-tuple-element.63), channel_id=1, source_target_pairs={{0,1},{1,2},{2,3},{3,4},{4,5},{5,6},{6,7},{7,0},{8,9},{9,10},{10,1... | collective-permute-start | bytes 1216520 | tf_op jit(solution)/shard_map/ppermute | solution.py:325
  117.5 13.5 %collective-permute-start.11 = (f32[792,128]{1,0:T(8,128)S(1)}, f32[792,128]{1,0:T(8,128)S(1)}, u32[]{:S(2)}, u32[]{:S(2)}) collective-permute-start(f32[792,128]{1,0:T(8,128)S(1)} %get-tuple-element.64), channel_id=1, source_target_pairs={{1,0},{2,1},{3,2},{4,3},{5,4},{6,5},{7,6},{0,7},{9,8},{10,9},{11,1... | collective-permute-start | bytes 1216520 | tf_op jit(solution)/shard_map/ppermute | solution.py:325
  166.6 7.6 %collective-permute-start.12 = (f32[440,128]{1,0:T(8,128)S(1)}, f32[440,128]{1,0:T(8,128)S(1)}, u32[]{:S(2)}, u32[]{:S(2)}) collective-permute-start(f32[440,128]{1,0:T(8,128)S(1)} %get-tuple-element.67), channel_id=1, source_target_pairs={{0,8},{8,16},{16,24},{24,32},{32,40},{40,48},{48,56},{56,64},{64,7... | collective-permute-start | bytes 675848 | tf_op jit(solution)/shard_map/ppermute | solution.py:325
  166.7 8.7 %collective-permute-start.13 = (f32[440,128]{1,0:T(8,128)S(1)}, f32[440,128]{1,0:T(8,128)S(1)}, u32[]{:S(2)}, u32[]{:S(2)}) collective-permute-start(f32[440,128]{1,0:T(8,128)S(1)} %get-tuple-element.68), channel_id=1, source_target_pairs={{8,0},{16,8},{24,16},{32,24},{40,32},{48,40},{56,48},{64,56},{72,6... | collective-permute-start | bytes 675848 | tf_op jit(solution)/shard_map/ppermute | solution.py:325
  175.7 12.0 %collective-permute-start.14 = (f32[968,128]{1,0:T(8,128)S(1)}, f32[968,128]{1,0:T(8,128)S(1)}, u32[]{:S(2)}, u32[]{:S(2)}) collective-permute-start(f32[968,128]{1,0:T(8,128)S(1)} %get-tuple-element.69), channel_id=1, source_target_pairs={{0,1},{1,2},{2,3},{3,4},{4,5},{5,6},{6,7},{7,0},{8,9},{9,10},{10,1... | collective-permute-start | bytes 1486856 | tf_op jit(solution)/shard_map/ppermute | solution.py:325
  176.9 12.5 %collective-permute-start.15 = (f32[968,128]{1,0:T(8,128)S(1)}, f32[968,128]{1,0:T(8,128)S(1)}, u32[]{:S(2)}, u32[]{:S(2)}) collective-permute-start(f32[968,128]{1,0:T(8,128)S(1)} %get-tuple-element.70), channel_id=1, source_target_pairs={{1,0},{2,1},{3,2},{4,3},{5,4},{6,5},{7,6},{0,7},{9,8},{10,9},{11,1... | collective-permute-start | bytes 1486856 | tf_op jit(solution)/shard_map/ppermute | solution.py:325

commit v4 on v3

--- a/solution.py
+++ b/solution.py
@@ -145,6 +145,9 @@
 
 
 GROUP = 4
+ROW_GROUP = 4
+SIDE_TURNS = 2
+TURNS = 2
 
 
 def geometry(width, margin):
@@ -171,12 +174,14 @@
 
 
 def over_rows(geo, row):
+    group = (geo[2] - geo[1]) // SIDE_TURNS if geo[0] == 1 else ROW_GROUP
+
     def body(i, carry):
-        for k in range(GROUP):
-            row(geo[1] + i * GROUP + k)
+        for k in range(group):
+            row(geo[1] + i * group + k)
         return carry
 
-    lax.fori_loop(0, (geo[2] - geo[1]) // GROUP, body, 0)
+    lax.fori_loop(0, (geo[2] - geo[1]) // group, body, 0)
 
 
 def z_row(slopes, faces, geo, x, j):
@@ -199,7 +204,7 @@
 
 def x_pass(src, pace, faces, geo, emit):
     ny, x_lo, x_hi, _ = geo
-    unroll = (x_hi - x_lo) // 4
+    unroll = (x_hi - x_lo) // TURNS
 
     def tile(x, j):
         return load_tile(src, geo, x, j)
@@ -247,7 +252,7 @@
                 emit(x, j, tile(x, j), p, total)
             return state
 
-        lax.fori_loop(0, 4, body, state)
+        lax.fori_loop(0, TURNS, body, state)
         return carry
 
     lax.fori_loop(0, ny, column, 0)

time: 237 us -> 230 us (0.970)
  Pallas kernels: 164 us -> 156 us
    pallas_call x3, Pallas kernels: 120 us -> 113 us  [step_call(): pl.pallas_call(functools.partial(runge_kutta, width, next_width, make_pac...]
  transfers between devices with their start and end apart: 17 -> 17, of which waited for: 10 -> 10; matrix products, arithmetic and copies ran while one was open for 0% -> 0% of each run, Pallas kernels for 18% -> 19%
where the time goes in v4:
time: 230 us; the launch traced here: 229 us
  Pallas kernels  156 us (68%)
  starting transfers between devices  36.1 us (16%)
  waiting for transfers between devices  30.1 us (13%)
  local copies, waits for them, and re-layouts  6.41 us (3%)
    pallas_call x3, Pallas kernels, step_call(): pl.pallas_call(functools.partial(runge_kutta, width, next_width, make_pac...  113 us
    ppermute x16, waiting for transfers between devices, shift_pair(): return (lax.ppermute(high, axis, up), lax.ppermute(low, axis, down))  28.9 us
    pallas_call x3, Pallas kernels, early_call(): pl.pallas_call(functools.partial(early_kernel, width, signed), out_shape=...  28.2 us
    ppermute x16, starting transfers between devices, shift_pair(): return (lax.ppermute(high, axis, up), lax.ppermute(low, axis, down))  28.1 us
    all_to_all x1, starting transfers between devices, shards(): lax.all_to_all(send.reshape(DEVICES, 1, SLOTS * NZ), ('gx', 'gy'), split_...  7.93 us
    pallas_call x1, Pallas kernels, shards(): pl.pallas_call(functools.partial(unpack_kernel, face), out_shape=(shape(C...  7.78 us
    pallas_call x1, Pallas kernels, shards(): pl.pallas_call(pack_kernel, out_shape=shape(DEVICES * SLOTS), scratch_sha...  5.84 us
    unnamed x18, local copies, waits for them, and re-layouts  4.88 us
  transfers between devices with their start and end apart: 17, of which 10 were waited for; matrix products, arithmetic and copies ran while one was open for 0% of the time, Pallas kernels for 19%

profile of v4, /device:TPU:24, one launch (start us, length us, event | category | flops | bytes accessed | tf_op | source)
XLA Modules:
  0.0 229.1 jit_solution(2458190663201579856)
XLA Ops:
  0.0 1.0 fusion
  1.0 0.1 collective-permute-start
  1.1 4.5 %collective-permute-start.1 = (f32[360,128]{1,0:T(8,128)S(1)}, f32[360,128]{1,0:T(8,128)S(1)}, u32[]{:S(2)}, u32[]{:S(2)}) collective-permute-start(f32[360,128]{1,0:T(8,128)S(1)} %bitcast.13), channel_id=1, source_target_pairs={{8,0},{16,8},{24,16},{32,24},{40,32},{48,40},{56,48},{64,56},{72,6... | collective-permute-start | bytes 552968 | tf_op jit(solution)/shard_map/ppermute | solution.py:330
  5.6 1.0 copy-done.5
  6.6 0.7 copy-done.6
  7.3 0.7 copy-done.7
  8.0 5.8 %pack.1 = f32[2176,128]{1,0:T(8,128)} custom-call(f32[1024,128]{1,0:T(8,128)S(1)} %copy-done.5, s32[1,1024]{1,0:T(1,128)S(1)} %bitcast.11, s32[1,1024]{1,0:T(1,128)S(1)} %bitcast.12), custom_call_target="tpu_custom_call" | custom-call | flops 5000 | bytes 15000000 | tf_op jit(solution)/shard_map/pack/pallas_call | solution.py:588
  13.9 7.9 %all-to-all-start = ((f32[128,1,2176]{2,1,0:T(1,128)}), f32[128,1,2176]{2,1,0:T(1,128)}, u32[]{:S(2)}, u32[]{:S(2)}) async-start(f32[128,1,2176]{2,1,0:T(1,128)} %bitcast.4), calls=%async_computation | async-start | bytes 2228224 | tf_op jit(solution)/shard_map/all_to_all | solution.py:599
  21.8 0.0 copy-start.8
  21.8 1.2 sides.4
  23.0 2.9 %collective-permute-start.2 = (f32[792,128]{1,0:T(8,128)}, f32[792,128]{1,0:T(8,128)S(1)}, u32[]{:S(2)}, u32[]{:S(2)}) collective-permute-start(f32[792,128]{1,0:T(8,128)} %get-tuple-element.46), channel_id=1, source_target_pairs={{0,1},{1,2},{2,3},{3,4},{4,5},{5,6},{6,7},{7,0},{8,9},{9,10},{10,1... | collective-permute-start | bytes 1216520 | tf_op jit(solution)/shard_map/ppermute | solution.py:330
  25.9 0.1 copy.10
  26.0 0.4 reshape.30.mask
  26.4 9.3 %early.3 = (f32[3520,128]{1,0:T(8,128)S(1)}, f32[3520,128]{1,0:T(8,128)S(1)}) custom-call(f32[2560,128]{1,0:T(8,128)S(1)} %bitcast.9, f32[360,128]{1,0:T(8,128)S(1)} %collective-permute-done.refs_1_.before, f32[360,128]{1,0:T(8,128)S(1)} %collective-permute-done.1.refs_2_.after), custom_call_target="tpu_custom_call" | custom-call | flops 10000 | bytes 30000000 | tf_op jit(solution)/shard_map/early/pallas_call | solution.py:385
  35.7 1.2 copy-done.1
  37.0 1.2 copy-done.3
  38.2 1.2 all-to-all-done
  39.4 7.8 %unpack.1 = (f32[2560,128]{1,0:T(8,128)S(1)}, f32[320,128]{1,0:T(8,128)S(1)}, f32[320,128]{1,0:T(8,128)S(1)}) custom-call(f32[2176,128]{1,0:T(8,128)} %bitcast.5.got, f32[2560,1]{1,0:T(8,128)S(1)} %reshape.30.mask), custom_call_target="tpu_custom_call" | custom-call | tf_op jit(solution)/shard_map/unpack/pallas_call | solution.py:610
  47.2 0.1 collective-permute-start.4
  47.2 3.8 %collective-permute-start.5 = (f32[320,128]{1,0:T(8,128)S(1)}, f32[320,128]{1,0:T(8,128)S(1)}, u32[]{:S(2)}, u32[]{:S(2)}) collective-permute-start(f32[320,128]{1,0:T(8,128)S(1)} %get-tuple-element.57), channel_id=1, source_target_pairs={{8,0},{16,8},{24,16},{32,24},{40,32},{48,40},{56,48},{64,56},{72,6... | collective-permute-start | bytes 491528 | tf_op jit(solution)/shard_map/ppermute | solution.py:330
  51.1 3.0 %collective-permute-done.4.before.refs_8_ = f32[320,128]{1,0:T(8,128)S(1)} collective-permute-done((f32[320,128]{1,0:T(8,128)S(1)}, f32[320,128]{1,0:T(8,128)S(1)}, u32[]{:S(2)}, u32[]{:S(2)}) %collective-permute-start.4) | collective-permute-done | bytes 163872 | tf_op jit(solution)/shard_map/ppermute | solution.py:330
  54.1 0.0 collective-permute-done.5.after.refs_9_
  54.1 0.2 sides.5
  54.3 4.5 %collective-permute-start.6 = (f32[704,128]{1,0:T(8,128)S(1)}, f32[704,128]{1,0:T(8,128)S(1)}, u32[]{:S(2)}, u32[]{:S(2)}) collective-permute-start(f32[704,128]{1,0:T(8,128)S(1)} %get-tuple-element.58), channel_id=1, source_target_pairs={{0,1},{1,2},{2,3},{3,4},{4,5},{5,6},{6,7},{7,0},{8,9},{9,10},{10,1... | collective-permute-start | bytes 1081352 | tf_op jit(solution)/shard_map/ppermute | solution.py:330
  58.9 7.7 %collective-permute-done.6.refs_10_ = f32[704,128]{1,0:T(8,128)S(1)} collective-permute-done((f32[704,128]{1,0:T(8,128)S(1)}, f32[704,128]{1,0:T(8,128)S(1)}, u32[]{:S(2)}, u32[]{:S(2)}) %collective-permute-start.6) | collective-permute-done | bytes 360480 | tf_op jit(solution)/shard_map/ppermute | solution.py:330
  66.6 5.8 %collective-permute-done.7.refs_11_ = f32[704,128]{1,0:T(8,128)S(1)} collective-permute-done((f32[704,128]{1,0:T(8,128)S(1)}, f32[704,128]{1,0:T(8,128)S(1)}, u32[]{:S(2)}, u32[]{:S(2)}) %collective-permute-start.7) | collective-permute-done | bytes 360480 | tf_op jit(solution)/shard_map/ppermute | solution.py:330
  72.4 34.8 %step.3 = (f32[2560,128]{1,0:T(8,128)S(1)}, f32[360,128]{1,0:T(8,128)S(1)}, f32[360,128]{1,0:T(8,128)S(1)}, f32[6336,128]{1,0:T(8,128)S(1)}) custom-call(f32[2560,128]{1,0:T(8,128)S(1)} %bitcast.10, f32[360,128]{1,0:T(8,128)S(1)} %collective-permute-done.refs_1_.before, f32[360,128]{1,0:T(8,128)S(1)} %collective-permute-done.1.refs_2_.after, ...), custom_call_target="tpu_custom_call" | custom-call | flops 35000 | bytes 105000000 | tf_op jit(solution)/shard_map/step/pallas_call | solution.py:506
  107.3 0.3 collective-permute-start.8
  107.5 3.8 %collective-permute-start.9 = (f32[360,128]{1,0:T(8,128)S(1)}, f32[360,128]{1,0:T(8,128)S(1)}, u32[]{:S(2)}, u32[]{:S(2)}) collective-permute-start(f32[360,128]{1,0:T(8,128)S(1)} %get-tuple-element.62), channel_id=1, source_target_pairs={{8,0},{16,8},{24,16},{32,24},{40,32},{48,40},{56,48},{64,56},{72,6... | collective-permute-start | bytes 552968 | tf_op jit(solution)/shard_map/ppermute | solution.py:330
  111.4 3.2 %collective-permute-done.8.before.refs_1_ = f32[360,128]{1,0:T(8,128)S(1)} collective-permute-done((f32[360,128]{1,0:T(8,128)S(1)}, f32[360,128]{1,0:T(8,128)S(1)}, u32[]{:S(2)}, u32[]{:S(2)}) %collective-permute-start.8) | collective-permute-done | bytes 184352 | tf_op jit(solution)/shard_map/ppermute | solution.py:330
  114.6 0.3 collective-permute-done.9.after.refs_2_
  114.8 0.3 sides.6
  115.1 0.1 collective-permute-start.10
  115.2 2.0 collective-permute-start.11
  117.2 9.2 %early.4.refs_5_ = f32[3520,128]{1,0:T(8,128)S(1)} custom-call(f32[2560,128]{1,0:T(8,128)S(1)} %get-tuple-element.60.own.refs_0_, f32[360,128]{1,0:T(8,128)S(1)} %collective-permute-done.8.before.refs_1_, f32[360,128]{1,0:T(8,128)S(1)} %collective-permute-done.9.after.refs_2_, f32[6336,128]{1,0:T(8,128)S(1)} %get-tuple-element.65.refs_3_.refs_6_), custom_call_target="tpu_custom_call" | custom-call | flops 10000 | bytes 30000000 | tf_op jit(solution)/shard_map/early/pallas_call | solution.py:385
  126.5 0.0 collective-permute-done.10.refs_3_
  126.5 2.1 collective-permute-done.11.refs_4_
  128.5 33.4 %step.4 = (f32[2560,128]{1,0:T(8,128)S(1)}, f32[440,128]{1,0:T(8,128)S(1)}, f32[440,128]{1,0:T(8,128)S(1)}) custom-call(f32[2560,128]{1,0:T(8,128)S(1)} %get-tuple-element.60.own.refs_0_, f32[360,128]{1,0:T(8,128)S(1)} %collective-permute-done.8.before.refs_1_, f32[360,128]{1,0:T(8,128)S(1)} %collective-permute-done.9.after.refs_2_, ...), custom_call_target="tpu_custom_call" | custom-call | flops 35000 | bytes 105000000 | tf_op jit(solution)/shard_map/step/pallas_call | solution.py:506
  161.9 0.1 collective-permute-start.12
  162.0 3.8 %collective-permute-start.13 = (f32[440,128]{1,0:T(8,128)S(1)}, f32[440,128]{1,0:T(8,128)S(1)}, u32[]{:S(2)}, u32[]{:S(2)}) collective-permute-start(f32[440,128]{1,0:T(8,128)S(1)} %get-tuple-element.68), channel_id=1, source_target_pairs={{8,0},{16,8},{24,16},{32,24},{40,32},{48,40},{56,48},{64,56},{72,6... | collective-permute-start | bytes 675848 | tf_op jit(solution)/shard_map/ppermute | solution.py:330
  165.9 3.7 %collective-permute-done.12.before.refs_1_ = f32[440,128]{1,0:T(8,128)S(1)} collective-permute-done((f32[440,128]{1,0:T(8,128)S(1)}, f32[440,128]{1,0:T(8,128)S(1)}, u32[]{:S(2)}, u32[]{:S(2)}) %collective-permute-start.12) | collective-permute-done | bytes 225312 | tf_op jit(solution)/shard_map/ppermute | solution.py:330
  169.5 1.1 collective-permute-done.13.after.refs_2_
  170.7 0.3 sides.7
  171.0 1.1 collective-permute-start.14
  172.1 1.0 collective-permute-start.15
  173.1 9.7 %early.5.refs_5_ = f32[3520,128]{1,0:T(8,128)S(1)} custom-call(f32[2560,128]{1,0:T(8,128)S(1)} %get-tuple-element.66.own.refs_0_, f32[440,128]{1,0:T(8,128)S(1)} %collective-permute-done.12.before.refs_1_, f32[440,128]{1,0:T(8,128)S(1)} %collective-permute-done.13.after.refs_2_, f32[6336,128]{1,0:T(8,128)S(1)} %get-tuple-element.65.refs_3_.refs_6_), custom_call_target="tpu_custom_call" | custom-call | flops 10000 | bytes 30000000 | tf_op jit(solution)/shard_map/early/pallas_call | solution.py:385
  182.8 2.0 collective-permute-done.15.refs_4_
  184.8 44.3 %step.5 = f32[2560,128]{1,0:T(8,128)} custom-call(f32[2560,128]{1,0:T(8,128)S(1)} %get-tuple-element.66.own.refs_0_, f32[440,128]{1,0:T(8,128)S(1)} %collective-permute-done.12.before.refs_1_, f32[440,128]{1,0:T(8,128)S(1)} %collective-permute-done.13.after.refs_2_, f32[968,128]{1,0:T(8,128)S(1)} %collective-permute-done.14.refs_3_, ...), custom_call_target="tpu_custom_call" | custom-call | flops 35000 | bytes 105000000 | tf_op jit(solution)/shard_map/step/pallas_call | solution.py:506
  (20 shorter events, 0.0 us)
Async XLA Ops:
  1.0 12.8 %collective-permute-start = (f32[360,128]{1,0:T(8,128)S(1)}, f32[360,128]{1,0:T(8,128)S(1)}, u32[]{:S(2)}, u32[]{:S(2)}) collective-permute-start(f32[360,128]{1,0:T(8,128)S(1)} %bitcast.14), channel_id=1, source_target_pairs={{0,8},{8,16},{16,24},{24,32},{32,40},{40,48},{48,56},{56,64},{64,7... | collective-permute-start | bytes 552968 | tf_op jit(solution)/shard_map/ppermute | solution.py:330
  1.1 12.7 %collective-permute-start.1 = (f32[360,128]{1,0:T(8,128)S(1)}, f32[360,128]{1,0:T(8,128)S(1)}, u32[]{:S(2)}, u32[]{:S(2)}) collective-permute-start(f32[360,128]{1,0:T(8,128)S(1)} %bitcast.13), channel_id=1, source_target_pairs={{8,0},{16,8},{24,16},{32,24},{40,32},{48,40},{56,48},{64,56},{72,6... | collective-permute-start | bytes 552968 | tf_op jit(solution)/shard_map/ppermute | solution.py:330
  5.6 1.0 copy-start.5
  6.6 0.7 copy-start.6
  7.3 0.7 copy-start.7
  13.9 8.0 %copy-start = (f32[64,40,128]{2,1,0:T(8,128)S(1)}, f32[64,40,128]{2,1,0:T(8,128)}, u32[]{:S(2)}) copy-start(f32[64,40,128]{2,1,0:T(8,128)} %param.5) | copy-start | bytes 3932164
  13.9 25.5 %all-to-all-start = ((f32[128,1,2176]{2,1,0:T(1,128)}), f32[128,1,2176]{2,1,0:T(1,128)}, u32[]{:S(2)}, u32[]{:S(2)}) async-start(f32[128,1,2176]{2,1,0:T(1,128)} %bitcast.4), calls=%async_computation | async-start | bytes 2228224 | tf_op jit(solution)/shard_map/all_to_all | solution.py:599
  21.8 4.1 %copy-start.8 = (s32[64,40]{0,1:T(8,128)S(1)}, s32[64,40]{0,1:T(8,128)}, u32[]{:S(2)}) copy-start(s32[64,40]{0,1:T(8,128)} %param.6) | copy-start | bytes 30724
  23.0 24.1 %collective-permute-start.2 = (f32[792,128]{1,0:T(8,128)}, f32[792,128]{1,0:T(8,128)S(1)}, u32[]{:S(2)}, u32[]{:S(2)}) collective-permute-start(f32[792,128]{1,0:T(8,128)} %get-tuple-element.46), channel_id=1, source_target_pairs={{0,1},{1,2},{2,3},{3,4},{4,5},{5,6},{6,7},{7,0},{8,9},{9,10},{10,1... | collective-permute-start | bytes 1216520 | tf_op jit(solution)/shard_map/ppermute | solution.py:330
  25.9 21.2 %collective-permute-start.3 = (f32[792,128]{1,0:T(8,128)}, f32[792,128]{1,0:T(8,128)}, u32[]{:S(2)}, u32[]{:S(2)}) collective-permute-start(f32[792,128]{1,0:T(8,128)} %get-tuple-element.47), channel_id=1, source_target_pairs={{1,0},{2,1},{3,2},{4,3},{5,4},{6,5},{7,6},{0,7},{9,8},{10,9},{11,1... | collective-permute-start | bytes 1216520 | tf_op jit(solution)/shard_map/ppermute | solution.py:330
  35.7 1.3 copy-start.1
  37.0 1.2 copy-start.3
  39.4 33.1 %copy-start.2 = (f32[3520,128]{1,0:T(8,128)S(1)}, f32[3520,128]{1,0:T(8,128)}, u32[]{:S(2)}) copy-start(f32[3520,128]{1,0:T(8,128)} %copy-done.1) | copy-start | bytes 5406724
  39.4 33.1 %copy-start.4 = (f32[3520,128]{1,0:T(8,128)S(1)}, f32[3520,128]{1,0:T(8,128)}, u32[]{:S(2)}) copy-start(f32[3520,128]{1,0:T(8,128)} %copy-done.3) | copy-start | bytes 5406724
  47.2 6.9 %collective-permute-start.4 = (f32[320,128]{1,0:T(8,128)S(1)}, f32[320,128]{1,0:T(8,128)S(1)}, u32[]{:S(2)}, u32[]{:S(2)}) collective-permute-start(f32[320,128]{1,0:T(8,128)S(1)} %get-tuple-element.56), channel_id=1, source_target_pairs={{0,8},{8,16},{16,24},{24,32},{32,40},{40,48},{48,56},{56,64},{64,7... | collective-permute-start | bytes 491528 | tf_op jit(solution)/shard_map/ppermute | solution.py:330
  47.2 6.8 %collective-permute-start.5 = (f32[320,128]{1,0:T(8,128)S(1)}, f32[320,128]{1,0:T(8,128)S(1)}, u32[]{:S(2)}, u32[]{:S(2)}) collective-permute-start(f32[320,128]{1,0:T(8,128)S(1)} %get-tuple-element.57), channel_id=1, source_target_pairs={{8,0},{16,8},{24,16},{32,24},{40,32},{48,40},{56,48},{64,56},{72,6... | collective-permute-start | bytes 491528 | tf_op jit(solution)/shard_map/ppermute | solution.py:330
  54.3 12.3 %collective-permute-start.6 = (f32[704,128]{1,0:T(8,128)S(1)}, f32[704,128]{1,0:T(8,128)S(1)}, u32[]{:S(2)}, u32[]{:S(2)}) collective-permute-start(f32[704,128]{1,0:T(8,128)S(1)} %get-tuple-element.58), channel_id=1, source_target_pairs={{0,1},{1,2},{2,3},{3,4},{4,5},{5,6},{6,7},{7,0},{8,9},{9,10},{10,1... | collective-permute-start | bytes 1081352 | tf_op jit(solution)/shard_map/ppermute | solution.py:330
  58.9 13.6 %collective-permute-start.7 = (f32[704,128]{1,0:T(8,128)S(1)}, f32[704,128]{1,0:T(8,128)S(1)}, u32[]{:S(2)}, u32[]{:S(2)}) collective-permute-start(f32[704,128]{1,0:T(8,128)S(1)} %get-tuple-element.59), channel_id=1, source_target_pairs={{1,0},{2,1},{3,2},{4,3},{5,4},{6,5},{7,6},{0,7},{9,8},{10,9},{11,1... | collective-permute-start | bytes 1081352 | tf_op jit(solution)/shard_map/ppermute | solution.py:330
  107.3 7.3 %collective-permute-start.8 = (f32[360,128]{1,0:T(8,128)S(1)}, f32[360,128]{1,0:T(8,128)S(1)}, u32[]{:S(2)}, u32[]{:S(2)}) collective-permute-start(f32[360,128]{1,0:T(8,128)S(1)} %get-tuple-element.61), channel_id=1, source_target_pairs={{0,8},{8,16},{16,24},{24,32},{32,40},{40,48},{48,56},{56,64},{64,7... | collective-permute-start | bytes 552968 | tf_op jit(solution)/shard_map/ppermute | solution.py:330
  107.5 7.3 %collective-permute-start.9 = (f32[360,128]{1,0:T(8,128)S(1)}, f32[360,128]{1,0:T(8,128)S(1)}, u32[]{:S(2)}, u32[]{:S(2)}) collective-permute-start(f32[360,128]{1,0:T(8,128)S(1)} %get-tuple-element.62), channel_id=1, source_target_pairs={{8,0},{16,8},{24,16},{32,24},{40,32},{48,40},{56,48},{64,56},{72,6... | collective-permute-start | bytes 552968 | tf_op jit(solution)/shard_map/ppermute | solution.py:330
  115.1 11.4 %collective-permute-start.10 = (f32[792,128]{1,0:T(8,128)S(1)}, f32[792,128]{1,0:T(8,128)S(1)}, u32[]{:S(2)}, u32[]{:S(2)}) collective-permute-start(f32[792,128]{1,0:T(8,128)S(1)} %get-tuple-element.63), channel_id=1, source_target_pairs={{0,1},{1,2},{2,3},{3,4},{4,5},{5,6},{6,7},{7,0},{8,9},{9,10},{10,1... | collective-permute-start | bytes 1216520 | tf_op jit(solution)/shard_map/ppermute | solution.py:330
  115.2 13.3 %collective-permute-start.11 = (f32[792,128]{1,0:T(8,128)S(1)}, f32[792,128]{1,0:T(8,128)S(1)}, u32[]{:S(2)}, u32[]{:S(2)}) collective-permute-start(f32[792,128]{1,0:T(8,128)S(1)} %get-tuple-element.64), channel_id=1, source_target_pairs={{1,0},{2,1},{3,2},{4,3},{5,4},{6,5},{7,6},{0,7},{9,8},{10,9},{11,1... | collective-permute-start | bytes 1216520 | tf_op jit(solution)/shard_map/ppermute | solution.py:330
  161.9 7.6 %collective-permute-start.12 = (f32[440,128]{1,0:T(8,128)S(1)}, f32[440,128]{1,0:T(8,128)S(1)}, u32[]{:S(2)}, u32[]{:S(2)}) collective-permute-start(f32[440,128]{1,0:T(8,128)S(1)} %get-tuple-element.67), channel_id=1, source_target_pairs={{0,8},{8,16},{16,24},{24,32},{32,40},{40,48},{48,56},{56,64},{64,7... | collective-permute-start | bytes 675848 | tf_op jit(solution)/shard_map/ppermute | solution.py:330
  162.0 8.6 %collective-permute-start.13 = (f32[440,128]{1,0:T(8,128)S(1)}, f32[440,128]{1,0:T(8,128)S(1)}, u32[]{:S(2)}, u32[]{:S(2)}) collective-permute-start(f32[440,128]{1,0:T(8,128)S(1)} %get-tuple-element.68), channel_id=1, source_target_pairs={{8,0},{16,8},{24,16},{32,24},{40,32},{48,40},{56,48},{64,56},{72,6... | collective-permute-start | bytes 675848 | tf_op jit(solution)/shard_map/ppermute | solution.py:330
  171.0 11.8 %collective-permute-start.14 = (f32[968,128]{1,0:T(8,128)S(1)}, f32[968,128]{1,0:T(8,128)S(1)}, u32[]{:S(2)}, u32[]{:S(2)}) collective-permute-start(f32[968,128]{1,0:T(8,128)S(1)} %get-tuple-element.69), channel_id=1, source_target_pairs={{0,1},{1,2},{2,3},{3,4},{4,5},{5,6},{6,7},{7,0},{8,9},{9,10},{10,1... | collective-permute-start | bytes 1486856 | tf_op jit(solution)/shard_map/ppermute | solution.py:330
  172.1 12.7 %collective-permute-start.15 = (f32[968,128]{1,0:T(8,128)S(1)}, f32[968,128]{1,0:T(8,128)S(1)}, u32[]{:S(2)}, u32[]{:S(2)}) collective-permute-start(f32[968,128]{1,0:T(8,128)S(1)} %get-tuple-element.70), channel_id=1, source_target_pairs={{1,0},{2,1},{3,2},{4,3},{5,4},{6,5},{7,6},{0,7},{9,8},{10,9},{11,1... | collective-permute-start | bytes 1486856 | tf_op jit(solution)/shard_map/ppermute | solution.py:330

commit v5 on v4

--- a/solution.py
+++ b/solution.py
@@ -513,6 +513,10 @@
     )(*pieces, *early, *(pace if make_pace else (pace,)))
 
 
+PACK_BLOCK = 2176
+UNPACK_BLOCK = 1280
+
+
 def split(x):
     high = x.astype(jnp.bfloat16)
     low = (x - high.astype(F32)).astype(jnp.bfloat16)
@@ -536,7 +540,7 @@
     target = own * SLOTS + rank
     parts[...] = split(rows[...])
 
-    block = 128
+    block = PACK_BLOCK
 
     def body(b, carry):
         slot = lax.broadcasted_iota(jnp.int32, (block, count), 0) + b * block
@@ -569,7 +573,7 @@
             parts[pl.ds(k * DEVICES + 16 * b, 16), :] = split(jnp.concatenate(pair, axis=0))
     named = jnp.concatenate([columns[k : k + 1, :] for k in range(CAP)], axis=1)
 
-    block = 128
+    block = UNPACK_BLOCK
 
     def body(b, carry):
         cell = lax.broadcasted_iota(jnp.int32, (block, CAP * DEVICES), 0) + b * block

time: 230 us -> 225 us (0.978)
  Pallas kernels: 156 us -> 150 us
    pallas_call x1, Pallas kernels: 7.78 us -> 4.6 us  [shards(): pl.pallas_call(functools.partial(unpack_kernel, face), out_shape=(shape(C...]
    pallas_call x1, Pallas kernels: 5.84 us -> 2.92 us  [shards(): pl.pallas_call(pack_kernel, out_shape=shape(DEVICES * SLOTS), scratch_sha...]
  transfers between devices with their start and end apart: 17 -> 17, of which waited for: 10 -> 11; matrix products, arithmetic and copies ran while one was open for 0% -> 0% of each run, Pallas kernels for 19% -> 17%
where the time goes in v5:
time: 225 us; the launch traced here: 223 us
  Pallas kernels  150 us (67%)
  starting transfers between devices  34.4 us (15%)
  waiting for transfers between devices  31.8 us (14%)
  local copies, waits for them, and re-layouts  6.41 us (3%)
    pallas_call x3, Pallas kernels, step_call(): pl.pallas_call(functools.partial(runge_kutta, width, next_width, make_pac...  113 us
    ppermute x16, waiting for transfers between devices, shift_pair(): return (lax.ppermute(high, axis, up), lax.ppermute(low, axis, down))  30.6 us
    pallas_call x3, Pallas kernels, early_call(): pl.pallas_call(functools.partial(early_kernel, width, signed), out_shape=...  28.2 us
    ppermute x16, starting transfers between devices, shift_pair(): return (lax.ppermute(high, axis, up), lax.ppermute(low, axis, down))  26.5 us
    all_to_all x1, starting transfers between devices, shards(): lax.all_to_all(send.reshape(DEVICES, 1, SLOTS * NZ), ('gx', 'gy'), split_...  7.93 us
    unnamed x18, local copies, waits for them, and re-layouts  4.88 us
    pallas_call x1, Pallas kernels, shards(): pl.pallas_call(functools.partial(unpack_kernel, face), out_shape=(shape(C...  4.6 us
  transfers between devices with their start and end apart: 17, of which 11 were waited for; matrix products, arithmetic and copies ran while one was open for 0% of the time, Pallas kernels for 17%

profile of v5, /device:TPU:24, one launch (start us, length us, event | category | flops | bytes accessed | tf_op | source)
XLA Modules:
  0.0 223.0 jit_solution(3353561900520418225)
XLA Ops:
  0.0 1.0 fusion
  1.0 0.1 collective-permute-start
  1.1 4.5 %collective-permute-start.1 = (f32[360,128]{1,0:T(8,128)S(1)}, f32[360,128]{1,0:T(8,128)S(1)}, u32[]{:S(2)}, u32[]{:S(2)}) collective-permute-start(f32[360,128]{1,0:T(8,128)S(1)} %bitcast.13), channel_id=1, source_target_pairs={{8,0},{16,8},{24,16},{32,24},{40,32},{48,40},{56,48},{64,56},{72,6... | collective-permute-start | bytes 552968 | tf_op jit(solution)/shard_map/ppermute | solution.py:330
  5.6 1.0 copy-done.5
  6.6 0.7 copy-done.6
  7.3 0.7 copy-done.7
  8.0 2.9 %pack.1 = f32[2176,128]{1,0:T(8,128)} custom-call(f32[1024,128]{1,0:T(8,128)S(1)} %copy-done.5, s32[1,1024]{1,0:T(1,128)S(1)} %bitcast.11, s32[1,1024]{1,0:T(1,128)S(1)} %bitcast.12), custom_call_target="tpu_custom_call" | custom-call | flops 5000 | bytes 15000000 | tf_op jit(solution)/shard_map/pack/pallas_call | solution.py:592
  10.9 0.0 collective-permute-done.1.refs_2_.after
  10.9 7.9 %all-to-all-start = ((f32[128,1,2176]{2,1,0:T(1,128)}), f32[128,1,2176]{2,1,0:T(1,128)}, u32[]{:S(2)}, u32[]{:S(2)}) async-start(f32[128,1,2176]{2,1,0:T(1,128)} %bitcast.4), calls=%async_computation | async-start | bytes 2228224 | tf_op jit(solution)/shard_map/all_to_all | solution.py:603
  18.9 0.0 copy-start.8
  18.9 1.2 sides.4
  20.1 2.9 %collective-permute-start.2 = (f32[792,128]{1,0:T(8,128)}, f32[792,128]{1,0:T(8,128)S(1)}, u32[]{:S(2)}, u32[]{:S(2)}) collective-permute-start(f32[792,128]{1,0:T(8,128)} %get-tuple-element.46), channel_id=1, source_target_pairs={{0,1},{1,2},{2,3},{3,4},{4,5},{5,6},{6,7},{7,0},{8,9},{9,10},{10,1... | collective-permute-start | bytes 1216520 | tf_op jit(solution)/shard_map/ppermute | solution.py:330
  23.0 0.1 copy.10
  23.1 0.4 reshape.30.mask
  23.5 9.3 %early.3 = (f32[3520,128]{1,0:T(8,128)S(1)}, f32[3520,128]{1,0:T(8,128)S(1)}) custom-call(f32[2560,128]{1,0:T(8,128)S(1)} %bitcast.9, f32[360,128]{1,0:T(8,128)S(1)} %collective-permute-done.refs_1_.before, f32[360,128]{1,0:T(8,128)S(1)} %collective-permute-done.1.refs_2_.after), custom_call_target="tpu_custom_call" | custom-call | flops 10000 | bytes 30000000 | tf_op jit(solution)/shard_map/early/pallas_call | solution.py:385
  32.8 1.2 copy-done.1
  34.1 1.2 copy-done.3
  35.3 1.2 all-to-all-done
  36.4 4.6 %unpack.1 = (f32[2560,128]{1,0:T(8,128)S(1)}, f32[320,128]{1,0:T(8,128)S(1)}, f32[320,128]{1,0:T(8,128)S(1)}) custom-call(f32[2176,128]{1,0:T(8,128)} %bitcast.5.got, f32[2560,1]{1,0:T(8,128)S(1)} %reshape.30.mask), custom_call_target="tpu_custom_call" | custom-call | tf_op jit(solution)/shard_map/unpack/pallas_call | solution.py:614
  41.0 1.5 collective-permute-done.3.refs_4_
  42.5 3.9 %collective-permute-start.5 = (f32[320,128]{1,0:T(8,128)S(1)}, f32[320,128]{1,0:T(8,128)S(1)}, u32[]{:S(2)}, u32[]{:S(2)}) collective-permute-start(f32[320,128]{1,0:T(8,128)S(1)} %get-tuple-element.57), channel_id=1, source_target_pairs={{8,0},{16,8},{24,16},{32,24},{40,32},{48,40},{56,48},{64,56},{72,6... | collective-permute-start | bytes 491528 | tf_op jit(solution)/shard_map/ppermute | solution.py:330
  46.4 3.0 %collective-permute-done.4.before.refs_8_ = f32[320,128]{1,0:T(8,128)S(1)} collective-permute-done((f32[320,128]{1,0:T(8,128)S(1)}, f32[320,128]{1,0:T(8,128)S(1)}, u32[]{:S(2)}, u32[]{:S(2)}) %collective-permute-start.4) | collective-permute-done | bytes 163872 | tf_op jit(solution)/shard_map/ppermute | solution.py:330
  49.4 0.2 sides.5
  49.6 3.1 %collective-permute-start.6 = (f32[704,128]{1,0:T(8,128)S(1)}, f32[704,128]{1,0:T(8,128)S(1)}, u32[]{:S(2)}, u32[]{:S(2)}) collective-permute-start(f32[704,128]{1,0:T(8,128)S(1)} %get-tuple-element.58), channel_id=1, source_target_pairs={{0,1},{1,2},{2,3},{3,4},{4,5},{5,6},{6,7},{7,0},{8,9},{9,10},{10,1... | collective-permute-start | bytes 1081352 | tf_op jit(solution)/shard_map/ppermute | solution.py:330
  52.8 0.0 collective-permute-start.7
  52.8 7.7 %collective-permute-done.6.refs_10_ = f32[704,128]{1,0:T(8,128)S(1)} collective-permute-done((f32[704,128]{1,0:T(8,128)S(1)}, f32[704,128]{1,0:T(8,128)S(1)}, u32[]{:S(2)}, u32[]{:S(2)}) %collective-permute-start.6) | collective-permute-done | bytes 360480 | tf_op jit(solution)/shard_map/ppermute | solution.py:330
  60.5 5.8 %collective-permute-done.7.refs_11_ = f32[704,128]{1,0:T(8,128)S(1)} collective-permute-done((f32[704,128]{1,0:T(8,128)S(1)}, f32[704,128]{1,0:T(8,128)S(1)}, u32[]{:S(2)}, u32[]{:S(2)}) %collective-permute-start.7) | collective-permute-done | bytes 360480 | tf_op jit(solution)/shard_map/ppermute | solution.py:330
  66.3 34.8 %step.3 = (f32[2560,128]{1,0:T(8,128)S(1)}, f32[360,128]{1,0:T(8,128)S(1)}, f32[360,128]{1,0:T(8,128)S(1)}, f32[6336,128]{1,0:T(8,128)S(1)}) custom-call(f32[2560,128]{1,0:T(8,128)S(1)} %bitcast.10, f32[360,128]{1,0:T(8,128)S(1)} %collective-permute-done.refs_1_.before, f32[360,128]{1,0:T(8,128)S(1)} %collective-permute-done.1.refs_2_.after, ...), custom_call_target="tpu_custom_call" | custom-call | flops 35000 | bytes 105000000 | tf_op jit(solution)/shard_map/step/pallas_call | solution.py:506
  101.2 0.1 collective-permute-start.8
  101.3 3.8 %collective-permute-start.9 = (f32[360,128]{1,0:T(8,128)S(1)}, f32[360,128]{1,0:T(8,128)S(1)}, u32[]{:S(2)}, u32[]{:S(2)}) collective-permute-start(f32[360,128]{1,0:T(8,128)S(1)} %get-tuple-element.62), channel_id=1, source_target_pairs={{8,0},{16,8},{24,16},{32,24},{40,32},{48,40},{56,48},{64,56},{72,6... | collective-permute-start | bytes 552968 | tf_op jit(solution)/shard_map/ppermute | solution.py:330
  105.1 3.2 %collective-permute-done.8.before.refs_1_ = f32[360,128]{1,0:T(8,128)S(1)} collective-permute-done((f32[360,128]{1,0:T(8,128)S(1)}, f32[360,128]{1,0:T(8,128)S(1)}, u32[]{:S(2)}, u32[]{:S(2)}) %collective-permute-start.8) | collective-permute-done | bytes 184352 | tf_op jit(solution)/shard_map/ppermute | solution.py:330
  108.3 0.3 collective-permute-done.9.after.refs_2_
  108.6 0.3 sides.6
  108.9 0.1 collective-permute-start.10
  109.0 2.0 collective-permute-start.11
  111.0 9.2 %early.4.refs_5_ = f32[3520,128]{1,0:T(8,128)S(1)} custom-call(f32[2560,128]{1,0:T(8,128)S(1)} %get-tuple-element.60.own.refs_0_, f32[360,128]{1,0:T(8,128)S(1)} %collective-permute-done.8.before.refs_1_, f32[360,128]{1,0:T(8,128)S(1)} %collective-permute-done.9.after.refs_2_, f32[6336,128]{1,0:T(8,128)S(1)} %get-tuple-element.65.refs_3_.refs_6_), custom_call_target="tpu_custom_call" | custom-call | flops 10000 | bytes 30000000 | tf_op jit(solution)/shard_map/early/pallas_call | solution.py:385
  120.2 2.2 %collective-permute-done.11.refs_4_ = f32[792,128]{1,0:T(8,128)S(1)} collective-permute-done((f32[792,128]{1,0:T(8,128)S(1)}, f32[792,128]{1,0:T(8,128)S(1)}, u32[]{:S(2)}, u32[]{:S(2)}) %collective-permute-start.11) | collective-permute-done | bytes 405536 | tf_op jit(solution)/shard_map/ppermute | solution.py:330
  122.5 33.4 %step.4 = (f32[2560,128]{1,0:T(8,128)S(1)}, f32[440,128]{1,0:T(8,128)S(1)}, f32[440,128]{1,0:T(8,128)S(1)}) custom-call(f32[2560,128]{1,0:T(8,128)S(1)} %get-tuple-element.60.own.refs_0_, f32[360,128]{1,0:T(8,128)S(1)} %collective-permute-done.8.before.refs_1_, f32[360,128]{1,0:T(8,128)S(1)} %collective-permute-done.9.after.refs_2_, ...), custom_call_target="tpu_custom_call" | custom-call | flops 35000 | bytes 105000000 | tf_op jit(solution)/shard_map/step/pallas_call | solution.py:506
  155.9 0.1 collective-permute-start.12
  155.9 3.8 %collective-permute-start.13 = (f32[440,128]{1,0:T(8,128)S(1)}, f32[440,128]{1,0:T(8,128)S(1)}, u32[]{:S(2)}, u32[]{:S(2)}) collective-permute-start(f32[440,128]{1,0:T(8,128)S(1)} %get-tuple-element.68), channel_id=1, source_target_pairs={{8,0},{16,8},{24,16},{32,24},{40,32},{48,40},{56,48},{64,56},{72,6... | collective-permute-start | bytes 675848 | tf_op jit(solution)/shard_map/ppermute | solution.py:330
  159.8 3.7 %collective-permute-done.12.before.refs_1_ = f32[440,128]{1,0:T(8,128)S(1)} collective-permute-done((f32[440,128]{1,0:T(8,128)S(1)}, f32[440,128]{1,0:T(8,128)S(1)}, u32[]{:S(2)}, u32[]{:S(2)}) %collective-permute-start.12) | collective-permute-done | bytes 225312 | tf_op jit(solution)/shard_map/ppermute | solution.py:330
  163.4 1.2 collective-permute-done.13.after.refs_2_
  164.6 0.3 sides.7
  164.9 1.1 collective-permute-start.14
  166.0 1.0 collective-permute-start.15
  167.0 9.7 %early.5.refs_5_ = f32[3520,128]{1,0:T(8,128)S(1)} custom-call(f32[2560,128]{1,0:T(8,128)S(1)} %get-tuple-element.66.own.refs_0_, f32[440,128]{1,0:T(8,128)S(1)} %collective-permute-done.12.before.refs_1_, f32[440,128]{1,0:T(8,128)S(1)} %collective-permute-done.13.after.refs_2_, f32[6336,128]{1,0:T(8,128)S(1)} %get-tuple-element.65.refs_3_.refs_6_), custom_call_target="tpu_custom_call" | custom-call | flops 10000 | bytes 30000000 | tf_op jit(solution)/shard_map/early/pallas_call | solution.py:385
  176.7 2.0 collective-permute-done.15.refs_4_
  178.7 44.3 %step.5 = f32[2560,128]{1,0:T(8,128)} custom-call(f32[2560,128]{1,0:T(8,128)S(1)} %get-tuple-element.66.own.refs_0_, f32[440,128]{1,0:T(8,128)S(1)} %collective-permute-done.12.before.refs_1_, f32[440,128]{1,0:T(8,128)S(1)} %collective-permute-done.13.after.refs_2_, f32[968,128]{1,0:T(8,128)S(1)} %collective-permute-done.14.refs_3_, ...), custom_call_target="tpu_custom_call" | custom-call | flops 35000 | bytes 105000000 | tf_op jit(solution)/shard_map/step/pallas_call | solution.py:506
  (20 shorter events, 0.0 us)
Async XLA Ops:
  1.0 9.9 %collective-permute-start = (f32[360,128]{1,0:T(8,128)S(1)}, f32[360,128]{1,0:T(8,128)S(1)}, u32[]{:S(2)}, u32[]{:S(2)}) collective-permute-start(f32[360,128]{1,0:T(8,128)S(1)} %bitcast.14), channel_id=1, source_target_pairs={{0,8},{8,16},{16,24},{24,32},{32,40},{40,48},{48,56},{56,64},{64,7... | collective-permute-start | bytes 552968 | tf_op jit(solution)/shard_map/ppermute | solution.py:330
  1.1 9.8 %collective-permute-start.1 = (f32[360,128]{1,0:T(8,128)S(1)}, f32[360,128]{1,0:T(8,128)S(1)}, u32[]{:S(2)}, u32[]{:S(2)}) collective-permute-start(f32[360,128]{1,0:T(8,128)S(1)} %bitcast.13), channel_id=1, source_target_pairs={{8,0},{16,8},{24,16},{32,24},{40,32},{48,40},{56,48},{64,56},{72,6... | collective-permute-start | bytes 552968 | tf_op jit(solution)/shard_map/ppermute | solution.py:330
  5.6 1.0 copy-start.5
  6.6 0.7 copy-start.6
  7.3 0.7 copy-start.7
  10.9 8.0 %copy-start = (f32[64,40,128]{2,1,0:T(8,128)S(1)}, f32[64,40,128]{2,1,0:T(8,128)}, u32[]{:S(2)}) copy-start(f32[64,40,128]{2,1,0:T(8,128)} %param.5) | copy-start | bytes 3932164
  10.9 25.5 %all-to-all-start = ((f32[128,1,2176]{2,1,0:T(1,128)}), f32[128,1,2176]{2,1,0:T(1,128)}, u32[]{:S(2)}, u32[]{:S(2)}) async-start(f32[128,1,2176]{2,1,0:T(1,128)} %bitcast.4), calls=%async_computation | async-start | bytes 2228224 | tf_op jit(solution)/shard_map/all_to_all | solution.py:603
  18.9 4.1 %copy-start.8 = (s32[64,40]{0,1:T(8,128)S(1)}, s32[64,40]{0,1:T(8,128)}, u32[]{:S(2)}) copy-start(s32[64,40]{0,1:T(8,128)} %param.6) | copy-start | bytes 30724
  20.1 21.0 %collective-permute-start.2 = (f32[792,128]{1,0:T(8,128)}, f32[792,128]{1,0:T(8,128)S(1)}, u32[]{:S(2)}, u32[]{:S(2)}) collective-permute-start(f32[792,128]{1,0:T(8,128)} %get-tuple-element.46), channel_id=1, source_target_pairs={{0,1},{1,2},{2,3},{3,4},{4,5},{5,6},{6,7},{7,0},{8,9},{9,10},{10,1... | collective-permute-start | bytes 1216520 | tf_op jit(solution)/shard_map/ppermute | solution.py:330
  23.0 19.5 %collective-permute-start.3 = (f32[792,128]{1,0:T(8,128)}, f32[792,128]{1,0:T(8,128)}, u32[]{:S(2)}, u32[]{:S(2)}) collective-permute-start(f32[792,128]{1,0:T(8,128)} %get-tuple-element.47), channel_id=1, source_target_pairs={{1,0},{2,1},{3,2},{4,3},{5,4},{6,5},{7,6},{0,7},{9,8},{10,9},{11,1... | collective-permute-start | bytes 1216520 | tf_op jit(solution)/shard_map/ppermute | solution.py:330
  32.8 1.3 copy-start.1
  34.1 1.2 copy-start.3
  36.4 29.9 %copy-start.2 = (f32[3520,128]{1,0:T(8,128)S(1)}, f32[3520,128]{1,0:T(8,128)}, u32[]{:S(2)}) copy-start(f32[3520,128]{1,0:T(8,128)} %copy-done.1) | copy-start | bytes 5406724
  36.4 29.9 %copy-start.4 = (f32[3520,128]{1,0:T(8,128)S(1)}, f32[3520,128]{1,0:T(8,128)}, u32[]{:S(2)}) copy-start(f32[3520,128]{1,0:T(8,128)} %copy-done.3) | copy-start | bytes 5406724
  42.5 6.9 %collective-permute-start.4 = (f32[320,128]{1,0:T(8,128)S(1)}, f32[320,128]{1,0:T(8,128)S(1)}, u32[]{:S(2)}, u32[]{:S(2)}) collective-permute-start(f32[320,128]{1,0:T(8,128)S(1)} %get-tuple-element.56), channel_id=1, source_target_pairs={{0,8},{8,16},{16,24},{24,32},{32,40},{40,48},{48,56},{56,64},{64,7... | collective-permute-start | bytes 491528 | tf_op jit(solution)/shard_map/ppermute | solution.py:330
  42.5 6.9 %collective-permute-start.5 = (f32[320,128]{1,0:T(8,128)S(1)}, f32[320,128]{1,0:T(8,128)S(1)}, u32[]{:S(2)}, u32[]{:S(2)}) collective-permute-start(f32[320,128]{1,0:T(8,128)S(1)} %get-tuple-element.57), channel_id=1, source_target_pairs={{8,0},{16,8},{24,16},{32,24},{40,32},{48,40},{56,48},{64,56},{72,6... | collective-permute-start | bytes 491528 | tf_op jit(solution)/shard_map/ppermute | solution.py:330
  49.6 10.9 %collective-permute-start.6 = (f32[704,128]{1,0:T(8,128)S(1)}, f32[704,128]{1,0:T(8,128)S(1)}, u32[]{:S(2)}, u32[]{:S(2)}) collective-permute-start(f32[704,128]{1,0:T(8,128)S(1)} %get-tuple-element.58), channel_id=1, source_target_pairs={{0,1},{1,2},{2,3},{3,4},{4,5},{5,6},{6,7},{7,0},{8,9},{9,10},{10,1... | collective-permute-start | bytes 1081352 | tf_op jit(solution)/shard_map/ppermute | solution.py:330
  52.8 13.6 %collective-permute-start.7 = (f32[704,128]{1,0:T(8,128)S(1)}, f32[704,128]{1,0:T(8,128)S(1)}, u32[]{:S(2)}, u32[]{:S(2)}) collective-permute-start(f32[704,128]{1,0:T(8,128)S(1)} %get-tuple-element.59), channel_id=1, source_target_pairs={{1,0},{2,1},{3,2},{4,3},{5,4},{6,5},{7,6},{0,7},{9,8},{10,9},{11,1... | collective-permute-start | bytes 1081352 | tf_op jit(solution)/shard_map/ppermute | solution.py:330
  101.2 7.1 %collective-permute-start.8 = (f32[360,128]{1,0:T(8,128)S(1)}, f32[360,128]{1,0:T(8,128)S(1)}, u32[]{:S(2)}, u32[]{:S(2)}) collective-permute-start(f32[360,128]{1,0:T(8,128)S(1)} %get-tuple-element.61), channel_id=1, source_target_pairs={{0,8},{8,16},{16,24},{24,32},{32,40},{40,48},{48,56},{56,64},{64,7... | collective-permute-start | bytes 552968 | tf_op jit(solution)/shard_map/ppermute | solution.py:330
  101.3 7.3 %collective-permute-start.9 = (f32[360,128]{1,0:T(8,128)S(1)}, f32[360,128]{1,0:T(8,128)S(1)}, u32[]{:S(2)}, u32[]{:S(2)}) collective-permute-start(f32[360,128]{1,0:T(8,128)S(1)} %get-tuple-element.62), channel_id=1, source_target_pairs={{8,0},{16,8},{24,16},{32,24},{40,32},{48,40},{56,48},{64,56},{72,6... | collective-permute-start | bytes 552968 | tf_op jit(solution)/shard_map/ppermute | solution.py:330
  108.9 11.4 %collective-permute-start.10 = (f32[792,128]{1,0:T(8,128)S(1)}, f32[792,128]{1,0:T(8,128)S(1)}, u32[]{:S(2)}, u32[]{:S(2)}) collective-permute-start(f32[792,128]{1,0:T(8,128)S(1)} %get-tuple-element.63), channel_id=1, source_target_pairs={{0,1},{1,2},{2,3},{3,4},{4,5},{5,6},{6,7},{7,0},{8,9},{9,10},{10,1... | collective-permute-start | bytes 1216520 | tf_op jit(solution)/shard_map/ppermute | solution.py:330
  109.0 13.5 %collective-permute-start.11 = (f32[792,128]{1,0:T(8,128)S(1)}, f32[792,128]{1,0:T(8,128)S(1)}, u32[]{:S(2)}, u32[]{:S(2)}) collective-permute-start(f32[792,128]{1,0:T(8,128)S(1)} %get-tuple-element.64), channel_id=1, source_target_pairs={{1,0},{2,1},{3,2},{4,3},{5,4},{6,5},{7,6},{0,7},{9,8},{10,9},{11,1... | collective-permute-start | bytes 1216520 | tf_op jit(solution)/shard_map/ppermute | solution.py:330
  155.9 7.6 %collective-permute-start.12 = (f32[440,128]{1,0:T(8,128)S(1)}, f32[440,128]{1,0:T(8,128)S(1)}, u32[]{:S(2)}, u32[]{:S(2)}) collective-permute-start(f32[440,128]{1,0:T(8,128)S(1)} %get-tuple-element.67), channel_id=1, source_target_pairs={{0,8},{8,16},{16,24},{24,32},{32,40},{40,48},{48,56},{56,64},{64,7... | collective-permute-start | bytes 675848 | tf_op jit(solution)/shard_map/ppermute | solution.py:330
  155.9 8.7 %collective-permute-start.13 = (f32[440,128]{1,0:T(8,128)S(1)}, f32[440,128]{1,0:T(8,128)S(1)}, u32[]{:S(2)}, u32[]{:S(2)}) collective-permute-start(f32[440,128]{1,0:T(8,128)S(1)} %get-tuple-element.68), channel_id=1, source_target_pairs={{8,0},{16,8},{24,16},{32,24},{40,32},{48,40},{56,48},{64,56},{72,6... | collective-permute-start | bytes 675848 | tf_op jit(solution)/shard_map/ppermute | solution.py:330
  164.9 11.8 %collective-permute-start.14 = (f32[968,128]{1,0:T(8,128)S(1)}, f32[968,128]{1,0:T(8,128)S(1)}, u32[]{:S(2)}, u32[]{:S(2)}) collective-permute-start(f32[968,128]{1,0:T(8,128)S(1)} %get-tuple-element.69), channel_id=1, source_target_pairs={{0,1},{1,2},{2,3},{3,4},{4,5},{5,6},{6,7},{7,0},{8,9},{9,10},{10,1... | collective-permute-start | bytes 1486856 | tf_op jit(solution)/shard_map/ppermute | solution.py:330
  166.0 12.7 %collective-permute-start.15 = (f32[968,128]{1,0:T(8,128)S(1)}, f32[968,128]{1,0:T(8,128)S(1)}, u32[]{:S(2)}, u32[]{:S(2)}) collective-permute-start(f32[968,128]{1,0:T(8,128)S(1)} %get-tuple-element.70), channel_id=1, source_target_pairs={{1,0},{2,1},{3,2},{4,3},{5,4},{6,5},{7,6},{0,7},{9,8},{10,9},{11,1... | collective-permute-start | bytes 1486856 | tf_op jit(solution)/shard_map/ppermute | solution.py:330

commit v6 on v5

--- a/solution.py
+++ b/solution.py
@@ -202,7 +202,7 @@
     over_rows(geo, row)
 
 
-def x_pass(src, pace, faces, geo, emit):
+def x_pass(src, pace, faces, geo, emit, signs=None):
     ny, x_lo, x_hi, _ = geo
     unroll = (x_hi - x_lo) // TURNS
 
@@ -247,7 +247,7 @@
                     emit(x, j, tile(x, j), rising, falling)
                     continue
                 p = load_tile(pace, geo, x, j)
-                sign = speed_sign(p)
+                sign = speed_sign(p) if signs is None else signs[at, :]
                 total = upwind(sign, left, right) + upwind(sign, z_left, z_right)
                 emit(x, j, tile(x, j), p, total)
             return state
@@ -259,15 +259,18 @@
 
 
 def stage(src, slopes, pace, term, faces, geo, finish):
+    signs, *faces = faces
+
     def keep(x, j, u, p, value):
         term[packed(geo, x, j), :] = value
+        signs[packed(geo, x, j), :] = speed_sign(p)
         z_row(slopes, faces, geo, x, j)
 
     def join(x, j, u, p, value):
         finish(x, j, u, u + p * root(value + term[packed(geo, x, j), :]))
 
     y_pass(src, pace, geo, keep)
-    x_pass(src, pace, faces, geo, join)
+    x_pass(src, pace, faces, geo, join, signs)
 
 
 def fill_block(ext, own, before, after, width, slopes=None):
@@ -409,7 +412,7 @@
     if make_pace:
         pace = refs.pop(0)
     base, first, second = refs[:3]
-    even, odd, term, faces = refs[3:5], refs[5:7], refs[7], refs[8:10]
+    even, odd, term, faces = refs[3:5], refs[5:7], refs[7], refs[8:11]
 
     fill_block(base, own, before, after, width)
     fill_sides(base, left, right, width, even)
@@ -506,7 +509,7 @@
     return pl.pallas_call(
         functools.partial(runge_kutta, width, next_width, make_pace),
         out_shape=tuple(outs),
-        scratch_shapes=[vmem(EXT)] * 7 + [vmem(XR * 56)] * 3,
+        scratch_shapes=[vmem(EXT)] * 7 + [vmem(XR * 56)] * 4,
         compiler_params=params(),
         cost_estimate=cost(35),
         name="step",

time: 225 us -> 223 us (level)
  no operation moved by 1% of the time
where the time goes in v6:
time: 223 us; the launch traced here: 221 us
  Pallas kernels  148 us (66%)
  starting transfers between devices  34.4 us (15%)
  waiting for transfers between devices  31.8 us (14%)
  local copies, waits for them, and re-layouts  6.41 us (3%)
    pallas_call x3, Pallas kernels, step_call(): pl.pallas_call(functools.partial(runge_kutta, width, next_width, make_pac...  111 us
    ppermute x16, waiting for transfers between devices, shift_pair(): return (lax.ppermute(high, axis, up), lax.ppermute(low, axis, down))  30.6 us
    pallas_call x3, Pallas kernels, early_call(): pl.pallas_call(functools.partial(early_kernel, width, signed), out_shape=...  28.2 us
    ppermute x16, starting transfers between devices, shift_pair(): return (lax.ppermute(high, axis, up), lax.ppermute(low, axis, down))  26.5 us
    all_to_all x1, starting transfers between devices, shards(): lax.all_to_all(send.reshape(DEVICES, 1, SLOTS * NZ), ('gx', 'gy'), split_...  7.93 us
    unnamed x18, local copies, waits for them, and re-layouts  4.88 us
    pallas_call x1, Pallas kernels, shards(): pl.pallas_call(functools.partial(unpack_kernel, face), out_shape=(shape(C...  4.6 us
  transfers between devices with their start and end apart: 17, of which 11 were waited for; matrix products, arithmetic and copies ran while one was open for 0% of the time, Pallas kernels for 17%

profile of v6, /device:TPU:24, one launch (start us, length us, event | category | flops | bytes accessed | tf_op | source)
XLA Modules:
  0.0 221.0 jit_solution(174227000708156849)
XLA Ops:
  0.0 1.0 fusion
  1.0 0.1 collective-permute-start
  1.1 4.5 %collective-permute-start.1 = (f32[360,128]{1,0:T(8,128)S(1)}, f32[360,128]{1,0:T(8,128)S(1)}, u32[]{:S(2)}, u32[]{:S(2)}) collective-permute-start(f32[360,128]{1,0:T(8,128)S(1)} %bitcast.13), channel_id=1, source_target_pairs={{8,0},{16,8},{24,16},{32,24},{40,32},{48,40},{56,48},{64,56},{72,6... | collective-permute-start | bytes 552968 | tf_op jit(solution)/shard_map/ppermute | solution.py:333
  5.6 1.0 copy-done.5
  6.6 0.7 copy-done.6
  7.3 0.7 copy-done.7
  8.0 2.9 %pack.1 = f32[2176,128]{1,0:T(8,128)} custom-call(f32[1024,128]{1,0:T(8,128)S(1)} %copy-done.5, s32[1,1024]{1,0:T(1,128)S(1)} %bitcast.11, s32[1,1024]{1,0:T(1,128)S(1)} %bitcast.12), custom_call_target="tpu_custom_call" | custom-call | flops 5000 | bytes 15000000 | tf_op jit(solution)/shard_map/pack/pallas_call | solution.py:595
  10.9 0.0 collective-permute-done.1.refs_2_.after
  10.9 7.9 %all-to-all-start = ((f32[128,1,2176]{2,1,0:T(1,128)}), f32[128,1,2176]{2,1,0:T(1,128)}, u32[]{:S(2)}, u32[]{:S(2)}) async-start(f32[128,1,2176]{2,1,0:T(1,128)} %bitcast.4), calls=%async_computation | async-start | bytes 2228224 | tf_op jit(solution)/shard_map/all_to_all | solution.py:606
  18.9 0.0 copy-start.8
  18.9 1.2 sides.4
  20.1 2.9 %collective-permute-start.2 = (f32[792,128]{1,0:T(8,128)}, f32[792,128]{1,0:T(8,128)S(1)}, u32[]{:S(2)}, u32[]{:S(2)}) collective-permute-start(f32[792,128]{1,0:T(8,128)} %get-tuple-element.46), channel_id=1, source_target_pairs={{0,1},{1,2},{2,3},{3,4},{4,5},{5,6},{6,7},{7,0},{8,9},{9,10},{10,1... | collective-permute-start | bytes 1216520 | tf_op jit(solution)/shard_map/ppermute | solution.py:333
  23.0 0.1 copy.10
  23.1 0.4 reshape.30.mask
  23.5 9.3 %early.3 = (f32[3520,128]{1,0:T(8,128)S(1)}, f32[3520,128]{1,0:T(8,128)S(1)}) custom-call(f32[2560,128]{1,0:T(8,128)S(1)} %bitcast.9, f32[360,128]{1,0:T(8,128)S(1)} %collective-permute-done.refs_1_.before, f32[360,128]{1,0:T(8,128)S(1)} %collective-permute-done.1.refs_2_.after), custom_call_target="tpu_custom_call" | custom-call | flops 10000 | bytes 30000000 | tf_op jit(solution)/shard_map/early/pallas_call | solution.py:388
  32.8 1.2 copy-done.1
  34.1 1.2 copy-done.3
  35.3 1.2 all-to-all-done
  36.4 4.6 %unpack.1 = (f32[2560,128]{1,0:T(8,128)S(1)}, f32[320,128]{1,0:T(8,128)S(1)}, f32[320,128]{1,0:T(8,128)S(1)}) custom-call(f32[2176,128]{1,0:T(8,128)} %bitcast.5.got, f32[2560,1]{1,0:T(8,128)S(1)} %reshape.30.mask), custom_call_target="tpu_custom_call" | custom-call | tf_op jit(solution)/shard_map/unpack/pallas_call | solution.py:617
  41.0 1.5 collective-permute-done.3.refs_4_
  42.5 3.9 %collective-permute-start.5 = (f32[320,128]{1,0:T(8,128)S(1)}, f32[320,128]{1,0:T(8,128)S(1)}, u32[]{:S(2)}, u32[]{:S(2)}) collective-permute-start(f32[320,128]{1,0:T(8,128)S(1)} %get-tuple-element.57), channel_id=1, source_target_pairs={{8,0},{16,8},{24,16},{32,24},{40,32},{48,40},{56,48},{64,56},{72,6... | collective-permute-start | bytes 491528 | tf_op jit(solution)/shard_map/ppermute | solution.py:333
  46.4 3.0 %collective-permute-done.4.before.refs_8_ = f32[320,128]{1,0:T(8,128)S(1)} collective-permute-done((f32[320,128]{1,0:T(8,128)S(1)}, f32[320,128]{1,0:T(8,128)S(1)}, u32[]{:S(2)}, u32[]{:S(2)}) %collective-permute-start.4) | collective-permute-done | bytes 163872 | tf_op jit(solution)/shard_map/ppermute | solution.py:333
  49.4 0.2 sides.5
  49.6 3.1 %collective-permute-start.6 = (f32[704,128]{1,0:T(8,128)S(1)}, f32[704,128]{1,0:T(8,128)S(1)}, u32[]{:S(2)}, u32[]{:S(2)}) collective-permute-start(f32[704,128]{1,0:T(8,128)S(1)} %get-tuple-element.58), channel_id=1, source_target_pairs={{0,1},{1,2},{2,3},{3,4},{4,5},{5,6},{6,7},{7,0},{8,9},{9,10},{10,1... | collective-permute-start | bytes 1081352 | tf_op jit(solution)/shard_map/ppermute | solution.py:333
  52.8 0.0 collective-permute-start.7
  52.8 7.7 %collective-permute-done.6.refs_10_ = f32[704,128]{1,0:T(8,128)S(1)} collective-permute-done((f32[704,128]{1,0:T(8,128)S(1)}, f32[704,128]{1,0:T(8,128)S(1)}, u32[]{:S(2)}, u32[]{:S(2)}) %collective-permute-start.6) | collective-permute-done | bytes 360480 | tf_op jit(solution)/shard_map/ppermute | solution.py:333
  60.5 5.8 %collective-permute-done.7.refs_11_ = f32[704,128]{1,0:T(8,128)S(1)} collective-permute-done((f32[704,128]{1,0:T(8,128)S(1)}, f32[704,128]{1,0:T(8,128)S(1)}, u32[]{:S(2)}, u32[]{:S(2)}) %collective-permute-start.7) | collective-permute-done | bytes 360480 | tf_op jit(solution)/shard_map/ppermute | solution.py:333
  66.3 34.2 %step.3 = (f32[2560,128]{1,0:T(8,128)S(1)}, f32[360,128]{1,0:T(8,128)S(1)}, f32[360,128]{1,0:T(8,128)S(1)}, f32[6336,128]{1,0:T(8,128)S(1)}) custom-call(f32[2560,128]{1,0:T(8,128)S(1)} %bitcast.10, f32[360,128]{1,0:T(8,128)S(1)} %collective-permute-done.refs_1_.before, f32[360,128]{1,0:T(8,128)S(1)} %collective-permute-done.1.refs_2_.after, ...), custom_call_target="tpu_custom_call" | custom-call | flops 35000 | bytes 105000000 | tf_op jit(solution)/shard_map/step/pallas_call | solution.py:509
  100.5 0.1 collective-permute-start.8
  100.6 3.8 %collective-permute-start.9 = (f32[360,128]{1,0:T(8,128)S(1)}, f32[360,128]{1,0:T(8,128)S(1)}, u32[]{:S(2)}, u32[]{:S(2)}) collective-permute-start(f32[360,128]{1,0:T(8,128)S(1)} %get-tuple-element.62), channel_id=1, source_target_pairs={{8,0},{16,8},{24,16},{32,24},{40,32},{48,40},{56,48},{64,56},{72,6... | collective-permute-start | bytes 552968 | tf_op jit(solution)/shard_map/ppermute | solution.py:333
  104.4 3.2 %collective-permute-done.8.before.refs_1_ = f32[360,128]{1,0:T(8,128)S(1)} collective-permute-done((f32[360,128]{1,0:T(8,128)S(1)}, f32[360,128]{1,0:T(8,128)S(1)}, u32[]{:S(2)}, u32[]{:S(2)}) %collective-permute-start.8) | collective-permute-done | bytes 184352 | tf_op jit(solution)/shard_map/ppermute | solution.py:333
  107.7 0.3 collective-permute-done.9.after.refs_2_
  107.9 0.3 sides.6
  108.2 0.1 collective-permute-start.10
  108.3 2.0 collective-permute-start.11
  110.3 9.2 %early.4.refs_5_ = f32[3520,128]{1,0:T(8,128)S(1)} custom-call(f32[2560,128]{1,0:T(8,128)S(1)} %get-tuple-element.60.own.refs_0_, f32[360,128]{1,0:T(8,128)S(1)} %collective-permute-done.8.before.refs_1_, f32[360,128]{1,0:T(8,128)S(1)} %collective-permute-done.9.after.refs_2_, f32[6336,128]{1,0:T(8,128)S(1)} %get-tuple-element.65.refs_3_.refs_6_), custom_call_target="tpu_custom_call" | custom-call | flops 10000 | bytes 30000000 | tf_op jit(solution)/shard_map/early/pallas_call | solution.py:388
  119.6 2.2 %collective-permute-done.11.refs_4_ = f32[792,128]{1,0:T(8,128)S(1)} collective-permute-done((f32[792,128]{1,0:T(8,128)S(1)}, f32[792,128]{1,0:T(8,128)S(1)}, u32[]{:S(2)}, u32[]{:S(2)}) %collective-permute-start.11) | collective-permute-done | bytes 405536 | tf_op jit(solution)/shard_map/ppermute | solution.py:333
  121.8 32.7 %step.4 = (f32[2560,128]{1,0:T(8,128)S(1)}, f32[440,128]{1,0:T(8,128)S(1)}, f32[440,128]{1,0:T(8,128)S(1)}) custom-call(f32[2560,128]{1,0:T(8,128)S(1)} %get-tuple-element.60.own.refs_0_, f32[360,128]{1,0:T(8,128)S(1)} %collective-permute-done.8.before.refs_1_, f32[360,128]{1,0:T(8,128)S(1)} %collective-permute-done.9.after.refs_2_, ...), custom_call_target="tpu_custom_call" | custom-call | flops 35000 | bytes 105000000 | tf_op jit(solution)/shard_map/step/pallas_call | solution.py:509
  154.5 0.1 collective-permute-start.12
  154.6 3.8 %collective-permute-start.13 = (f32[440,128]{1,0:T(8,128)S(1)}, f32[440,128]{1,0:T(8,128)S(1)}, u32[]{:S(2)}, u32[]{:S(2)}) collective-permute-start(f32[440,128]{1,0:T(8,128)S(1)} %get-tuple-element.68), channel_id=1, source_target_pairs={{8,0},{16,8},{24,16},{32,24},{40,32},{48,40},{56,48},{64,56},{72,6... | collective-permute-start | bytes 675848 | tf_op jit(solution)/shard_map/ppermute | solution.py:333
  158.5 3.7 %collective-permute-done.12.before.refs_1_ = f32[440,128]{1,0:T(8,128)S(1)} collective-permute-done((f32[440,128]{1,0:T(8,128)S(1)}, f32[440,128]{1,0:T(8,128)S(1)}, u32[]{:S(2)}, u32[]{:S(2)}) %collective-permute-start.12) | collective-permute-done | bytes 225312 | tf_op jit(solution)/shard_map/ppermute | solution.py:333
  162.1 1.2 collective-permute-done.13.after.refs_2_
  163.3 0.3 sides.7
  163.6 1.1 collective-permute-start.14
  164.7 1.0 collective-permute-start.15
  165.7 9.7 %early.5.refs_5_ = f32[3520,128]{1,0:T(8,128)S(1)} custom-call(f32[2560,128]{1,0:T(8,128)S(1)} %get-tuple-element.66.own.refs_0_, f32[440,128]{1,0:T(8,128)S(1)} %collective-permute-done.12.before.refs_1_, f32[440,128]{1,0:T(8,128)S(1)} %collective-permute-done.13.after.refs_2_, f32[6336,128]{1,0:T(8,128)S(1)} %get-tuple-element.65.refs_3_.refs_6_), custom_call_target="tpu_custom_call" | custom-call | flops 10000 | bytes 30000000 | tf_op jit(solution)/shard_map/early/pallas_call | solution.py:388
  175.4 2.0 collective-permute-done.15.refs_4_
  177.4 43.6 %step.5 = f32[2560,128]{1,0:T(8,128)} custom-call(f32[2560,128]{1,0:T(8,128)S(1)} %get-tuple-element.66.own.refs_0_, f32[440,128]{1,0:T(8,128)S(1)} %collective-permute-done.12.before.refs_1_, f32[440,128]{1,0:T(8,128)S(1)} %collective-permute-done.13.after.refs_2_, f32[968,128]{1,0:T(8,128)S(1)} %collective-permute-done.14.refs_3_, ...), custom_call_target="tpu_custom_call" | custom-call | flops 35000 | bytes 105000000 | tf_op jit(solution)/shard_map/step/pallas_call | solution.py:509
  (20 shorter events, 0.0 us)
Async XLA Ops:
  1.0 9.9 %collective-permute-start = (f32[360,128]{1,0:T(8,128)S(1)}, f32[360,128]{1,0:T(8,128)S(1)}, u32[]{:S(2)}, u32[]{:S(2)}) collective-permute-start(f32[360,128]{1,0:T(8,128)S(1)} %bitcast.14), channel_id=1, source_target_pairs={{0,8},{8,16},{16,24},{24,32},{32,40},{40,48},{48,56},{56,64},{64,7... | collective-permute-start | bytes 552968 | tf_op jit(solution)/shard_map/ppermute | solution.py:333
  1.1 9.8 %collective-permute-start.1 = (f32[360,128]{1,0:T(8,128)S(1)}, f32[360,128]{1,0:T(8,128)S(1)}, u32[]{:S(2)}, u32[]{:S(2)}) collective-permute-start(f32[360,128]{1,0:T(8,128)S(1)} %bitcast.13), channel_id=1, source_target_pairs={{8,0},{16,8},{24,16},{32,24},{40,32},{48,40},{56,48},{64,56},{72,6... | collective-permute-start | bytes 552968 | tf_op jit(solution)/shard_map/ppermute | solution.py:333
  5.6 1.0 copy-start.5
  6.6 0.7 copy-start.6
  7.3 0.7 copy-start.7
  10.9 8.0 %copy-start = (f32[64,40,128]{2,1,0:T(8,128)S(1)}, f32[64,40,128]{2,1,0:T(8,128)}, u32[]{:S(2)}) copy-start(f32[64,40,128]{2,1,0:T(8,128)} %param.5) | copy-start | bytes 3932164
  10.9 25.5 %all-to-all-start = ((f32[128,1,2176]{2,1,0:T(1,128)}), f32[128,1,2176]{2,1,0:T(1,128)}, u32[]{:S(2)}, u32[]{:S(2)}) async-start(f32[128,1,2176]{2,1,0:T(1,128)} %bitcast.4), calls=%async_computation | async-start | bytes 2228224 | tf_op jit(solution)/shard_map/all_to_all | solution.py:606
  18.9 4.1 %copy-start.8 = (s32[64,40]{0,1:T(8,128)S(1)}, s32[64,40]{0,1:T(8,128)}, u32[]{:S(2)}) copy-start(s32[64,40]{0,1:T(8,128)} %param.6) | copy-start | bytes 30724
  20.1 21.0 %collective-permute-start.2 = (f32[792,128]{1,0:T(8,128)}, f32[792,128]{1,0:T(8,128)S(1)}, u32[]{:S(2)}, u32[]{:S(2)}) collective-permute-start(f32[792,128]{1,0:T(8,128)} %get-tuple-element.46), channel_id=1, source_target_pairs={{0,1},{1,2},{2,3},{3,4},{4,5},{5,6},{6,7},{7,0},{8,9},{9,10},{10,1... | collective-permute-start | bytes 1216520 | tf_op jit(solution)/shard_map/ppermute | solution.py:333
  23.0 19.5 %collective-permute-start.3 = (f32[792,128]{1,0:T(8,128)}, f32[792,128]{1,0:T(8,128)}, u32[]{:S(2)}, u32[]{:S(2)}) collective-permute-start(f32[792,128]{1,0:T(8,128)} %get-tuple-element.47), channel_id=1, source_target_pairs={{1,0},{2,1},{3,2},{4,3},{5,4},{6,5},{7,6},{0,7},{9,8},{10,9},{11,1... | collective-permute-start | bytes 1216520 | tf_op jit(solution)/shard_map/ppermute | solution.py:333
  32.8 1.3 copy-start.1
  34.1 1.2 copy-start.3
  36.4 29.9 %copy-start.2 = (f32[3520,128]{1,0:T(8,128)S(1)}, f32[3520,128]{1,0:T(8,128)}, u32[]{:S(2)}) copy-start(f32[3520,128]{1,0:T(8,128)} %copy-done.1) | copy-start | bytes 5406724
  36.4 29.9 %copy-start.4 = (f32[3520,128]{1,0:T(8,128)S(1)}, f32[3520,128]{1,0:T(8,128)}, u32[]{:S(2)}) copy-start(f32[3520,128]{1,0:T(8,128)} %copy-done.3) | copy-start | bytes 5406724
  42.5 6.9 %collective-permute-start.4 = (f32[320,128]{1,0:T(8,128)S(1)}, f32[320,128]{1,0:T(8,128)S(1)}, u32[]{:S(2)}, u32[]{:S(2)}) collective-permute-start(f32[320,128]{1,0:T(8,128)S(1)} %get-tuple-element.56), channel_id=1, source_target_pairs={{0,8},{8,16},{16,24},{24,32},{32,40},{40,48},{48,56},{56,64},{64,7... | collective-permute-start | bytes 491528 | tf_op jit(solution)/shard_map/ppermute | solution.py:333
  42.5 6.9 %collective-permute-start.5 = (f32[320,128]{1,0:T(8,128)S(1)}, f32[320,128]{1,0:T(8,128)S(1)}, u32[]{:S(2)}, u32[]{:S(2)}) collective-permute-start(f32[320,128]{1,0:T(8,128)S(1)} %get-tuple-element.57), channel_id=1, source_target_pairs={{8,0},{16,8},{24,16},{32,24},{40,32},{48,40},{56,48},{64,56},{72,6... | collective-permute-start | bytes 491528 | tf_op jit(solution)/shard_map/ppermute | solution.py:333
  49.6 10.9 %collective-permute-start.6 = (f32[704,128]{1,0:T(8,128)S(1)}, f32[704,128]{1,0:T(8,128)S(1)}, u32[]{:S(2)}, u32[]{:S(2)}) collective-permute-start(f32[704,128]{1,0:T(8,128)S(1)} %get-tuple-element.58), channel_id=1, source_target_pairs={{0,1},{1,2},{2,3},{3,4},{4,5},{5,6},{6,7},{7,0},{8,9},{9,10},{10,1... | collective-permute-start | bytes 1081352 | tf_op jit(solution)/shard_map/ppermute | solution.py:333
  52.8 13.6 %collective-permute-start.7 = (f32[704,128]{1,0:T(8,128)S(1)}, f32[704,128]{1,0:T(8,128)S(1)}, u32[]{:S(2)}, u32[]{:S(2)}) collective-permute-start(f32[704,128]{1,0:T(8,128)S(1)} %get-tuple-element.59), channel_id=1, source_target_pairs={{1,0},{2,1},{3,2},{4,3},{5,4},{6,5},{7,6},{0,7},{9,8},{10,9},{11,1... | collective-permute-start | bytes 1081352 | tf_op jit(solution)/shard_map/ppermute | solution.py:333
  100.5 7.1 %collective-permute-start.8 = (f32[360,128]{1,0:T(8,128)S(1)}, f32[360,128]{1,0:T(8,128)S(1)}, u32[]{:S(2)}, u32[]{:S(2)}) collective-permute-start(f32[360,128]{1,0:T(8,128)S(1)} %get-tuple-element.61), channel_id=1, source_target_pairs={{0,8},{8,16},{16,24},{24,32},{32,40},{40,48},{48,56},{56,64},{64,7... | collective-permute-start | bytes 552968 | tf_op jit(solution)/shard_map/ppermute | solution.py:333
  100.6 7.3 %collective-permute-start.9 = (f32[360,128]{1,0:T(8,128)S(1)}, f32[360,128]{1,0:T(8,128)S(1)}, u32[]{:S(2)}, u32[]{:S(2)}) collective-permute-start(f32[360,128]{1,0:T(8,128)S(1)} %get-tuple-element.62), channel_id=1, source_target_pairs={{8,0},{16,8},{24,16},{32,24},{40,32},{48,40},{56,48},{64,56},{72,6... | collective-permute-start | bytes 552968 | tf_op jit(solution)/shard_map/ppermute | solution.py:333
  108.2 11.4 %collective-permute-start.10 = (f32[792,128]{1,0:T(8,128)S(1)}, f32[792,128]{1,0:T(8,128)S(1)}, u32[]{:S(2)}, u32[]{:S(2)}) collective-permute-start(f32[792,128]{1,0:T(8,128)S(1)} %get-tuple-element.63), channel_id=1, source_target_pairs={{0,1},{1,2},{2,3},{3,4},{4,5},{5,6},{6,7},{7,0},{8,9},{9,10},{10,1... | collective-permute-start | bytes 1216520 | tf_op jit(solution)/shard_map/ppermute | solution.py:333
  108.3 13.5 %collective-permute-start.11 = (f32[792,128]{1,0:T(8,128)S(1)}, f32[792,128]{1,0:T(8,128)S(1)}, u32[]{:S(2)}, u32[]{:S(2)}) collective-permute-start(f32[792,128]{1,0:T(8,128)S(1)} %get-tuple-element.64), channel_id=1, source_target_pairs={{1,0},{2,1},{3,2},{4,3},{5,4},{6,5},{7,6},{0,7},{9,8},{10,9},{11,1... | collective-permute-start | bytes 1216520 | tf_op jit(solution)/shard_map/ppermute | solution.py:333
  154.5 7.6 %collective-permute-start.12 = (f32[440,128]{1,0:T(8,128)S(1)}, f32[440,128]{1,0:T(8,128)S(1)}, u32[]{:S(2)}, u32[]{:S(2)}) collective-permute-start(f32[440,128]{1,0:T(8,128)S(1)} %get-tuple-element.67), channel_id=1, source_target_pairs={{0,8},{8,16},{16,24},{24,32},{32,40},{40,48},{48,56},{56,64},{64,7... | collective-permute-start | bytes 675848 | tf_op jit(solution)/shard_map/ppermute | solution.py:333
  154.6 8.7 %collective-permute-start.13 = (f32[440,128]{1,0:T(8,128)S(1)}, f32[440,128]{1,0:T(8,128)S(1)}, u32[]{:S(2)}, u32[]{:S(2)}) collective-permute-start(f32[440,128]{1,0:T(8,128)S(1)} %get-tuple-element.68), channel_id=1, source_target_pairs={{8,0},{16,8},{24,16},{32,24},{40,32},{48,40},{56,48},{64,56},{72,6... | collective-permute-start | bytes 675848 | tf_op jit(solution)/shard_map/ppermute | solution.py:333
  163.6 11.8 %collective-permute-start.14 = (f32[968,128]{1,0:T(8,128)S(1)}, f32[968,128]{1,0:T(8,128)S(1)}, u32[]{:S(2)}, u32[]{:S(2)}) collective-permute-start(f32[968,128]{1,0:T(8,128)S(1)} %get-tuple-element.69), channel_id=1, source_target_pairs={{0,1},{1,2},{2,3},{3,4},{4,5},{5,6},{6,7},{7,0},{8,9},{9,10},{10,1... | collective-permute-start | bytes 1486856 | tf_op jit(solution)/shard_map/ppermute | solution.py:333
  164.7 12.7 %collective-permute-start.15 = (f32[968,128]{1,0:T(8,128)S(1)}, f32[968,128]{1,0:T(8,128)S(1)}, u32[]{:S(2)}, u32[]{:S(2)}) collective-permute-start(f32[968,128]{1,0:T(8,128)S(1)} %get-tuple-element.70), channel_id=1, source_target_pairs={{1,0},{2,1},{3,2},{4,3},{5,4},{6,5},{7,6},{0,7},{9,8},{10,9},{11,1... | collective-permute-start | bytes 1486856 | tf_op jit(solution)/shard_map/ppermute | solution.py:333
